TPU v7x, 32 devices: a whole 2x2x4 slice. The times are simulated.
32 devices in a mesh: lower: 4 (over y, core), upper: 2 (over x), depth: 4 (over z).
Axes of the slice: x: 2, y: 2, z: 4, core: 2. Of those that a mesh axis runs over, the one named last changes fastest.
Arguments:
- lower_vectors: bfloat16 [4, 32768, 512], P('depth', 'lower', 'upper'), may hold values from -0.0234375 to 0.0234375
- upper_vectors: bfloat16 [4, 32768, 768], P('depth', 'lower', 'upper'), may hold values from -6 to 6
- energy_lower: float32 [512], P(('lower', 'depth')), may hold values from 0 to 0.5
- energy_upper: float32 [768], P('upper'), may hold values from 1 to 2
- sym_lower: int32 [512], P(('lower', 'depth')), may hold values from 0 to 3
- sym_upper: int32 [768], P('upper'), may hold values from 0 to 3
- j_lower: int32 [512], P(('lower', 'depth')), may hold values from 0 to 2
- j_upper: int32 [768], P('upper'), may hold values from 0 to 2
Outputs:
- einstein: float32 [512, 768], P(('lower', 'depth'), 'upper')
All inputs are finite; a program needn't handle non-finite values.
Results may differ from a plain program's by a relative error of at most 0.0003.
Values may be sent and summed in bfloat16 or wider, within the bound.
No kernel may reach another device: no remote copies, remote signals or barrier semaphores. Data moves between devices by JAX's collectives and lax.ppermute only.
A program may use at most 64 MiB of HBM per device.

v0:
```python
import jax
import jax.numpy as jnp
from jax import lax
from jax.sharding import PartitionSpec as P


def local(
    lower_vectors, upper_vectors, energy_lower, energy_upper, sym_lower, sym_upper, j_lower, j_upper
):
    lower_rows = lower_vectors[0]
    upper_rows = upper_vectors[0]
    partial_terms = lax.dot_general(
        lax.all_gather(lower_rows, "upper", axis=1, tiled=True),
        upper_rows,
        (((0,), (0,)), ((), ())),
        preferred_element_type=jnp.float32,
    )
    moments = lax.psum_scatter(partial_terms, ("lower", "depth"), scatter_dimension=0, tiled=True)
    parity = sym_lower % 2
    sym_rule = sym_upper[None, :] - sym_lower[:, None] == (1 - 2 * parity)[:, None]
    j_rule = jnp.abs(j_upper[None, :] - j_lower[:, None]) <= 1
    allowed = jnp.logical_and(sym_rule, j_rule)
    frequency = energy_upper[None, :] - energy_lower[:, None]
    weight_upper = (2 * j_upper + 1).astype(jnp.float32)
    value = frequency * frequency * frequency * (moments * moments) / weight_upper[None, :]
    return jnp.where(allowed, value, jnp.zeros_like(value))


def solution(mesh):
    return jax.shard_map(
        local,
        mesh=mesh,
        in_specs=(
            P("depth", "lower", "upper"),
            P("depth", "lower", "upper"),
            P(("lower", "depth")),
            P("upper"),
            P(("lower", "depth")),
            P("upper"),
            P(("lower", "depth")),
            P("upper"),
        ),
        out_specs=P(("lower", "depth"), "upper"),
        check_vma=False,
    )
```

profile of v0, /device:TPU:0, one launch (start us, length us, event | category | flops | bytes accessed | tf_op | source)
XLA Modules:
  0.0 191.3 jit_solution(1023552684796298549)
XLA Ops:
  6.5 0.0 all-gather.3.cloned.1.call-start
  6.5 0.7 all-gather.3.cloned.1.call-update
  7.3 0.0 copy-start.5
  7.3 0.0 copy-start
  7.3 0.0 copy-start.1
  7.3 0.0 copy-start.2
  7.3 0.0 copy-start.3
  7.3 0.0 copy-start.4
  7.3 0.0 reduce-scatter.2.cloned.1.call-start
  7.4 108.2 %all-gather.3.cloned.1.call-done = bf16[1,8192,512]{2,1,0:T(8,128)(2,1)} async-done(((bf16[1,8192,256]{2,1,0:T(8,128)(2,1)}), bf16[1,8192,512]{2,1,0:T(8,128)(2,1)}) %all-gather.3.cloned.1.call-update) | async-done | bytes 8388624 | tf_op jit(solution)/shard_map/all_gather | solution.py:13
  115.6 10.6 %fusion = f32[512,384]{1,0:T(8,128)} fusion(bf16[1,8192,512]{2,1,0:T(8,128)(2,1)} %all-gather.3.cloned.1.call-done, bf16[1,8192,384]{2,1,0:T(8,128)(2,1)} %param.9), kind=kOutput, calls=%fused_computation | convolution fusion | flops 3221225472 | bytes 15466496 | tf_op jit(solution)/shard_map/dot_general | solution.py:12
  126.2 0.0 reduce-scatter.2.cloned.1.call-update
  126.2 0.0 copy-done.5
  126.3 0.0 copy-done
  126.3 56.7 %reduce-scatter.2.cloned.1.call-done = f32[32,384]{1,0:T(8,128)} async-done(((f32[512,384]{1,0:T(8,128)}), f32[32,384]{1,0:T(8,128)}) %reduce-scatter.2.cloned.1.call-update) | async-done | bytes 49168 | tf_op jit(solution)/shard_map/reduce_scatter | solution.py:18
  183.0 0.0 copy-done.1
  183.0 0.0 copy-done.2
  183.0 0.0 copy-done.3
  183.0 0.0 copy-done.4
  183.0 1.5 fusion.5
  (2 shorter events, 0.0 us)
Async XLA Ops:
  6.5 109.1 %all-gather.3.cloned.1.call-start = ((), (), s32[]{:S(2)}) async-start(), calls=%async_computation.2 | async-start | bytes 12582912 | tf_op jit(solution)/shard_map/all_gather | solution.py:13
  7.3 119.0 %copy-start.5 = (s32[32]{0:T(128)S(1)}, s32[32]{0:T(128)}, u32[]{:S(2)}) copy-start(s32[32]{0:T(128)} %param.12) | copy-start | bytes 388
  7.3 119.0 %copy-start = (s32[384]{0:T(512)S(1)}, s32[384]{0:T(512)}, u32[]{:S(2)}) copy-start(s32[384]{0:T(512)} %param.15) | copy-start | bytes 4612
  7.3 175.7 %copy-start.1 = (f32[384]{0:T(512)S(1)}, f32[384]{0:T(512)}, u32[]{:S(2)}) copy-start(f32[384]{0:T(512)} %param.11) | copy-start | bytes 4612
  7.3 175.7 %copy-start.2 = (s32[384]{0:T(512)S(1)}, s32[384]{0:T(512)}, u32[]{:S(2)}) copy-start(s32[384]{0:T(512)} %param.13) | copy-start | bytes 4612
  7.3 175.7 %copy-start.3 = (f32[32]{0:T(128)S(1)}, f32[32]{0:T(128)}, u32[]{:S(2)}) copy-start(f32[32]{0:T(128)} %param.10) | copy-start | bytes 388
  7.3 175.7 %copy-start.4 = (s32[32]{0:T(128)S(1)}, s32[32]{0:T(128)}, u32[]{:S(2)}) copy-start(s32[32]{0:T(128)} %param.14) | copy-start | bytes 388
  7.3 175.6 %reduce-scatter.2.cloned.1.call-start = ((), (), s32[]{:S(2)}) async-start(), calls=%async_computation.1 | async-start | bytes 835584 | tf_op jit(solution)/shard_map/reduce_scatter | solution.py:18
Sparse Core Ops, SparseCore 0:
  8.9 106.6 all-gather.2
  126.4 56.5 reduce-scatter.1
where the time goes:
time: 191 us
  waiting for transfers between devices  166 us (87%)
  between operations  13.5 us (7%)
  matrix products  10.6 us (6%)
    all_gather x1, waiting for transfers between devices, local(): lax.all_gather(lower_rows, 'upper', axis=1, tiled=True)  108 us
    reduce_scatter x1, waiting for transfers between devices, local(): lax.psum_scatter(partial_terms, ('lower', 'depth'), scatter_dimension=0,...  56.7 us
    dot_general x1, matrix products, local(): lax.dot_general(lax.all_gather(lower_rows, 'upper', axis=1, tiled=True),...  10.6 us
  transfers between devices with their start and end apart: 2, of which 2 were waited for; matrix products, arithmetic and copies ran while one was open for 0% of the time, Pallas kernels for 0%

commit v1 on v0

v1 whole, which is shorter than its diff:
```python
import jax
import jax.numpy as jnp
from jax import lax
from jax.experimental import pallas as pl
from jax.experimental.pallas import tpu as pltpu
from jax.sharding import PartitionSpec as P

OWNERS = ("lower", "depth")
VMEM_LIMIT = 16 * 1024 * 1024


def params():
    return pltpu.CompilerParams(vmem_limit_bytes=VMEM_LIMIT)


def cost():
    return pl.CostEstimate(flops=1024, bytes_accessed=1024, transcendentals=0)


def dot(a, b):
    return jnp.dot(a, b, preferred_element_type=jnp.float32)


def after(x, *others):
    return lax.optimization_barrier((x,) + others)[0]


def in_hbm(x):
    return pltpu.with_memory_space_constraint(x, pltpu.HBM)


def whole(shape):
    return pl.BlockSpec(shape, lambda *_: (0,) * len(shape))


def turn(lower_rows, heads, pieces, unit, mine, n_dep):
    rows, cols = lower_rows.shape
    per_block = cols // mine
    kind = lower_rows.dtype
    block = 2 * unit
    skipped = heads // block
    steps = (rows - heads) // block

    def body(low, *outs):
        i = pl.program_id(0)
        flipped = low[...].astype(jnp.float32).T
        by_owner = flipped.reshape(per_block, mine, block)
        for (start, stop, begin, end), out in zip(pieces, outs):

            @pl.when((i >= begin // 2) & (i < end // 2))
            def _():
                out[...] = by_owner[:, start:stop].reshape(per_block * (stop - start), block).astype(kind)

        @pl.when(i == steps - 1)
        def _():
            by_depth = flipped.reshape(per_block // n_dep, n_dep, mine, block)
            for z in range(n_dep):
                outs[-1][z] = by_depth[:, z].reshape(cols // n_dep, block).astype(kind)

    def spec(start, stop, begin, end):
        return pl.BlockSpec(
            (per_block * (stop - start), block),
            lambda i: (0, jnp.clip(i - begin // 2, 0, (end - begin) // 2 - 1)),
        )

    tail_shape = (n_dep, cols // n_dep, block)
    return pl.pallas_call(
        body,
        grid=(steps,),
        in_specs=[pl.BlockSpec((block, cols), lambda i: (i + skipped, 0))],
        out_specs=[spec(*piece) for piece in pieces] + [whole(tail_shape)],
        out_shape=[
            jax.ShapeDtypeStruct((per_block * (stop - start), (end - begin) * unit), kind)
            for start, stop, begin, end in pieces
        ]
        + [jax.ShapeDtypeStruct(tail_shape, kind)],
        compiler_params=params(),
        cost_estimate=cost(),
    )(in_hbm(lower_rows))


def split_states(product, per_block, parts):
    states, width = product.shape
    by_owner = product.reshape(per_block, parts, states // per_block // parts, width)
    return [by_owner[:, i].reshape(states // parts, width) for i in range(parts)]


def own_product(slot, lower_rows, upper_rows, n_up, per_block, parts):
    rows, cols = lower_rows.shape
    width = upper_rows.shape[1]
    steps = 4
    block = rows // steps

    def body(at, low, up, *refs):
        outs, total = refs[:-1], refs[-1]
        i = pl.program_id(0)
        term = dot(low[...].T, up[...])

        @pl.when(i == 0)
        def _():
            total[...] = term

        @pl.when(i > 0)
        def _():
            total[...] += term

        @pl.when(i == steps - 1)
        def _():
            for out, part in zip(outs, split_states(total[...], per_block, parts)):
                out[0] = part

    return pl.pallas_call(
        body,
        grid_spec=pltpu.PrefetchScalarGridSpec(
            num_scalar_prefetch=1,
            grid=(steps,),
            in_specs=[
                pl.BlockSpec((block, cols), lambda i, at: (i, 0)),
                pl.BlockSpec((block, width), lambda i, at: (i, 0)),
            ],
            out_specs=[pl.BlockSpec((1, cols // parts, width), lambda i, at: (at[0], 0, 0))] * parts,
            scratch_shapes=[pltpu.VMEM((cols, width), jnp.float32)],
        ),
        out_shape=[jax.ShapeDtypeStruct((n_up, cols // parts, width), jnp.float32)] * parts,
        compiler_params=params(),
        cost_estimate=cost(),
    )(slot.reshape(1), in_hbm(lower_rows), in_hbm(upper_rows))


def rows_product(got, upper_rows, first, so_far, per_block, parts):
    k, states = got.shape
    width = upper_rows.shape[1]

    def body(low, up, *refs):
        outs = refs[-parts:]
        for i, part in enumerate(split_states(dot(low[...].T, up[...]), per_block, parts)):
            outs[i][...] = part + refs[i][...] if so_far else part

    shape = (states // parts, width)
    return pl.pallas_call(
        body,
        grid=(1,),
        in_specs=[whole((k, states)), pl.BlockSpec((k, width), lambda i: (first // k, 0))]
        + [whole(shape)] * len(so_far),
        out_specs=[whole(shape)] * parts,
        out_shape=[jax.ShapeDtypeStruct(shape, jnp.float32)] * parts,
        compiler_params=params(),
        cost_estimate=cost(),
    )(got, in_hbm(upper_rows), *so_far)


def turned_product(got, upper_rows, first, block, so_far):
    states, k = got.shape
    width = upper_rows.shape[1]

    def body(low, up, before, out):
        term = dot(low[...], up[...])

        @pl.when(pl.program_id(0) == 0)
        def _():
            out[...] = before[...] + term

        @pl.when(pl.program_id(0) > 0)
        def _():
            out[...] += term

    return pl.pallas_call(
        body,
        grid=(k // block,),
        in_specs=[
            pl.BlockSpec((states, block), lambda i: (0, i)),
            pl.BlockSpec((block, width), lambda i: (i + first // block, 0)),
            whole((states, width)),
        ],
        out_specs=whole((states, width)),
        out_shape=jax.ShapeDtypeStruct((states, width), jnp.float32),
        compiler_params=params(),
        cost_estimate=cost(),
    )(got, in_hbm(upper_rows), so_far)


def last_product(slot, got, upper_rows, first, so_far, buffer):
    states, k = got.shape
    width = upper_rows.shape[1]

    def body(at, low, up, before, _, out):
        out[0] = before[...] + dot(low[...], up[...])

    return pl.pallas_call(
        body,
        grid_spec=pltpu.PrefetchScalarGridSpec(
            num_scalar_prefetch=1,
            grid=(1,),
            in_specs=[
                whole((states, k)),
                pl.BlockSpec((k, width), lambda i, at: (first // k, 0)),
                whole((states, width)),
                pl.BlockSpec(memory_space=pl.ANY),
            ],
            out_specs=pl.BlockSpec((1, states, width), lambda i, at: (at[0], 0, 0)),
        ),
        out_shape=jax.ShapeDtypeStruct(buffer.shape, buffer.dtype),
        input_output_aliases={4: 0},
        compiler_params=params(),
        cost_estimate=cost(),
    )(slot.reshape(1), got, in_hbm(upper_rows), so_far, buffer)


def tail_product(depth, got, own, forward, backward):
    n_dep, states, k = got.shape
    width = own.shape[1]
    n = len(forward)

    def body(at, low, mid, *refs):
        z = at[0]
        out = refs[-1]
        out[...] = dot(low[z], mid[...])
        for i in range(n):

            @pl.when(z > i)
            def _():
                out[...] += dot(low[z - 1 - i], refs[i][...])

            @pl.when(z + 1 + i < n_dep)
            def _():
                out[...] += dot(low[z + 1 + i], refs[n + i][...])

    vmem = pl.BlockSpec(memory_space=pltpu.VMEM)
    return pl.pallas_call(
        body,
        in_specs=[pl.BlockSpec(memory_space=pltpu.SMEM)] + [vmem] * (2 + 2 * n),
        out_specs=vmem,
        out_shape=jax.ShapeDtypeStruct((states, width), jnp.float32),
        compiler_params=params(),
        cost_estimate=cost(),
    )(depth.reshape(1), got, own, *forward, *backward)


def make_local(n_low, n_up, n_dep):
    n_owners = n_low * n_dep
    n_core = n_low // n_up
    others = range(1, n_up)

    def shifted(x, shift):
        return lax.ppermute(x, "upper", [((u + shift) % n_up, u) for u in range(n_up)])

    def low(y, c):
        return (y % n_up) * n_core + c

    def local(
        lower_vectors, upper_vectors, energy_lower, energy_upper, sym_lower, sym_upper, j_lower, j_upper
    ):
        lower_rows = lower_vectors[0]
        upper_rows = upper_vectors[0]
        rows, cols = lower_rows.shape
        width = upper_rows.shape[1]
        mine = energy_lower.shape[0]
        per_block = cols // mine
        unit = rows // 16
        heads = 4 * unit
        half = mine // 2
        pieces = ((0, half, 4, 10), (0, half, 0, 4), (half, mine, 4, 10), (half, mine, 0, 4))
        me = lax.axis_index("upper")
        depth = lax.axis_index("depth")
        my_low = lax.axis_index("lower")
        my_y, my_core = my_low // n_core, my_low % n_core

        parity = sym_lower % 2
        sym_rule = sym_upper[None, :] - sym_lower[:, None] == (1 - 2 * parity)[:, None]
        j_rule = jnp.abs(j_upper[None, :] - j_lower[:, None]) <= 1
        allowed = jnp.logical_and(sym_rule, j_rule)
        frequency = energy_upper[None, :] - energy_lower[:, None]
        weight_upper = (2 * j_upper + 1).astype(jnp.float32)
        cubed = frequency * frequency * frequency

        crossed = []

        def cross(x, *others_first):
            if len(crossed) > 1:
                x = after(x, *crossed[-2], *others_first)
            crossed.append([shifted(x, s) for s in others])

        up = [(z, z + 1) for z in range(n_dep - 1)]
        down = [(z + 1, z) for z in range(n_dep - 1)]
        forward, backward = [], []

        def pass_on(held_up, held_down):
            i = len(forward)
            forward.append(lax.ppermute(held_up, "depth", up[i:]))
            backward.append(lax.ppermute(held_down, "depth", down[: n_dep - 1 - i]))

        first = lower_rows[:heads]
        cross(first)
        later_rows = after(lower_rows, first)
        *turned, tail_rows = turn(later_rows, heads, pieces, unit, mine, n_dep)
        buffers = own_product(me, after(later_rows, turned[0]), upper_rows, n_up, per_block, 2)
        cross(after(turned[0], *buffers))
        up_tail = after(upper_rows[14 * unit :], turned[0])
        pass_on(up_tail, up_tail)
        cross(turned[1])
        for i in range(1, n_dep - 1):
            pass_on(*after((forward[-1], backward[-1]), *crossed[i - 1]))
        sorted_tail = lax.all_to_all(after(tail_rows, *crossed[1]), "depth", 0, 0)
        cross(turned[2], forward[0], backward[0])
        cross(turned[3], forward[1], backward[1], sorted_tail)
        so_far = [rows_product(g, upper_rows, 0, (), per_block, 2) for g in crossed[0]]

        def combined(i, got_1, got_2):
            buffer = buffers[i]
            for s in others:
                total = turned_product(got_1[s - 1], upper_rows, 8 * unit, 2 * unit, so_far[s - 1][i])
                slot = (me + s) % n_up
                buffer = last_product(slot, got_2[s - 1], upper_rows, heads, total, buffer)
            by_owner = buffer.reshape(n_owners, half, width)
            return buffer, jnp.sum(lax.all_to_all(by_owner, OWNERS, 0, 0), axis=0)

        _, sum_a = combined(0, crossed[1], crossed[2])
        cross(sorted_tail, forward[-1], backward[-1], sum_a)
        last, sum_b = combined(1, crossed[3], crossed[4])
        main = jnp.concatenate([sum_a, sum_b], axis=0)

        terms = [tail_product(depth, after(g, last), up_tail, forward, backward) for g in crossed[5]]

        def term_for(y):
            block = jnp.zeros_like(terms[0])
            for s in others:
                block = jnp.where((me + s) % n_up == y % n_up, terms[s - 1], block)
            return block

        tail_sum = term_for(my_y)
        for t in others:
            tail_sum = tail_sum + lax.ppermute(
                term_for(my_y + t), "lower", [(low(y, c), low(y + t, c)) for y in range(n_up) for c in range(n_core)]
            )
        by_core = tail_sum.reshape(n_core, mine, width)
        total = main + lax.dynamic_index_in_dim(by_core, my_core, 0, keepdims=False)
        for k in range(1, n_core):
            leaving = lax.dynamic_index_in_dim(by_core, (my_core + k) % n_core, 0, keepdims=False)
            total = total + lax.ppermute(
                leaving,
                "lower",
                [(low(y, c), low(y, (c + k) % n_core)) for y in range(n_up) for c in range(n_core)],
            )
        value = cubed * (total * total) / weight_upper[None, :]
        return jnp.where(allowed, value, jnp.zeros_like(value))

    return local


def solution(mesh):
    return jax.shard_map(
        make_local(mesh.shape["lower"], mesh.shape["upper"], mesh.shape["depth"]),
        mesh=mesh,
        in_specs=(
            P("depth", "lower", "upper"),
            P("depth", "lower", "upper"),
            P(("lower", "depth")),
            P("upper"),
            P(("lower", "depth")),
            P("upper"),
            P(("lower", "depth")),
            P("upper"),
        ),
        out_specs=P(("lower", "depth"), "upper"),
        check_vma=False,
    )
```

time: 191 us -> 124 us (0.65)
  waiting for transfers between devices: 166 us -> 48 us
  starting transfers between devices: 0.04 us -> 37 us
  Pallas kernels: 0 us -> 28.8 us
  between operations: 13.5 us -> 0.34 us
  matrix products: 10.6 us -> 0 us
  local copies, waits for them, and re-layouts: 0.03 us -> 8.22 us
    all_gather x1 -> x0, waiting for transfers between devices: 108 us -> none  [local(): lax.all_gather(lower_rows, 'upper', axis=1, tiled=True)]
    reduce_scatter x1 -> x0, waiting for transfers between devices: 56.7 us -> none  [local(): lax.psum_scatter(partial_terms, ('lower', 'depth'), scatter_dimension=0,...]
    ppermute x0 -> x14, waiting for transfers between devices: none -> 33.8 us  [the longest x3 19.6 us: pass_on(): backward.append(lax.ppermute(held_down, 'depth', down[:n_dep - 1 - i]))]
    pallas_call x0 -> x8, Pallas kernels: none -> 28.8 us  [the longest x1 6.87 us: own_product(): pl.pallas_call(body, grid_spec=pltpu.PrefetchScalarGridSpec(num_scalar_pr...]
    ppermute x0 -> x14, starting transfers between devices: none -> 19.2 us  [the longest x3 7.69 us: pass_on(): forward.append(lax.ppermute(held_up, 'depth', up[i:]))]
    all_to_all x0 -> x3, starting transfers between devices: none -> 17.8 us  [the longest x2 12.7 us: combined(): return (buffer, jnp.sum(lax.all_to_all(by_owner, OWNERS, 0, 0), axis=0))]
    all_to_all x0 -> x3, waiting for transfers between devices: none -> 14.2 us  [the longest x2 14.2 us: combined(): return (buffer, jnp.sum(lax.all_to_all(by_owner, OWNERS, 0, 0), axis=0))]
    dot_general x1 -> x0, matrix products: 10.6 us -> none  [local(): lax.dot_general(lax.all_gather(lower_rows, 'upper', axis=1, tiled=True),...]
  transfers between devices with their start and end apart: 2 -> 17, of which waited for: 2 -> 8; matrix products, arithmetic and copies ran while one was open for 0% -> 1% of each run, Pallas kernels for 0% -> 23%
where the time goes in v1:
time: 124 us; the launch traced here: 123 us
  waiting for transfers between devices  48 us (39%)
  starting transfers between devices  37 us (30%)
  Pallas kernels  28.8 us (23%)
  local copies, waits for them, and re-layouts  8.22 us (7%)
    ppermute x3, waiting for transfers between devices, pass_on(): backward.append(lax.ppermute(held_down, 'depth', down[:n_dep - 1 - i]))  19.6 us
    all_to_all x2, waiting for transfers between devices, combined(): return (buffer, jnp.sum(lax.all_to_all(by_owner, OWNERS, 0, 0), axis=0))  14.2 us
    all_to_all x2, starting transfers between devices, combined(): return (buffer, jnp.sum(lax.all_to_all(by_owner, OWNERS, 0, 0), axis=0))  12.7 us
    ppermute x6, waiting for transfers between devices, shifted(): lax.ppermute(x, 'upper', [((u + shift) % n_up, u) for u in range(n_up)])  9.28 us
    ppermute x3, starting transfers between devices, pass_on(): forward.append(lax.ppermute(held_up, 'depth', up[i:]))  7.69 us
    pallas_call x1, Pallas kernels, own_product(): pl.pallas_call(body, grid_spec=pltpu.PrefetchScalarGridSpec(num_scalar_pr...  6.87 us
    ppermute x6, starting transfers between devices, shifted(): lax.ppermute(x, 'upper', [((u + shift) % n_up, u) for u in range(n_up)])  6.34 us
    pallas_call x2, Pallas kernels, turned_product(): pl.pallas_call(body, grid=(k // block,), in_specs=[pl.BlockSpec((states,...  6.05 us
  transfers between devices with their start and end apart: 17, of which 8 were waited for; matrix products, arithmetic and copies ran while one was open for 1% of the time, Pallas kernels for 23%

profile of v1, /device:TPU:0, one launch (start us, length us, event | category | flops | bytes accessed | tf_op | source)
XLA Modules:
  0.0 123.1 jit_solution(538435799826720876)
XLA Ops:
  0.0 2.3 %slice_bitcast_fusion = bf16[2048,256]{1,0:T(8,128)(2,1)} fusion(bf16[1,8192,256]{2,1,0:T(8,128)(2,1)} %param.8), kind=kLoop, calls=%fused_computation | loop fusion | bytes 2097152 | tf_op jit(solution)/shard_map/slice | solution.py:292
  2.3 2.9 %collective-permute-start = (bf16[2048,256]{1,0:T(8,128)(2,1)}, bf16[2048,256]{1,0:T(8,128)(2,1)S(1)}, u32[]{:S(2)}, u32[]{:S(2)}) collective-permute-start(bf16[2048,256]{1,0:T(8,128)(2,1)} %slice_bitcast_fusion), channel_id=1, source_target_pairs={{4,0},{0,4},{5,1},{1,5},{6,2},{2,6},{7,3},{3,7},{12,8},{8,12},{13,... | collective-permute-start | bytes 3145736 | tf_op jit(solution)/shard_map/ppermute | solution.py:245
  5.2 5.6 %shard_map.82 = (bf16[128,3072]{1,0:T(8,128)(2,1)S(1)}, bf16[128,2048]{1,0:T(8,128)(2,1)S(1)}, bf16[128,3072]{1,0:T(8,128)(2,1)S(1)}, bf16[128,2048]{1,0:T(8,128)(2,1)}, bf16[4,64,1024]{2,1,0:T(8,128)(2,1)S(1)}) custom-call(bf16[8192,256]{1,0:T(8,128)(2,1)} %bitcast.22), custom_call_target="tpu_custom_call" | custom-call | flops 1024 | bytes 1024 | tf_op jit(solution)/shard_map/pallas_call | solution.py:67
  10.8 0.9 copy-done.6
  11.7 0.8 copy-done.8
  12.5 1.7 %slice_bitcast_fusion.1.mid = bf16[1024,384]{1,0:T(8,128)(2,1)S(1)} fusion(bf16[1,8192,384]{2,1,0:T(8,128)(2,1)} %param.9), kind=kLoop, calls=%fused_computation.1 | loop fusion | bytes 1572864 | tf_op jit(solution)/shard_map/slice | solution.py:298
  14.2 0.0 copy-done.5
  14.2 0.0 copy-done.2
  14.2 1.3 %collective-permute-start.4 = (bf16[1024,384]{1,0:T(8,128)(2,1)S(1)}, bf16[1024,384]{1,0:T(8,128)(2,1)S(1)}, u32[]{:S(2)}, u32[]{:S(2)}) collective-permute-start(bf16[1024,384]{1,0:T(8,128)(2,1)S(1)} %slice_bitcast_fusion.1.mid), channel_id=1, source_target_pairs={{1,0},{2,1},{3,2},{5,4},{6,5},{7,6},{9,8},{10,9},{11,10},{13,12},{... | collective-permute-start | bytes 2359304 | tf_op jit(solution)/shard_map/ppermute | solution.py:290
  15.5 4.6 %collective-permute-start.3 = (bf16[1024,384]{1,0:T(8,128)(2,1)S(1)}, bf16[1024,384]{1,0:T(8,128)(2,1)S(1)}, u32[]{:S(2)}, u32[]{:S(2)}) collective-permute-start(bf16[1024,384]{1,0:T(8,128)(2,1)S(1)} %slice_bitcast_fusion.1.mid), channel_id=1, source_target_pairs={{0,1},{1,2},{2,3},{4,5},{5,6},{6,7},{8,9},{9,10},{10,11},{12,13},{... | collective-permute-start | bytes 2359304 | tf_op jit(solution)/shard_map/ppermute | solution.py:289
  20.1 0.0 copy-start.7
  20.1 6.9 %shard_map.83 = (f32[2,128,384]{2,1,0:T(8,128)}, f32[2,128,384]{2,1,0:T(8,128)}) custom-call(s32[1]{0:T(128)} %bitcast.4.at, bf16[8192,256]{1,0:T(8,128)(2,1)} %bitcast.23, bf16[8192,384]{1,0:T(8,128)(2,1)} %bitcast.16), custom_call_target="tpu_custom_call" | custom-call | flops 1024 | bytes 1024 | tf_op jit(solution)/shard_map/pallas_call | solution.py:112
  27.0 0.0 copy-done.7
  27.0 0.1 collective-permute-start.2
  27.1 8.0 %collective-permute-done.4.refs_3_ = bf16[1024,384]{1,0:T(8,128)(2,1)S(1)} collective-permute-done((bf16[1024,384]{1,0:T(8,128)(2,1)S(1)}, bf16[1024,384]{1,0:T(8,128)(2,1)S(1)}, u32[]{:S(2)}, u32[]{:S(2)}) %collective-permute-start.4) | collective-permute-done | bytes 786464 | tf_op jit(solution)/shard_map/ppermute | solution.py:290
  35.1 1.2 collective-permute-done.3.refs_0_
  36.3 0.0 collective-permute-done.low
  36.3 1.6 %collective-permute-start.5 = (bf16[1024,384]{1,0:T(8,128)(2,1)S(1)}, bf16[1024,384]{1,0:T(8,128)(2,1)}, u32[]{:S(2)}, u32[]{:S(2)}) collective-permute-start(bf16[1024,384]{1,0:T(8,128)(2,1)S(1)} %collective-permute-done.3.refs_0_), channel_id=1, source_target_pairs={{1,2},{2,3},{5,6},{6,7},{9,10},{10,11},{13,14},{14,15},{17,18},{18... | collective-permute-start | bytes 2359304 | tf_op jit(solution)/shard_map/ppermute | solution.py:289
  37.8 1.3 %collective-permute-start.6 = (bf16[1024,384]{1,0:T(8,128)(2,1)S(1)}, bf16[1024,384]{1,0:T(8,128)(2,1)}, u32[]{:S(2)}, u32[]{:S(2)}) collective-permute-start(bf16[1024,384]{1,0:T(8,128)(2,1)S(1)} %collective-permute-done.4.refs_3_), channel_id=1, source_target_pairs={{1,0},{2,1},{5,4},{6,5},{9,8},{10,9},{13,12},{14,13},{17,16},{18,1... | collective-permute-start | bytes 2359304 | tf_op jit(solution)/shard_map/ppermute | solution.py:290
  39.1 6.3 %collective-permute-done.2.low = bf16[128,3072]{1,0:T(8,128)(2,1)S(1)} collective-permute-done((bf16[128,3072]{1,0:T(8,128)(2,1)S(1)}, bf16[128,3072]{1,0:T(8,128)(2,1)S(1)}, u32[]{:S(2)}, u32[]{:S(2)}) %collective-permute-start.2) | collective-permute-done | bytes 786464 | tf_op jit(solution)/shard_map/ppermute | solution.py:245
  45.4 0.9 copy-done
  46.4 5.1 %all-to-all-start.1 = ((bf16[4,64,1024]{2,1,0:T(8,128)(2,1)}), bf16[4,64,1024]{2,1,0:T(8,128)(2,1)}, u32[]{:S(2)}, u32[]{:S(2)}) async-start(bf16[4,64,1024]{2,1,0:T(8,128)(2,1)} %copy-done.2), calls=%async_computation.1 | async-start | bytes 1048576 | tf_op jit(solution)/shard_map/all_to_all | solution.py:303
  51.5 1.5 %collective-permute-start.1 = (bf16[128,2048]{1,0:T(8,128)(2,1)}, bf16[128,2048]{1,0:T(8,128)(2,1)}, u32[]{:S(2)}, u32[]{:S(2)}) collective-permute-start(bf16[128,2048]{1,0:T(8,128)(2,1)} %copy-done.8), channel_id=1, source_target_pairs={{4,0},{0,4},{5,1},{1,5},{6,2},{2,6},{7,3},{3,7},{12,8},{8,12},{13,... | collective-permute-start | bytes 1572872 | tf_op jit(solution)/shard_map/ppermute | solution.py:245
  53.0 0.5 collective-permute-start.8
  53.5 0.0 collective-permute-done.5.refs_1_
  53.5 11.6 %collective-permute-done.6.refs_4_ = bf16[1024,384]{1,0:T(8,128)(2,1)} collective-permute-done((bf16[1024,384]{1,0:T(8,128)(2,1)S(1)}, bf16[1024,384]{1,0:T(8,128)(2,1)}, u32[]{:S(2)}, u32[]{:S(2)}) %collective-permute-start.6) | collective-permute-done | bytes 786464 | tf_op jit(solution)/shard_map/ppermute | solution.py:290
  65.1 1.5 %collective-permute-start.9 = (bf16[1024,384]{1,0:T(8,128)(2,1)}, bf16[1024,384]{1,0:T(8,128)(2,1)}, u32[]{:S(2)}, u32[]{:S(2)}) collective-permute-start(bf16[1024,384]{1,0:T(8,128)(2,1)} %collective-permute-done.5.refs_1_), channel_id=1, source_target_pairs={{2,3},{6,7},{10,11},{14,15},{18,19},{22,23},{26,27},{30,31}} | collective-permute-start | bytes 2359304 | tf_op jit(solution)/shard_map/ppermute | solution.py:289
  66.7 1.3 %collective-permute-start.10 = (bf16[1024,384]{1,0:T(8,128)(2,1)}, bf16[1024,384]{1,0:T(8,128)(2,1)}, u32[]{:S(2)}, u32[]{:S(2)}) collective-permute-start(bf16[1024,384]{1,0:T(8,128)(2,1)} %collective-permute-done.6.refs_4_), channel_id=1, source_target_pairs={{1,0},{5,4},{9,8},{13,12},{17,16},{21,20},{25,24},{29,28}} | collective-permute-start | bytes 2359304 | tf_op jit(solution)/shard_map/ppermute | solution.py:290
  68.0 0.0 copy-start.1
  68.0 2.2 %shard_map.84 = (f32[128,384]{1,0:T(8,128)S(1)}, f32[128,384]{1,0:T(8,128)S(1)}) custom-call(bf16[2048,256]{1,0:T(8,128)(2,1)S(1)} %collective-permute-done.low, bf16[8192,384]{1,0:T(8,128)(2,1)} %bitcast.17), custom_call_target="tpu_custom_call" | custom-call | flops 1024 | bytes 1024 | tf_op jit(solution)/shard_map/pallas_call | solution.py:140
  70.2 0.0 copy-start.3
  70.2 0.7 copy-done.3
  70.9 0.0 copy-done.1
  70.9 3.0 %shard_map.85.before = f32[128,384]{1,0:T(8,128)S(1)} custom-call(bf16[128,3072]{1,0:T(8,128)(2,1)S(1)} %copy-done.1, bf16[8192,384]{1,0:T(8,128)(2,1)} %bitcast.18, f32[128,384]{1,0:T(8,128)S(1)} %get-tuple-element.36.before), custom_call_target="tpu_custom_call" | custom-call | flops 1024 | bytes 1024 | tf_op jit(solution)/shard_map/pallas_call | solution.py:167
  73.9 0.0 collective-permute-done.1.low
  73.9 2.7 %shard_map.86 = f32[2,128,384]{2,1,0:T(8,128)} custom-call(s32[1]{0:T(128)} %bitcast.at, bf16[128,2048]{1,0:T(8,128)(2,1)} %collective-permute-done.1.low, bf16[8192,384]{1,0:T(8,128)(2,1)} %bitcast.19, f32[128,384]{1,0:T(8,128)S(1)} %shard_map.85.before, f32[2,128,384]{2,1,0:T(8,128)} %get-tuple-element.33._), custom_call_target="tpu_custom_call", output_to_operand_aliasing={{}: (4, {})} | custom-call | flops 1024 | bytes 1024 | tf_op jit(solution)/shard_map/pallas_call | solution.py:189
  76.6 0.0 all-to-all-done.1
  76.6 9.2 %all-to-all-start = ((f32[16,16,384]{2,1,0:T(8,128)}), f32[16,16,384]{2,1,0:T(8,128)S(1)}, u32[]{:S(2)}, u32[]{:S(2)}) async-start(f32[16,16,384]{2,1,0:T(8,128)} %bitcast.5), calls=%async_computation | async-start | bytes 786432 | tf_op jit(solution)/shard_map/all_to_all | solution.py:315
  85.7 0.6 collective-permute-start.7
  86.4 12.2 %all-to-all-done = f32[16,16,384]{2,1,0:T(8,128)S(1)} async-done(((f32[16,16,384]{2,1,0:T(8,128)}), f32[16,16,384]{2,1,0:T(8,128)S(1)}, u32[]{:S(2)}, u32[]{:S(2)}) %all-to-all-start) | async-done | bytes 393248 | tf_op jit(solution)/shard_map/all_to_all | solution.py:315
  98.6 0.0 collective-permute-done.8.low
  98.6 0.0 collective-permute-done.9.refs_2_
  98.7 0.0 collective-permute-done.10.refs_5_
  98.7 0.6 collective-permute-start.11
  99.3 0.9 copy-done.4
  100.2 3.1 %shard_map.87.before = f32[128,384]{1,0:T(8,128)S(1)} custom-call(bf16[128,3072]{1,0:T(8,128)(2,1)} %collective-permute-done.8.low, bf16[8192,384]{1,0:T(8,128)(2,1)} %bitcast.20, f32[128,384]{1,0:T(8,128)S(1)} %copy-done.4), custom_call_target="tpu_custom_call" | custom-call | flops 1024 | bytes 1024 | tf_op jit(solution)/shard_map/pallas_call | solution.py:167
  103.3 0.0 copy-start.9
  103.3 0.0 copy-start.14
  103.3 0.0 copy-start.10
  103.4 0.0 copy-start.11
  103.4 0.0 copy-start.12
  103.4 0.0 copy-start.13
  103.4 0.0 collective-permute-done.7.low
  103.4 2.5 %shard_map.88 = f32[2,128,384]{2,1,0:T(8,128)} custom-call(s32[1]{0:T(128)} %bitcast.at, bf16[128,2048]{1,0:T(8,128)(2,1)S(1)} %collective-permute-done.7.low, bf16[8192,384]{1,0:T(8,128)(2,1)} %bitcast.21, f32[128,384]{1,0:T(8,128)S(1)} %shard_map.87.before, f32[2,128,384]{2,1,0:T(8,128)} %get-tuple-element.34._), custom_call_target="tpu_custom_call", output_to_operand_aliasing={{}: (4, {})} | custom-call | flops 1024 | bytes 1024 | tf_op jit(solution)/shard_map/pallas_call | solution.py:189
  105.9 3.6 %all-to-all-start.2 = ((f32[16,16,384]{2,1,0:T(8,128)}), f32[16,16,384]{2,1,0:T(8,128)S(1)}, u32[]{:S(2)}, u32[]{:S(2)}) async-start(f32[16,16,384]{2,1,0:T(8,128)} %bitcast.7), calls=%async_computation.2 | async-start | bytes 786432 | tf_op jit(solution)/shard_map/all_to_all | solution.py:315
  109.5 3.0 %collective-permute-done.11.low = bf16[4,64,1024]{2,1,0:T(8,128)(2,1)S(1)} collective-permute-done((bf16[4,64,1024]{2,1,0:T(8,128)(2,1)}, bf16[4,64,1024]{2,1,0:T(8,128)(2,1)S(1)}, u32[]{:S(2)}, u32[]{:S(2)}) %collective-permute-start.11) | collective-permute-done | bytes 524320 | tf_op jit(solution)/shard_map/ppermute | solution.py:245
  112.5 2.8 %shard_map.89 = f32[64,384]{1,0:T(8,128)S(1)} custom-call(s32[1]{0:T(128)} %bitcast.8.at, bf16[4,64,1024]{2,1,0:T(8,128)(2,1)S(1)} %collective-permute-done.11.low, bf16[1024,384]{1,0:T(8,128)(2,1)S(1)} %slice_bitcast_fusion.1.mid, bf16[1024,384]{1,0:T(8,128)(2,1)S(1)} %collective-permute-done.3.refs_0_, bf16[1024,384]{1,0:T(8,128)(2,1)} %collective-permute-done.5.refs_1_, ...), custom_call_target="tpu_custom_call" | custom-call | flops 1024 | bytes 1024 | tf_op jit(solution)/shard_map/pallas_call | solution.py:229
  115.3 1.2 %collective-permute-start.12 = (f32[64,384]{1,0:T(8,128)S(1)}, f32[64,384]{1,0:T(8,128)S(1)}, u32[]{:S(2)}, u32[]{:S(2)}) collective-permute-start(f32[64,384]{1,0:T(8,128)S(1)} %broadcast_select_fusion), channel_id=1, source_target_pairs={{0,16},{8,24},{16,0},{24,8},{1,17},{9,25},{17,1},{25,9},{2,18},{10... | collective-permute-start | bytes 294920 | tf_op jit(solution)/shard_map/ppermute | solution.py:332
  116.6 0.0 copy-done.9
  116.6 3.7 %collective-permute-done.12 = f32[64,384]{1,0:T(8,128)S(1)} collective-permute-done((f32[64,384]{1,0:T(8,128)S(1)}, f32[64,384]{1,0:T(8,128)S(1)}, u32[]{:S(2)}, u32[]{:S(2)}) %collective-permute-start.12) | collective-permute-done | bytes 98336 | tf_op jit(solution)/shard_map/ppermute | solution.py:332
  120.3 0.1 collective-permute-start.13
  120.4 1.9 %all-to-all-done.2 = f32[16,16,384]{2,1,0:T(8,128)S(1)} async-done(((f32[16,16,384]{2,1,0:T(8,128)}), f32[16,16,384]{2,1,0:T(8,128)S(1)}, u32[]{:S(2)}, u32[]{:S(2)}) %all-to-all-start.2) | async-done | bytes 393248 | tf_op jit(solution)/shard_map/all_to_all | solution.py:315
  122.4 0.0 collective-permute-done.13
  122.4 0.7 fusion.2
  (18 shorter events, 0.1 us)
Async XLA Ops:
  2.3 34.0 %collective-permute-start = (bf16[2048,256]{1,0:T(8,128)(2,1)}, bf16[2048,256]{1,0:T(8,128)(2,1)S(1)}, u32[]{:S(2)}, u32[]{:S(2)}) collective-permute-start(bf16[2048,256]{1,0:T(8,128)(2,1)} %slice_bitcast_fusion), channel_id=1, source_target_pairs={{4,0},{0,4},{5,1},{1,5},{6,2},{2,6},{7,3},{3,7},{12,8},{8,12},{13,... | collective-permute-start | bytes 3145736 | tf_op jit(solution)/shard_map/ppermute | solution.py:245
  10.8 0.9 copy-start.6
  11.7 0.8 copy-start.8
  12.5 1.7 %copy-start.5 = (bf16[128,3072]{1,0:T(8,128)(2,1)}, bf16[128,3072]{1,0:T(8,128)(2,1)S(1)}, u32[]{:S(2)}) copy-start(bf16[128,3072]{1,0:T(8,128)(2,1)S(1)} %get-tuple-element.45) | copy-start | bytes 2359300
  12.5 1.7 %copy-start.2 = (bf16[4,64,1024]{2,1,0:T(8,128)(2,1)}, bf16[4,64,1024]{2,1,0:T(8,128)(2,1)S(1)}, u32[]{:S(2)}) copy-start(bf16[4,64,1024]{2,1,0:T(8,128)(2,1)S(1)} %get-tuple-element.42) | copy-start | bytes 1572868
  14.2 20.9 %collective-permute-start.4 = (bf16[1024,384]{1,0:T(8,128)(2,1)S(1)}, bf16[1024,384]{1,0:T(8,128)(2,1)S(1)}, u32[]{:S(2)}, u32[]{:S(2)}) collective-permute-start(bf16[1024,384]{1,0:T(8,128)(2,1)S(1)} %slice_bitcast_fusion.1.mid), channel_id=1, source_target_pairs={{1,0},{2,1},{3,2},{5,4},{6,5},{7,6},{9,8},{10,9},{11,10},{13,12},{... | collective-permute-start | bytes 2359304 | tf_op jit(solution)/shard_map/ppermute | solution.py:290
  15.5 20.8 %collective-permute-start.3 = (bf16[1024,384]{1,0:T(8,128)(2,1)S(1)}, bf16[1024,384]{1,0:T(8,128)(2,1)S(1)}, u32[]{:S(2)}, u32[]{:S(2)}) collective-permute-start(bf16[1024,384]{1,0:T(8,128)(2,1)S(1)} %slice_bitcast_fusion.1.mid), channel_id=1, source_target_pairs={{0,1},{1,2},{2,3},{4,5},{5,6},{6,7},{8,9},{9,10},{10,11},{12,13},{... | collective-permute-start | bytes 2359304 | tf_op jit(solution)/shard_map/ppermute | solution.py:289
  20.1 6.9 %copy-start.7 = (bf16[128,3072]{1,0:T(8,128)(2,1)S(1)}, bf16[128,3072]{1,0:T(8,128)(2,1)}, u32[]{:S(2)}) copy-start(bf16[128,3072]{1,0:T(8,128)(2,1)} %copy-done.6) | copy-start | bytes 2359300
  27.0 18.4 %collective-permute-start.2 = (bf16[128,3072]{1,0:T(8,128)(2,1)S(1)}, bf16[128,3072]{1,0:T(8,128)(2,1)S(1)}, u32[]{:S(2)}, u32[]{:S(2)}) collective-permute-start(bf16[128,3072]{1,0:T(8,128)(2,1)S(1)} %copy-done.7), channel_id=1, source_target_pairs={{4,0},{0,4},{5,1},{1,5},{6,2},{2,6},{7,3},{3,7},{12,8},{8,12},{13,... | collective-permute-start | bytes 2359304 | tf_op jit(solution)/shard_map/ppermute | solution.py:245
  36.3 17.2 %collective-permute-start.5 = (bf16[1024,384]{1,0:T(8,128)(2,1)S(1)}, bf16[1024,384]{1,0:T(8,128)(2,1)}, u32[]{:S(2)}, u32[]{:S(2)}) collective-permute-start(bf16[1024,384]{1,0:T(8,128)(2,1)S(1)} %collective-permute-done.3.refs_0_), channel_id=1, source_target_pairs={{1,2},{2,3},{5,6},{6,7},{9,10},{10,11},{13,14},{14,15},{17,18},{18... | collective-permute-start | bytes 2359304 | tf_op jit(solution)/shard_map/ppermute | solution.py:289
  37.8 27.3 %collective-permute-start.6 = (bf16[1024,384]{1,0:T(8,128)(2,1)S(1)}, bf16[1024,384]{1,0:T(8,128)(2,1)}, u32[]{:S(2)}, u32[]{:S(2)}) collective-permute-start(bf16[1024,384]{1,0:T(8,128)(2,1)S(1)} %collective-permute-done.4.refs_3_), channel_id=1, source_target_pairs={{1,0},{2,1},{5,4},{6,5},{9,8},{10,9},{13,12},{14,13},{17,16},{18,1... | collective-permute-start | bytes 2359304 | tf_op jit(solution)/shard_map/ppermute | solution.py:290
  45.4 0.9 copy-start
  46.4 30.2 %all-to-all-start.1 = ((bf16[4,64,1024]{2,1,0:T(8,128)(2,1)}), bf16[4,64,1024]{2,1,0:T(8,128)(2,1)}, u32[]{:S(2)}, u32[]{:S(2)}) async-start(bf16[4,64,1024]{2,1,0:T(8,128)(2,1)} %copy-done.2), calls=%async_computation.1 | async-start | bytes 1048576 | tf_op jit(solution)/shard_map/all_to_all | solution.py:303
  51.5 22.4 %collective-permute-start.1 = (bf16[128,2048]{1,0:T(8,128)(2,1)}, bf16[128,2048]{1,0:T(8,128)(2,1)}, u32[]{:S(2)}, u32[]{:S(2)}) collective-permute-start(bf16[128,2048]{1,0:T(8,128)(2,1)} %copy-done.8), channel_id=1, source_target_pairs={{4,0},{0,4},{5,1},{1,5},{6,2},{2,6},{7,3},{3,7},{12,8},{8,12},{13,... | collective-permute-start | bytes 1572872 | tf_op jit(solution)/shard_map/ppermute | solution.py:245
  53.0 45.7 %collective-permute-start.8 = (bf16[128,3072]{1,0:T(8,128)(2,1)}, bf16[128,3072]{1,0:T(8,128)(2,1)}, u32[]{:S(2)}, u32[]{:S(2)}) collective-permute-start(bf16[128,3072]{1,0:T(8,128)(2,1)} %copy-done.5), channel_id=1, source_target_pairs={{4,0},{0,4},{5,1},{1,5},{6,2},{2,6},{7,3},{3,7},{12,8},{8,12},{13,... | collective-permute-start | bytes 2359304 | tf_op jit(solution)/shard_map/ppermute | solution.py:245
  65.1 33.5 %collective-permute-start.9 = (bf16[1024,384]{1,0:T(8,128)(2,1)}, bf16[1024,384]{1,0:T(8,128)(2,1)}, u32[]{:S(2)}, u32[]{:S(2)}) collective-permute-start(bf16[1024,384]{1,0:T(8,128)(2,1)} %collective-permute-done.5.refs_1_), channel_id=1, source_target_pairs={{2,3},{6,7},{10,11},{14,15},{18,19},{22,23},{26,27},{30,31}} | collective-permute-start | bytes 2359304 | tf_op jit(solution)/shard_map/ppermute | solution.py:289
  66.7 32.0 %collective-permute-start.10 = (bf16[1024,384]{1,0:T(8,128)(2,1)}, bf16[1024,384]{1,0:T(8,128)(2,1)}, u32[]{:S(2)}, u32[]{:S(2)}) collective-permute-start(bf16[1024,384]{1,0:T(8,128)(2,1)} %collective-permute-done.6.refs_4_), channel_id=1, source_target_pairs={{1,0},{5,4},{9,8},{13,12},{17,16},{21,20},{25,24},{29,28}} | collective-permute-start | bytes 2359304 | tf_op jit(solution)/shard_map/ppermute | solution.py:290
  68.0 2.9 %copy-start.1 = (bf16[128,3072]{1,0:T(8,128)(2,1)S(1)}, bf16[128,3072]{1,0:T(8,128)(2,1)}, u32[]{:S(2)}) copy-start(bf16[128,3072]{1,0:T(8,128)(2,1)} %copy-done) | copy-start | bytes 2359300
  70.2 0.7 copy-start.3
  76.6 22.0 %all-to-all-start = ((f32[16,16,384]{2,1,0:T(8,128)}), f32[16,16,384]{2,1,0:T(8,128)S(1)}, u32[]{:S(2)}, u32[]{:S(2)}) async-start(f32[16,16,384]{2,1,0:T(8,128)} %bitcast.5), calls=%async_computation | async-start | bytes 786432 | tf_op jit(solution)/shard_map/all_to_all | solution.py:315
  85.7 17.7 %collective-permute-start.7 = (bf16[128,2048]{1,0:T(8,128)(2,1)}, bf16[128,2048]{1,0:T(8,128)(2,1)S(1)}, u32[]{:S(2)}, u32[]{:S(2)}) collective-permute-start(bf16[128,2048]{1,0:T(8,128)(2,1)} %get-tuple-element.43), channel_id=1, source_target_pairs={{4,0},{0,4},{5,1},{1,5},{6,2},{2,6},{7,3},{3,7},{12,8},{8,12},{13,... | collective-permute-start | bytes 1572872 | tf_op jit(solution)/shard_map/ppermute | solution.py:245
  98.7 13.8 %collective-permute-start.11 = (bf16[4,64,1024]{2,1,0:T(8,128)(2,1)}, bf16[4,64,1024]{2,1,0:T(8,128)(2,1)S(1)}, u32[]{:S(2)}, u32[]{:S(2)}) collective-permute-start(bf16[4,64,1024]{2,1,0:T(8,128)(2,1)} %all-to-all-done.1), channel_id=1, source_target_pairs={{4,0},{0,4},{5,1},{1,5},{6,2},{2,6},{7,3},{3,7},{12,8},{8,12},{13,... | collective-permute-start | bytes 1572872 | tf_op jit(solution)/shard_map/ppermute | solution.py:245
  99.3 0.9 copy-start.4
  103.3 13.2 %copy-start.9 = (s32[384]{0:T(512)S(1)}, s32[384]{0:T(512)}, u32[]{:S(2)}) copy-start(s32[384]{0:T(512)} %param.15) | copy-start | bytes 4612
  103.3 17.1 %copy-start.14 = (s32[32]{0:T(128)S(1)}, s32[32]{0:T(128)}, u32[]{:S(2)}) copy-start(s32[32]{0:T(128)} %param.12) | copy-start | bytes 388
  103.3 19.0 %copy-start.10 = (f32[384]{0:T(512)S(1)}, f32[384]{0:T(512)}, u32[]{:S(2)}) copy-start(f32[384]{0:T(512)} %param.11) | copy-start | bytes 4612
  103.4 19.0 %copy-start.11 = (s32[384]{0:T(512)S(1)}, s32[384]{0:T(512)}, u32[]{:S(2)}) copy-start(s32[384]{0:T(512)} %param.13) | copy-start | bytes 4612
  103.4 19.0 %copy-start.12 = (f32[32]{0:T(128)S(1)}, f32[32]{0:T(128)}, u32[]{:S(2)}) copy-start(f32[32]{0:T(128)} %param.10) | copy-start | bytes 388
  103.4 19.0 %copy-start.13 = (s32[32]{0:T(128)S(1)}, s32[32]{0:T(128)}, u32[]{:S(2)}) copy-start(s32[32]{0:T(128)} %param.14) | copy-start | bytes 388
  105.9 16.4 %all-to-all-start.2 = ((f32[16,16,384]{2,1,0:T(8,128)}), f32[16,16,384]{2,1,0:T(8,128)S(1)}, u32[]{:S(2)}, u32[]{:S(2)}) async-start(f32[16,16,384]{2,1,0:T(8,128)} %bitcast.7), calls=%async_computation.2 | async-start | bytes 786432 | tf_op jit(solution)/shard_map/all_to_all | solution.py:315
  115.3 5.0 %collective-permute-start.12 = (f32[64,384]{1,0:T(8,128)S(1)}, f32[64,384]{1,0:T(8,128)S(1)}, u32[]{:S(2)}, u32[]{:S(2)}) collective-permute-start(f32[64,384]{1,0:T(8,128)S(1)} %broadcast_select_fusion), channel_id=1, source_target_pairs={{0,16},{8,24},{16,0},{24,8},{1,17},{9,25},{17,1},{25,9},{2,18},{10... | collective-permute-start | bytes 294920 | tf_op jit(solution)/shard_map/ppermute | solution.py:332
  120.3 2.1 %collective-permute-start.13 = (f32[32,384]{1,0:T(8,128)S(1)}, f32[32,384]{1,0:T(8,128)S(1)}, u32[]{:S(2)}, u32[]{:S(2)}) collective-permute-start(f32[32,384]{1,0:T(8,128)S(1)} %dynamic-slice_bitcast_fusion), channel_id=1, source_target_pairs={{0,8},{8,0},{16,24},{24,16},{1,9},{9,1},{17,25},{25,17},{2,10},{10... | collective-permute-start | bytes 147464 | tf_op jit(solution)/shard_map/ppermute | solution.py:339

commit v2 on v1

v2 whole, which is shorter than its diff:
```python
import jax
import jax.numpy as jnp
from jax import lax
from jax.experimental import pallas as pl
from jax.experimental.pallas import tpu as pltpu
from jax.sharding import PartitionSpec as P

OWNERS = ("lower", "depth")
VMEM_LIMIT = 16 * 1024 * 1024


def params():
    return pltpu.CompilerParams(vmem_limit_bytes=VMEM_LIMIT)


def cost(microseconds):
    return pl.CostEstimate(flops=0, bytes_accessed=int(microseconds * 3.0e6), transcendentals=0)


def dot(a, b):
    return jnp.dot(a, b, preferred_element_type=jnp.float32)


def after(x, *others):
    return lax.optimization_barrier((x,) + others)[0]


def in_hbm(x):
    return pltpu.with_memory_space_constraint(x, pltpu.HBM)


def whole(shape):
    return pl.BlockSpec(shape, lambda *_: (0,) * len(shape))


def turn(lower_rows, parts, unit, mine, n_dep):
    rows, cols = lower_rows.shape
    per_block = cols // mine
    kind = lower_rows.dtype
    block = 2 * unit
    mains = rows // block - 2

    def body(low, *outs):
        i = pl.program_id(0)
        flipped = low[...].astype(jnp.float32).T

        @pl.when(i < mains)
        def _():
            for out, part in zip(outs, split_states(flipped, per_block, parts)):
                out[...] = part.astype(kind)

        @pl.when(i == mains)
        def _():
            by_depth = flipped.reshape(per_block // n_dep, n_dep, mine, block)
            for z in range(n_dep):
                outs[-1][z] = by_depth[:, z].reshape(cols // n_dep, block).astype(kind)

    tail_shape = (n_dep, cols // n_dep, block)
    return pl.pallas_call(
        body,
        grid=(mains + 1,),
        in_specs=[pl.BlockSpec((block, cols), lambda i: (jnp.where(i < mains, i, i + 1), 0))],
        out_specs=[pl.BlockSpec((cols // parts, block), lambda i: (0, jnp.minimum(i, mains - 1)))] * parts
        + [whole(tail_shape)],
        out_shape=[jax.ShapeDtypeStruct((cols // parts, mains * block), kind)] * parts
        + [jax.ShapeDtypeStruct(tail_shape, kind)],
        compiler_params=params(),
        cost_estimate=cost(0.01),
    )(in_hbm(lower_rows))


def split_states(product, per_block, parts):
    states, width = product.shape
    by_owner = product.reshape(per_block, parts, states // per_block // parts, width)
    return [by_owner[:, i].reshape(states // parts, width) for i in range(parts)]


def own_product(slot, lower_rows, upper_rows, n_up, per_block, parts):
    rows, cols = lower_rows.shape
    width = upper_rows.shape[1]
    steps = 4
    block = rows // steps

    def body(at, low, up, *refs):
        outs, total = refs[:-1], refs[-1]
        i = pl.program_id(0)
        term = dot(low[...].T, up[...])

        @pl.when(i == 0)
        def _():
            total[...] = term

        @pl.when(i > 0)
        def _():
            total[...] += term

        @pl.when(i == steps - 1)
        def _():
            for out, part in zip(outs, split_states(total[...], per_block, parts)):
                out[0] = part

    return pl.pallas_call(
        body,
        grid_spec=pltpu.PrefetchScalarGridSpec(
            num_scalar_prefetch=1,
            grid=(steps,),
            in_specs=[
                pl.BlockSpec((block, cols), lambda i, at: (i, 0)),
                pl.BlockSpec((block, width), lambda i, at: (i, 0)),
            ],
            out_specs=[pl.BlockSpec((1, cols // parts, width), lambda i, at: (at[0], 0, 0))] * parts,
            scratch_shapes=[pltpu.VMEM((cols, width), jnp.float32)],
        ),
        out_shape=[jax.ShapeDtypeStruct((n_up, cols // parts, width), jnp.float32)] * parts,
        compiler_params=params(),
        cost_estimate=cost(0.01),
    )(slot.reshape(1), in_hbm(lower_rows), in_hbm(upper_rows))


def rows_product(got, upper_rows, first, block, so_far, per_block, parts):
    k, states = got.shape
    width = upper_rows.shape[1]
    steps = k // block

    def body(low, up, *refs):
        outs, total = refs[-1 - parts : -1], refs[-1]
        i = pl.program_id(0)
        term = dot(low[...].T, up[...])

        @pl.when(i == 0)
        def _():
            total[...] = term

        @pl.when(i > 0)
        def _():
            total[...] += term

        @pl.when(i == steps - 1)
        def _():
            for j, part in enumerate(split_states(total[...], per_block, parts)):
                outs[j][...] = part + refs[j][...] if so_far else part

    shape = (states // parts, width)
    return pl.pallas_call(
        body,
        grid=(steps,),
        in_specs=[
            pl.BlockSpec((block, states), lambda i: (i, 0)),
            pl.BlockSpec((block, width), lambda i: (i + first // block, 0)),
        ]
        + [whole(shape)] * len(so_far),
        out_specs=[whole(shape)] * parts,
        out_shape=[jax.ShapeDtypeStruct(shape, jnp.float32)] * parts,
        scratch_shapes=[pltpu.VMEM((states, width), jnp.float32)],
        compiler_params=params(),
        cost_estimate=cost(0.01),
    )(got, in_hbm(upper_rows), *so_far)


def turned_product(slot, got, upper_rows, so_far, buffer):
    states, k = got.shape
    width = upper_rows.shape[1]
    steps = 3
    block = k // steps

    def body(at, low, up, before, _, out, total):
        i = pl.program_id(0)
        term = dot(low[...], up[...])

        @pl.when(i == 0)
        def _():
            total[...] = before[...] + term

        @pl.when((i > 0) & (i < steps - 1))
        def _():
            total[...] += term

        @pl.when(i == steps - 1)
        def _():
            out[0] = total[...] + term

    return pl.pallas_call(
        body,
        grid_spec=pltpu.PrefetchScalarGridSpec(
            num_scalar_prefetch=1,
            grid=(steps,),
            in_specs=[
                pl.BlockSpec((states, block), lambda i, at: (0, i)),
                pl.BlockSpec((block, width), lambda i, at: (i, 0)),
                whole((states, width)),
                pl.BlockSpec(memory_space=pl.ANY),
            ],
            out_specs=pl.BlockSpec((1, states, width), lambda i, at: (at[0], 0, 0)),
            scratch_shapes=[pltpu.VMEM((states, width), jnp.float32)],
        ),
        out_shape=jax.ShapeDtypeStruct(buffer.shape, buffer.dtype),
        input_output_aliases={4: 0},
        compiler_params=params(),
        cost_estimate=cost(0.01),
    )(slot.reshape(1), got, in_hbm(upper_rows), so_far, buffer)


def tail_product(depth, got, own, forward, backward):
    n_dep, states, k = got.shape
    width = own.shape[1]
    n = len(forward)

    def body(at, low, mid, *refs):
        z = at[0]
        out = refs[-1]
        out[...] = dot(low[z], mid[...])
        for i in range(n):

            @pl.when(z > i)
            def _():
                out[...] += dot(low[z - 1 - i], refs[i][...])

            @pl.when(z + 1 + i < n_dep)
            def _():
                out[...] += dot(low[z + 1 + i], refs[n + i][...])

    vmem = pl.BlockSpec(memory_space=pltpu.VMEM)
    return pl.pallas_call(
        body,
        in_specs=[pl.BlockSpec(memory_space=pltpu.SMEM)] + [vmem] * (2 + 2 * n),
        out_specs=vmem,
        out_shape=jax.ShapeDtypeStruct((states, width), jnp.float32),
        compiler_params=params(),
        cost_estimate=cost(0.01),
    )(depth.reshape(1), got, own, *forward, *backward)


def make_local(n_low, n_up, n_dep):
    n_owners = n_low * n_dep
    n_core = n_low // n_up
    others = range(1, n_up)

    def shifted(x, shift):
        return lax.ppermute(x, "upper", [((u + shift) % n_up, u) for u in range(n_up)])

    def low(y, c):
        return (y % n_up) * n_core + c

    def local(
        lower_vectors, upper_vectors, energy_lower, energy_upper, sym_lower, sym_upper, j_lower, j_upper
    ):
        lower_rows = lower_vectors[0]
        upper_rows = upper_vectors[0]
        rows, cols = lower_rows.shape
        width = upper_rows.shape[1]
        mine = energy_lower.shape[0]
        per_block = cols // mine
        unit = rows // 16
        main_rows = 12 * unit
        half = mine // 2
        me = lax.axis_index("upper")
        depth = lax.axis_index("depth")
        my_low = lax.axis_index("lower")
        my_y, my_core = my_low // n_core, my_low % n_core

        parity = sym_lower % 2
        sym_rule = sym_upper[None, :] - sym_lower[:, None] == (1 - 2 * parity)[:, None]
        j_rule = jnp.abs(j_upper[None, :] - j_lower[:, None]) <= 1
        allowed = jnp.logical_and(sym_rule, j_rule)
        frequency = energy_upper[None, :] - energy_lower[:, None]
        weight_upper = (2 * j_upper + 1).astype(jnp.float32)
        cubed = frequency * frequency * frequency

        crossed = []

        def cross(x, *others_first):
            if len(crossed) > 1:
                x = after(x, *crossed[-2], *others_first)
            crossed.append([shifted(x, s) for s in others])

        up = [(z, z + 1) for z in range(n_dep - 1)]
        down = [(z + 1, z) for z in range(n_dep - 1)]
        forward, backward = [], []

        def pass_on(held_up, held_down):
            i = len(forward)
            forward.append(lax.ppermute(held_up, "depth", up[i:]))
            backward.append(lax.ppermute(held_down, "depth", down[: n_dep - 1 - i]))

        first = lower_rows[main_rows : main_rows + 2 * unit]
        cross(first)
        later_rows = after(lower_rows, first)
        *turned, tail_rows = turn(later_rows, 2, unit, mine, n_dep)
        cross(after(turned[0], *crossed[0]))
        up_tail = after(upper_rows[main_rows + 2 * unit :], *crossed[0])
        pass_on(up_tail, up_tail)
        for i in range(1, n_dep - 1):
            pass_on(forward[-1], backward[-1])
        sorted_tail = lax.all_to_all(tail_rows, "depth", 0, 0)
        buffers = own_product(me, after(later_rows, turned[0]), upper_rows, n_up, per_block, 2)
        cross(turned[1])
        so_far = [rows_product(g, upper_rows, main_rows, 2 * unit, (), per_block, 2) for g in crossed[0]]

        def combined(i, got, *others_first):
            buffer = buffers[i]
            for s in others:
                slot = (me + s) % n_up
                buffer = turned_product(slot, got[s - 1], upper_rows, so_far[s - 1][i], buffer)
            buffer = after(buffer, *others_first) if others_first else buffer
            by_owner = buffer.reshape(n_owners, half, width)
            return buffer, jnp.sum(lax.all_to_all(by_owner, OWNERS, 0, 0), axis=0)

        _, sum_a = combined(0, crossed[1], sorted_tail)
        cross(sorted_tail, sum_a)
        last, sum_b = combined(1, crossed[2], sum_a)
        main = jnp.concatenate([sum_a, sum_b], axis=0)

        terms = [tail_product(depth, after(g, last), up_tail, forward, backward) for g in crossed[3]]

        def term_for(y):
            block = jnp.zeros_like(terms[0])
            for s in others:
                block = jnp.where((me + s) % n_up == y % n_up, terms[s - 1], block)
            return block

        total = main
        for t in range(n_up):
            by_core = term_for(my_y + t).reshape(n_core, mine, width)
            for k in range(n_core):
                term = lax.dynamic_index_in_dim(by_core, (my_core + k) % n_core, 0, keepdims=False)
                if t or k:
                    pairs = [(low(y, c), low(y + t, (c + k) % n_core)) for y in range(n_up) for c in range(n_core)]
                    term = lax.ppermute(term, "lower", pairs)
                total = total + term
        value = cubed * (total * total) / weight_upper[None, :]
        return jnp.where(allowed, value, jnp.zeros_like(value))

    return local


def solution(mesh):
    return jax.shard_map(
        make_local(mesh.shape["lower"], mesh.shape["upper"], mesh.shape["depth"]),
        mesh=mesh,
        in_specs=(
            P("depth", "lower", "upper"),
            P("depth", "lower", "upper"),
            P(("lower", "depth")),
            P("upper"),
            P(("lower", "depth")),
            P("upper"),
            P(("lower", "depth")),
            P("upper"),
        ),
        out_specs=P(("lower", "depth"), "upper"),
        check_vma=False,
    )
```

time: 124 us -> 111 us (0.90)
  waiting for transfers between devices: 48 us -> 34.8 us
  starting transfers between devices: 37 us -> 42.2 us
  local copies, waits for them, and re-layouts: 8.22 us -> 3.52 us
    ppermute x3, waiting for transfers between devices: 19.6 us -> 3.44 us  [pass_on(): backward.append(lax.ppermute(held_down, 'depth', down[:n_dep - 1 - i]))]
    ppermute x3, waiting for transfers between devices: 1.19 us -> 9.3 us  [pass_on(): forward.append(lax.ppermute(held_up, 'depth', up[i:]))]
    all_to_all x2, starting transfers between devices: 12.7 us -> 17.1 us  [combined(): return (buffer, jnp.sum(lax.all_to_all(by_owner, OWNERS, 0, 0), axis=0))]
    ppermute x2 -> x3, waiting for transfers between devices: 3.71 us -> 0.01 us  [local(): term = lax.ppermute(term, 'lower', pairs)]
    unnamed x30 -> x18, local copies, waits for them, and re-layouts: 4.25 us -> 1.21 us
    ppermute x6 -> x4, waiting for transfers between devices: 9.28 us -> 6.29 us  [shifted(): lax.ppermute(x, 'upper', [((u + shift) % n_up, u) for u in range(n_up)])]
    all_to_all x1, starting transfers between devices: 5.11 us -> 6.8 us  [local(): sorted_tail = lax.all_to_all(tail_rows, 'depth', 0, 0)]
    slice x2, local copies, waits for them, and re-layouts: 3.95 us -> 2.29 us  [the longest x1 1.21 us: local(): up_tail = after(upper_rows[main_rows + 2 * unit:], *crossed[0])]
  transfers between devices with their start and end apart: 17 -> 16, of which waited for: 8 -> 7; matrix products, arithmetic and copies ran while one was open for 1% -> 2% of each run, Pallas kernels for 23% -> 25%
where the time goes in v2:
time: 111 us; the launch traced here: 110 us
  starting transfers between devices  42.2 us (38%)
  waiting for transfers between devices  34.8 us (31%)
  Pallas kernels  27.7 us (25%)
  local copies, waits for them, and re-layouts  3.52 us (3%)
  other arithmetic  1.81 us (2%)
    all_to_all x2, starting transfers between devices, combined(): return (buffer, jnp.sum(lax.all_to_all(by_owner, OWNERS, 0, 0), axis=0))  17.1 us
    all_to_all x2, waiting for transfers between devices, combined(): return (buffer, jnp.sum(lax.all_to_all(by_owner, OWNERS, 0, 0), axis=0))  15.7 us
    ppermute x3, waiting for transfers between devices, pass_on(): forward.append(lax.ppermute(held_up, 'depth', up[i:]))  9.3 us
    pallas_call x2, Pallas kernels, turned_product(): pl.pallas_call(body, grid_spec=pltpu.PrefetchScalarGridSpec(num_scalar_pr...  9.29 us
    pallas_call x1, Pallas kernels, own_product(): pl.pallas_call(body, grid_spec=pltpu.PrefetchScalarGridSpec(num_scalar_pr...  6.88 us
    all_to_all x1, starting transfers between devices, local(): sorted_tail = lax.all_to_all(tail_rows, 'depth', 0, 0)  6.8 us
    pallas_call x1, Pallas kernels, turn(): pl.pallas_call(body, grid=(mains + 1,), in_specs=[pl.BlockSpec((block, co...  6.65 us
    ppermute x3, starting transfers between devices, pass_on(): forward.append(lax.ppermute(held_up, 'depth', up[i:]))  6.64 us
  transfers between devices with their start and end apart: 16, of which 7 were waited for; matrix products, arithmetic and copies ran while one was open for 2% of the time, Pallas kernels for 25%

profile of v2, /device:TPU:0, one launch (start us, length us, event | category | flops | bytes accessed | tf_op | source)
XLA Modules:
  0.0 110.2 jit_solution(18343752643816211484)
XLA Ops:
  0.0 1.1 slice_bitcast_fusion.1
  1.1 3.0 %collective-permute-start = (bf16[1024,256]{1,0:T(8,128)(2,1)S(1)}, bf16[1024,256]{1,0:T(8,128)(2,1)S(1)}, u32[]{:S(2)}, u32[]{:S(2)}) collective-permute-start(bf16[1024,256]{1,0:T(8,128)(2,1)S(1)} %slice_bitcast_fusion.1), channel_id=1, source_target_pairs={{4,0},{0,4},{5,1},{1,5},{6,2},{2,6},{7,3},{3,7},{12,8},{8,12},{13,... | collective-permute-start | bytes 1572872 | tf_op jit(solution)/shard_map/ppermute | solution.py:239
  4.1 6.7 %shard_map.82 = (bf16[128,6144]{1,0:T(8,128)(2,1)}, bf16[128,6144]{1,0:T(8,128)(2,1)S(1)}, bf16[4,64,1024]{2,1,0:T(8,128)(2,1)}) custom-call(bf16[8192,256]{1,0:T(8,128)(2,1)} %bitcast.25), custom_call_target="tpu_custom_call" | custom-call | bytes 30000 | tf_op jit(solution)/shard_map/pallas_call | solution.py:59
  10.7 0.0 copy-start.2
  10.7 1.2 %copy-done.2 = bf16[128,6144]{1,0:T(8,128)(2,1)} copy-done((bf16[128,6144]{1,0:T(8,128)(2,1)}, bf16[128,6144]{1,0:T(8,128)(2,1)S(1)}, u32[]{:S(2)}) %copy-start.2) | copy-done | bytes 1572888
  11.9 4.1 %collective-permute-done.low = bf16[1024,256]{1,0:T(8,128)(2,1)S(1)} collective-permute-done((bf16[1024,256]{1,0:T(8,128)(2,1)S(1)}, bf16[1024,256]{1,0:T(8,128)(2,1)S(1)}, u32[]{:S(2)}, u32[]{:S(2)}) %collective-permute-start) | collective-permute-done | bytes 524320 | tf_op jit(solution)/shard_map/ppermute | solution.py:239
  16.0 0.0 copy-start
  16.0 1.7 %collective-permute-start.1 = (bf16[128,6144]{1,0:T(8,128)(2,1)}, bf16[128,6144]{1,0:T(8,128)(2,1)}, u32[]{:S(2)}, u32[]{:S(2)}) collective-permute-start(bf16[128,6144]{1,0:T(8,128)(2,1)} %get-tuple-element.23), channel_id=1, source_target_pairs={{4,0},{0,4},{5,1},{1,5},{6,2},{2,6},{7,3},{3,7},{12,8},{8,12},{13,... | collective-permute-start | bytes 4718600 | tf_op jit(solution)/shard_map/ppermute | solution.py:239
  17.7 1.2 %slice_bitcast_fusion.mid = bf16[1024,384]{1,0:T(8,128)(2,1)S(1)} fusion(bf16[1,8192,384]{2,1,0:T(8,128)(2,1)} %param.9), kind=kLoop, calls=%fused_computation | loop fusion | bytes 1572864 | tf_op jit(solution)/shard_map/slice | solution.py:290
  19.0 0.0 copy-done
  19.0 3.5 %collective-permute-start.4 = (bf16[1024,384]{1,0:T(8,128)(2,1)S(1)}, bf16[1024,384]{1,0:T(8,128)(2,1)S(1)}, u32[]{:S(2)}, u32[]{:S(2)}) collective-permute-start(bf16[1024,384]{1,0:T(8,128)(2,1)S(1)} %slice_bitcast_fusion.mid), channel_id=1, source_target_pairs={{0,1},{1,2},{2,3},{4,5},{5,6},{6,7},{8,9},{9,10},{10,11},{12,13},{... | collective-permute-start | bytes 2359304 | tf_op jit(solution)/shard_map/ppermute | solution.py:282
  22.5 1.3 %collective-permute-start.7 = (bf16[1024,384]{1,0:T(8,128)(2,1)S(1)}, bf16[1024,384]{1,0:T(8,128)(2,1)}, u32[]{:S(2)}, u32[]{:S(2)}) collective-permute-start(bf16[1024,384]{1,0:T(8,128)(2,1)S(1)} %slice_bitcast_fusion.mid), channel_id=1, source_target_pairs={{1,0},{2,1},{3,2},{5,4},{6,5},{7,6},{9,8},{10,9},{11,10},{13,12},{... | collective-permute-start | bytes 2359304 | tf_op jit(solution)/shard_map/ppermute | solution.py:283
  23.8 6.8 %all-to-all-start = ((bf16[4,64,1024]{2,1,0:T(8,128)(2,1)}), bf16[4,64,1024]{2,1,0:T(8,128)(2,1)}, u32[]{:S(2)}, u32[]{:S(2)}) async-start(bf16[4,64,1024]{2,1,0:T(8,128)(2,1)} %get-tuple-element.27), calls=%async_computation | async-start | bytes 1048576 | tf_op jit(solution)/shard_map/all_to_all | solution.py:294
  30.6 0.5 collective-permute-start.2
  31.1 9.3 %collective-permute-done.4.refs_0_ = bf16[1024,384]{1,0:T(8,128)(2,1)S(1)} collective-permute-done((bf16[1024,384]{1,0:T(8,128)(2,1)S(1)}, bf16[1024,384]{1,0:T(8,128)(2,1)S(1)}, u32[]{:S(2)}, u32[]{:S(2)}) %collective-permute-start.4) | collective-permute-done | bytes 786464 | tf_op jit(solution)/shard_map/ppermute | solution.py:282
  40.4 1.5 %collective-permute-start.5 = (bf16[1024,384]{1,0:T(8,128)(2,1)S(1)}, bf16[1024,384]{1,0:T(8,128)(2,1)}, u32[]{:S(2)}, u32[]{:S(2)}) collective-permute-start(bf16[1024,384]{1,0:T(8,128)(2,1)S(1)} %collective-permute-done.4.refs_0_), channel_id=1, source_target_pairs={{1,2},{2,3},{5,6},{6,7},{9,10},{10,11},{13,14},{14,15},{17,18},{18... | collective-permute-start | bytes 2359304 | tf_op jit(solution)/shard_map/ppermute | solution.py:282
  42.0 3.4 %collective-permute-done.7.refs_3_ = bf16[1024,384]{1,0:T(8,128)(2,1)} collective-permute-done((bf16[1024,384]{1,0:T(8,128)(2,1)S(1)}, bf16[1024,384]{1,0:T(8,128)(2,1)}, u32[]{:S(2)}, u32[]{:S(2)}) %collective-permute-start.7) | collective-permute-done | bytes 786464 | tf_op jit(solution)/shard_map/ppermute | solution.py:283
  45.4 1.3 %collective-permute-start.8 = (bf16[1024,384]{1,0:T(8,128)(2,1)}, bf16[1024,384]{1,0:T(8,128)(2,1)}, u32[]{:S(2)}, u32[]{:S(2)}) collective-permute-start(bf16[1024,384]{1,0:T(8,128)(2,1)} %collective-permute-done.7.refs_3_), channel_id=1, source_target_pairs={{1,0},{2,1},{5,4},{6,5},{9,8},{10,9},{13,12},{14,13},{17,16},{18,1... | collective-permute-start | bytes 2359304 | tf_op jit(solution)/shard_map/ppermute | solution.py:283
  46.7 0.0 copy-start.1
  46.7 6.9 %shard_map.84 = (f32[2,128,384]{2,1,0:T(8,128)}, f32[2,128,384]{2,1,0:T(8,128)}) custom-call(s32[1]{0:T(128)} %bitcast.4.at, bf16[8192,256]{1,0:T(8,128)(2,1)} %bitcast.26, bf16[8192,384]{1,0:T(8,128)(2,1)} %bitcast.21), custom_call_target="tpu_custom_call" | custom-call | bytes 30000 | tf_op jit(solution)/shard_map/pallas_call | solution.py:102
  53.6 0.0 copy-done.1
  53.6 1.6 %shard_map.83 = (f32[128,384]{1,0:T(8,128)S(1)}, f32[128,384]{1,0:T(8,128)S(1)}) custom-call(bf16[1024,256]{1,0:T(8,128)(2,1)S(1)} %copy-done.1, bf16[8192,384]{1,0:T(8,128)(2,1)} %bitcast.22), custom_call_target="tpu_custom_call" | custom-call | bytes 30000 | tf_op jit(solution)/shard_map/pallas_call | solution.py:144
  55.2 0.0 collective-permute-done.1.low
  55.2 4.8 %shard_map.85 = f32[2,128,384]{2,1,0:T(8,128)} custom-call(s32[1]{0:T(128)} %bitcast.at, bf16[128,6144]{1,0:T(8,128)(2,1)} %collective-permute-done.1.low, bf16[8192,384]{1,0:T(8,128)(2,1)} %bitcast.23, f32[128,384]{1,0:T(8,128)S(1)} %get-tuple-element.24.before, f32[2,128,384]{2,1,0:T(8,128)} %get-tuple-element.26._), custom_call_target="tpu_custom_call", output_to_operand_aliasing={{}: (4, {})} | custom-call | bytes 30000 | tf_op jit(solution)/shard_map/pallas_call | solution.py:182
  60.0 0.0 all-to-all-done
  60.0 10.6 %all-to-all-start.1 = ((f32[16,16,384]{2,1,0:T(8,128)}), f32[16,16,384]{2,1,0:T(8,128)}, u32[]{:S(2)}, u32[]{:S(2)}) async-start(f32[16,16,384]{2,1,0:T(8,128)} %bitcast.5), calls=%async_computation.1 | async-start | bytes 786432 | tf_op jit(solution)/shard_map/all_to_all | solution.py:306
  70.7 0.0 collective-permute-done.5.refs_1_
  70.7 1.6 %collective-permute-start.6 = (bf16[1024,384]{1,0:T(8,128)(2,1)}, bf16[1024,384]{1,0:T(8,128)(2,1)}, u32[]{:S(2)}, u32[]{:S(2)}) collective-permute-start(bf16[1024,384]{1,0:T(8,128)(2,1)} %collective-permute-done.5.refs_1_), channel_id=1, source_target_pairs={{2,3},{6,7},{10,11},{14,15},{18,19},{22,23},{26,27},{30,31}} | collective-permute-start | bytes 2359304 | tf_op jit(solution)/shard_map/ppermute | solution.py:282
  72.2 0.0 collective-permute-done.8.refs_4_
  72.2 1.3 %collective-permute-start.9 = (bf16[1024,384]{1,0:T(8,128)(2,1)}, bf16[1024,384]{1,0:T(8,128)(2,1)}, u32[]{:S(2)}, u32[]{:S(2)}) collective-permute-start(bf16[1024,384]{1,0:T(8,128)(2,1)} %collective-permute-done.8.refs_4_), channel_id=1, source_target_pairs={{1,0},{5,4},{9,8},{13,12},{17,16},{21,20},{25,24},{29,28}} | collective-permute-start | bytes 2359304 | tf_op jit(solution)/shard_map/ppermute | solution.py:283
  73.5 10.1 %all-to-all-done.1 = f32[16,16,384]{2,1,0:T(8,128)} async-done(((f32[16,16,384]{2,1,0:T(8,128)}), f32[16,16,384]{2,1,0:T(8,128)}, u32[]{:S(2)}, u32[]{:S(2)}) %all-to-all-start.1) | async-done | bytes 393248 | tf_op jit(solution)/shard_map/all_to_all | solution.py:306
  83.6 1.0 reduce_sum.18
  84.6 0.6 collective-permute-start.3
  85.2 0.3 collective-permute-done.2.low
  85.5 0.0 copy-start.3
  85.5 4.5 %shard_map.86 = f32[2,128,384]{2,1,0:T(8,128)} custom-call(s32[1]{0:T(128)} %bitcast.at, bf16[128,6144]{1,0:T(8,128)(2,1)S(1)} %collective-permute-done.2.low, bf16[8192,384]{1,0:T(8,128)(2,1)} %bitcast.24, f32[128,384]{1,0:T(8,128)S(1)} %get-tuple-element.31.before, f32[2,128,384]{2,1,0:T(8,128)} %get-tuple-element.32._), custom_call_target="tpu_custom_call", output_to_operand_aliasing={{}: (4, {})} | custom-call | bytes 30000 | tf_op jit(solution)/shard_map/pallas_call | solution.py:182
  90.0 0.0 copy-start.8
  90.0 0.0 copy-start.4
  90.0 0.0 copy-start.5
  90.0 0.0 copy-start.6
  90.0 0.0 copy-start.7
  90.0 6.5 %all-to-all-start.2 = ((f32[16,16,384]{2,1,0:T(8,128)}), f32[16,16,384]{2,1,0:T(8,128)S(1)}, u32[]{:S(2)}, u32[]{:S(2)}) async-start(f32[16,16,384]{2,1,0:T(8,128)} %bitcast.6), calls=%async_computation.2 | async-start | bytes 786432 | tf_op jit(solution)/shard_map/all_to_all | solution.py:306
  96.5 0.0 copy-done.3
  96.6 1.9 %collective-permute-done.3.low = bf16[4,64,1024]{2,1,0:T(8,128)(2,1)} collective-permute-done((bf16[4,64,1024]{2,1,0:T(8,128)(2,1)}, bf16[4,64,1024]{2,1,0:T(8,128)(2,1)}, u32[]{:S(2)}, u32[]{:S(2)}) %collective-permute-start.3) | collective-permute-done | bytes 524320 | tf_op jit(solution)/shard_map/ppermute | solution.py:239
  98.5 0.0 collective-permute-done.6.refs_2_
  98.5 0.0 collective-permute-done.9.refs_5_
  98.5 3.2 %shard_map.87 = f32[64,384]{1,0:T(8,128)S(1)} custom-call(s32[1]{0:T(128)} %bitcast.7.at, bf16[4,64,1024]{2,1,0:T(8,128)(2,1)} %collective-permute-done.3.low, bf16[1024,384]{1,0:T(8,128)(2,1)S(1)} %slice_bitcast_fusion.mid, bf16[1024,384]{1,0:T(8,128)(2,1)S(1)} %collective-permute-done.4.refs_0_, bf16[1024,384]{1,0:T(8,128)(2,1)} %collective-permute-done.5.refs_1_, ...), custom_call_target="tpu_custom_call" | custom-call | bytes 30000 | tf_op jit(solution)/shard_map/pallas_call | solution.py:223
  101.8 0.6 collective-permute-start.12
  102.4 0.8 collective-permute-start.11
  103.3 0.5 collective-permute-start.10
  103.7 0.0 copy-done.8
  103.8 5.6 %all-to-all-done.2 = f32[16,16,384]{2,1,0:T(8,128)S(1)} async-done(((f32[16,16,384]{2,1,0:T(8,128)}), f32[16,16,384]{2,1,0:T(8,128)S(1)}, u32[]{:S(2)}, u32[]{:S(2)}) %all-to-all-start.2) | async-done | bytes 393248 | tf_op jit(solution)/shard_map/all_to_all | solution.py:306
  109.4 0.0 collective-permute-done.12
  109.4 0.0 collective-permute-done.11
  109.5 0.0 collective-permute-done.10
  109.5 0.0 copy-done.4
  109.5 0.0 copy-done.5
  109.5 0.0 copy-done.6
  109.5 0.0 copy-done.7
  109.5 0.7 fusion.2
  (6 shorter events, 0.1 us)
Async XLA Ops:
  1.1 14.9 %collective-permute-start = (bf16[1024,256]{1,0:T(8,128)(2,1)S(1)}, bf16[1024,256]{1,0:T(8,128)(2,1)S(1)}, u32[]{:S(2)}, u32[]{:S(2)}) collective-permute-start(bf16[1024,256]{1,0:T(8,128)(2,1)S(1)} %slice_bitcast_fusion.1), channel_id=1, source_target_pairs={{4,0},{0,4},{5,1},{1,5},{6,2},{2,6},{7,3},{3,7},{12,8},{8,12},{13,... | collective-permute-start | bytes 1572872 | tf_op jit(solution)/shard_map/ppermute | solution.py:239
  10.7 1.2 %copy-start.2 = (bf16[128,6144]{1,0:T(8,128)(2,1)}, bf16[128,6144]{1,0:T(8,128)(2,1)S(1)}, u32[]{:S(2)}) copy-start(bf16[128,6144]{1,0:T(8,128)(2,1)S(1)} %get-tuple-element.30) | copy-start | bytes 4718596
  16.0 3.0 %copy-start = (bf16[1024,256]{1,0:T(8,128)(2,1)}, bf16[1024,256]{1,0:T(8,128)(2,1)S(1)}, u32[]{:S(2)}) copy-start(bf16[1024,256]{1,0:T(8,128)(2,1)S(1)} %collective-permute-done.low) | copy-start | bytes 1572868
  16.0 39.2 %collective-permute-start.1 = (bf16[128,6144]{1,0:T(8,128)(2,1)}, bf16[128,6144]{1,0:T(8,128)(2,1)}, u32[]{:S(2)}, u32[]{:S(2)}) collective-permute-start(bf16[128,6144]{1,0:T(8,128)(2,1)} %get-tuple-element.23), channel_id=1, source_target_pairs={{4,0},{0,4},{5,1},{1,5},{6,2},{2,6},{7,3},{3,7},{12,8},{8,12},{13,... | collective-permute-start | bytes 4718600 | tf_op jit(solution)/shard_map/ppermute | solution.py:239
  19.0 21.5 %collective-permute-start.4 = (bf16[1024,384]{1,0:T(8,128)(2,1)S(1)}, bf16[1024,384]{1,0:T(8,128)(2,1)S(1)}, u32[]{:S(2)}, u32[]{:S(2)}) collective-permute-start(bf16[1024,384]{1,0:T(8,128)(2,1)S(1)} %slice_bitcast_fusion.mid), channel_id=1, source_target_pairs={{0,1},{1,2},{2,3},{4,5},{5,6},{6,7},{8,9},{9,10},{10,11},{12,13},{... | collective-permute-start | bytes 2359304 | tf_op jit(solution)/shard_map/ppermute | solution.py:282
  22.5 22.9 %collective-permute-start.7 = (bf16[1024,384]{1,0:T(8,128)(2,1)S(1)}, bf16[1024,384]{1,0:T(8,128)(2,1)}, u32[]{:S(2)}, u32[]{:S(2)}) collective-permute-start(bf16[1024,384]{1,0:T(8,128)(2,1)S(1)} %slice_bitcast_fusion.mid), channel_id=1, source_target_pairs={{1,0},{2,1},{3,2},{5,4},{6,5},{7,6},{9,8},{10,9},{11,10},{13,12},{... | collective-permute-start | bytes 2359304 | tf_op jit(solution)/shard_map/ppermute | solution.py:283
  23.8 36.2 %all-to-all-start = ((bf16[4,64,1024]{2,1,0:T(8,128)(2,1)}), bf16[4,64,1024]{2,1,0:T(8,128)(2,1)}, u32[]{:S(2)}, u32[]{:S(2)}) async-start(bf16[4,64,1024]{2,1,0:T(8,128)(2,1)} %get-tuple-element.27), calls=%async_computation | async-start | bytes 1048576 | tf_op jit(solution)/shard_map/all_to_all | solution.py:294
  30.6 54.9 %collective-permute-start.2 = (bf16[128,6144]{1,0:T(8,128)(2,1)}, bf16[128,6144]{1,0:T(8,128)(2,1)S(1)}, u32[]{:S(2)}, u32[]{:S(2)}) collective-permute-start(bf16[128,6144]{1,0:T(8,128)(2,1)} %copy-done.2), channel_id=1, source_target_pairs={{4,0},{0,4},{5,1},{1,5},{6,2},{2,6},{7,3},{3,7},{12,8},{8,12},{13,... | collective-permute-start | bytes 4718600 | tf_op jit(solution)/shard_map/ppermute | solution.py:239
  40.4 30.2 %collective-permute-start.5 = (bf16[1024,384]{1,0:T(8,128)(2,1)S(1)}, bf16[1024,384]{1,0:T(8,128)(2,1)}, u32[]{:S(2)}, u32[]{:S(2)}) collective-permute-start(bf16[1024,384]{1,0:T(8,128)(2,1)S(1)} %collective-permute-done.4.refs_0_), channel_id=1, source_target_pairs={{1,2},{2,3},{5,6},{6,7},{9,10},{10,11},{13,14},{14,15},{17,18},{18... | collective-permute-start | bytes 2359304 | tf_op jit(solution)/shard_map/ppermute | solution.py:282
  45.4 26.8 %collective-permute-start.8 = (bf16[1024,384]{1,0:T(8,128)(2,1)}, bf16[1024,384]{1,0:T(8,128)(2,1)}, u32[]{:S(2)}, u32[]{:S(2)}) collective-permute-start(bf16[1024,384]{1,0:T(8,128)(2,1)} %collective-permute-done.7.refs_3_), channel_id=1, source_target_pairs={{1,0},{2,1},{5,4},{6,5},{9,8},{10,9},{13,12},{14,13},{17,16},{18,1... | collective-permute-start | bytes 2359304 | tf_op jit(solution)/shard_map/ppermute | solution.py:283
  46.7 6.9 %copy-start.1 = (bf16[1024,256]{1,0:T(8,128)(2,1)S(1)}, bf16[1024,256]{1,0:T(8,128)(2,1)}, u32[]{:S(2)}) copy-start(bf16[1024,256]{1,0:T(8,128)(2,1)} %copy-done) | copy-start | bytes 1572868
  60.0 23.6 %all-to-all-start.1 = ((f32[16,16,384]{2,1,0:T(8,128)}), f32[16,16,384]{2,1,0:T(8,128)}, u32[]{:S(2)}, u32[]{:S(2)}) async-start(f32[16,16,384]{2,1,0:T(8,128)} %bitcast.5), calls=%async_computation.1 | async-start | bytes 786432 | tf_op jit(solution)/shard_map/all_to_all | solution.py:306
  70.7 27.9 %collective-permute-start.6 = (bf16[1024,384]{1,0:T(8,128)(2,1)}, bf16[1024,384]{1,0:T(8,128)(2,1)}, u32[]{:S(2)}, u32[]{:S(2)}) collective-permute-start(bf16[1024,384]{1,0:T(8,128)(2,1)} %collective-permute-done.5.refs_1_), channel_id=1, source_target_pairs={{2,3},{6,7},{10,11},{14,15},{18,19},{22,23},{26,27},{30,31}} | collective-permute-start | bytes 2359304 | tf_op jit(solution)/shard_map/ppermute | solution.py:282
  72.2 26.3 %collective-permute-start.9 = (bf16[1024,384]{1,0:T(8,128)(2,1)}, bf16[1024,384]{1,0:T(8,128)(2,1)}, u32[]{:S(2)}, u32[]{:S(2)}) collective-permute-start(bf16[1024,384]{1,0:T(8,128)(2,1)} %collective-permute-done.8.refs_4_), channel_id=1, source_target_pairs={{1,0},{5,4},{9,8},{13,12},{17,16},{21,20},{25,24},{29,28}} | collective-permute-start | bytes 2359304 | tf_op jit(solution)/shard_map/ppermute | solution.py:283
  84.6 13.9 %collective-permute-start.3 = (bf16[4,64,1024]{2,1,0:T(8,128)(2,1)}, bf16[4,64,1024]{2,1,0:T(8,128)(2,1)}, u32[]{:S(2)}, u32[]{:S(2)}) collective-permute-start(bf16[4,64,1024]{2,1,0:T(8,128)(2,1)} %all-to-all-done), channel_id=1, source_target_pairs={{4,0},{0,4},{5,1},{1,5},{6,2},{2,6},{7,3},{3,7},{12,8},{8,12},{13,... | collective-permute-start | bytes 1572872 | tf_op jit(solution)/shard_map/ppermute | solution.py:239
  85.5 11.0 %copy-start.3 = (s32[384]{0:T(512)S(1)}, s32[384]{0:T(512)}, u32[]{:S(2)}) copy-start(s32[384]{0:T(512)} %param.15) | copy-start | bytes 4612
  90.0 13.8 %copy-start.8 = (s32[32]{0:T(128)S(1)}, s32[32]{0:T(128)}, u32[]{:S(2)}) copy-start(s32[32]{0:T(128)} %param.12) | copy-start | bytes 388
  90.0 19.5 %copy-start.4 = (f32[384]{0:T(512)S(1)}, f32[384]{0:T(512)}, u32[]{:S(2)}) copy-start(f32[384]{0:T(512)} %param.11) | copy-start | bytes 4612
  90.0 19.5 %copy-start.5 = (s32[384]{0:T(512)S(1)}, s32[384]{0:T(512)}, u32[]{:S(2)}) copy-start(s32[384]{0:T(512)} %param.13) | copy-start | bytes 4612
  90.0 19.5 %copy-start.6 = (f32[32]{0:T(128)S(1)}, f32[32]{0:T(128)}, u32[]{:S(2)}) copy-start(f32[32]{0:T(128)} %param.10) | copy-start | bytes 388
  90.0 19.5 %copy-start.7 = (s32[32]{0:T(128)S(1)}, s32[32]{0:T(128)}, u32[]{:S(2)}) copy-start(s32[32]{0:T(128)} %param.14) | copy-start | bytes 388
  90.0 19.4 %all-to-all-start.2 = ((f32[16,16,384]{2,1,0:T(8,128)}), f32[16,16,384]{2,1,0:T(8,128)S(1)}, u32[]{:S(2)}, u32[]{:S(2)}) async-start(f32[16,16,384]{2,1,0:T(8,128)} %bitcast.6), calls=%async_computation.2 | async-start | bytes 786432 | tf_op jit(solution)/shard_map/all_to_all | solution.py:306
  101.8 7.6 %collective-permute-start.12 = (f32[32,384]{1,0:T(8,128)S(1)}, f32[32,384]{1,0:T(8,128)S(1)}, u32[]{:S(2)}, u32[]{:S(2)}) collective-permute-start(f32[32,384]{1,0:T(8,128)S(1)} %get-tuple-element.40), channel_id=1, source_target_pairs={{0,24},{8,16},{16,8},{24,0},{1,25},{9,17},{17,9},{25,1},{2,26},{10... | collective-permute-start | bytes 147464 | tf_op jit(solution)/shard_map/ppermute | solution.py:328
  102.4 7.0 %collective-permute-start.11 = (f32[32,384]{1,0:T(8,128)S(1)}, f32[32,384]{1,0:T(8,128)S(1)}, u32[]{:S(2)}, u32[]{:S(2)}) collective-permute-start(f32[32,384]{1,0:T(8,128)S(1)} %get-tuple-element.39), channel_id=1, source_target_pairs={{0,16},{8,24},{16,0},{24,8},{1,17},{9,25},{17,1},{25,9},{2,18},{10... | collective-permute-start | bytes 147464 | tf_op jit(solution)/shard_map/ppermute | solution.py:328
  103.3 6.2 %collective-permute-start.10 = (f32[32,384]{1,0:T(8,128)S(1)}, f32[32,384]{1,0:T(8,128)S(1)}, u32[]{:S(2)}, u32[]{:S(2)}) collective-permute-start(f32[32,384]{1,0:T(8,128)S(1)} %dynamic-slice_bitcast_fusion.2), channel_id=1, source_target_pairs={{0,8},{8,0},{16,24},{24,16},{1,9},{9,1},{17,25},{25,17},{2,10},{10... | collective-permute-start | bytes 147464 | tf_op jit(solution)/shard_map/ppermute | solution.py:328

commit v3 on v2

--- a/solution.py
+++ b/solution.py
@@ -73,48 +73,6 @@
     states, width = product.shape
     by_owner = product.reshape(per_block, parts, states // per_block // parts, width)
     return [by_owner[:, i].reshape(states // parts, width) for i in range(parts)]
-
-
-def own_product(slot, lower_rows, upper_rows, n_up, per_block, parts):
-    rows, cols = lower_rows.shape
-    width = upper_rows.shape[1]
-    steps = 4
-    block = rows // steps
-
-    def body(at, low, up, *refs):
-        outs, total = refs[:-1], refs[-1]
-        i = pl.program_id(0)
-        term = dot(low[...].T, up[...])
-
-        @pl.when(i == 0)
-        def _():
-            total[...] = term
-
-        @pl.when(i > 0)
-        def _():
-            total[...] += term
-
-        @pl.when(i == steps - 1)
-        def _():
-            for out, part in zip(outs, split_states(total[...], per_block, parts)):
-                out[0] = part
-
-    return pl.pallas_call(
-        body,
-        grid_spec=pltpu.PrefetchScalarGridSpec(
-            num_scalar_prefetch=1,
-            grid=(steps,),
-            in_specs=[
-                pl.BlockSpec((block, cols), lambda i, at: (i, 0)),
-                pl.BlockSpec((block, width), lambda i, at: (i, 0)),
-            ],
-            out_specs=[pl.BlockSpec((1, cols // parts, width), lambda i, at: (at[0], 0, 0))] * parts,
-            scratch_shapes=[pltpu.VMEM((cols, width), jnp.float32)],
-        ),
-        out_shape=[jax.ShapeDtypeStruct((n_up, cols // parts, width), jnp.float32)] * parts,
-        compiler_params=params(),
-        cost_estimate=cost(0.01),
-    )(slot.reshape(1), in_hbm(lower_rows), in_hbm(upper_rows))
 
 
 def rows_product(got, upper_rows, first, block, so_far, per_block, parts):
@@ -157,83 +115,111 @@
     )(got, in_hbm(upper_rows), *so_far)
 
 
-def turned_product(slot, got, upper_rows, so_far, buffer):
-    states, k = got.shape
+def turned_products(me, core, own, so_far, got, upper_rows, n_core):
+    n_up = 1 + len(got)
+    states, k = got[0].shape
     width = upper_rows.shape[1]
     steps = 3
     block = k // steps
-
-    def body(at, low, up, before, _, out, total):
-        i = pl.program_id(0)
-        term = dot(low[...], up[...])
-
-        @pl.when(i == 0)
-        def _():
-            total[...] = before[...] + term
-
-        @pl.when((i > 0) & (i < steps - 1))
-        def _():
-            total[...] += term
-
-        @pl.when(i == steps - 1)
-        def _():
-            out[0] = total[...] + term
-
+    share = states // n_core
+
+    def body(me_at, core_at, mine, up, *refs):
+        befores, lows_at = refs[: n_up - 1], refs[n_up - 1 : 2 * n_up - 2]
+        outs = refs[2 * n_up - 2 : 2 * n_up - 2 + n_core]
+        lows, ups, sems = refs[2 * n_up - 2 + n_core :]
+
+        def start(source, target, sem):
+            copy = pltpu.make_async_copy(source, target, sem)
+            copy.start()
+            return copy
+
+        copies = []
+        for j in range(steps):
+            span = pl.ds(j * block, block)
+            copies.append(
+                [start(up.at[span], ups.at[j], sems.at[0, j])]
+                + [start(low.at[:, span], lows.at[i, j], sems.at[i + 1, j]) for i, low in enumerate(lows_at)]
+            )
+
+        def put(slot, product):
+            by_core = product.reshape(n_core, share, width)
+            for c in range(n_core):
+                for t, out in enumerate(outs):
+
+                    @pl.when(lax.rem(core_at[0] + t, n_core) == c)
+                    def _():
+                        out[slot] = by_core[c]
+
+        put(me_at[0], mine[...])
+        totals = [before[...] for before in befores]
+        for j, group in enumerate(copies):
+            for copy in group:
+                copy.wait()
+            totals = [total + dot(lows[i, j], ups[j]) for i, total in enumerate(totals)]
+        for i, total in enumerate(totals):
+            put(lax.rem(me_at[0] + 1 + i, n_up), total)
+
+    vmem, hbm = pl.BlockSpec(memory_space=pltpu.VMEM), pl.BlockSpec(memory_space=pltpu.HBM)
     return pl.pallas_call(
         body,
-        grid_spec=pltpu.PrefetchScalarGridSpec(
-            num_scalar_prefetch=1,
-            grid=(steps,),
-            in_specs=[
-                pl.BlockSpec((states, block), lambda i, at: (0, i)),
-                pl.BlockSpec((block, width), lambda i, at: (i, 0)),
-                whole((states, width)),
-                pl.BlockSpec(memory_space=pl.ANY),
-            ],
-            out_specs=pl.BlockSpec((1, states, width), lambda i, at: (at[0], 0, 0)),
-            scratch_shapes=[pltpu.VMEM((states, width), jnp.float32)],
-        ),
-        out_shape=jax.ShapeDtypeStruct(buffer.shape, buffer.dtype),
-        input_output_aliases={4: 0},
+        in_specs=[pl.BlockSpec(memory_space=pltpu.SMEM)] * 2 + [vmem, hbm] + [vmem] * (n_up - 1) + [hbm] * (n_up - 1),
+        out_specs=[vmem] * n_core,
+        out_shape=[jax.ShapeDtypeStruct((n_up, share, width), jnp.float32)] * n_core,
+        scratch_shapes=[
+            pltpu.VMEM((n_up - 1, steps, states, block), got[0].dtype),
+            pltpu.VMEM((steps, block, width), upper_rows.dtype),
+            pltpu.SemaphoreType.DMA((n_up, steps)),
+        ],
         compiler_params=params(),
         cost_estimate=cost(0.01),
-    )(slot.reshape(1), got, in_hbm(upper_rows), so_far, buffer)
+    )(me.reshape(1), core.reshape(1), own, in_hbm(upper_rows), *so_far, *got)
 
 
 def tail_product(depth, got, own, forward, backward):
     n_dep, states, k = got.shape
     width = own.shape[1]
-    n = len(forward)
+    n = n_dep - 1
 
     def body(at, low, mid, *refs):
+        out, lows, ups, sems = refs[2 * n :]
         z = at[0]
-        out = refs[-1]
-        out[...] = dot(low[z], mid[...])
-        for i in range(n):
-
-            @pl.when(z > i)
-            def _():
-                out[...] += dot(low[z - 1 - i], refs[i][...])
-
-            @pl.when(z + 1 + i < n_dep)
-            def _():
-                out[...] += dot(low[z + 1 + i], refs[n + i][...])
-
-    vmem = pl.BlockSpec(memory_space=pltpu.VMEM)
+        of_low = pltpu.make_async_copy(low, lows, sems.at[n_dep])
+        of_low.start()
+        copies = [pltpu.make_async_copy(mid, ups.at[0], sems.at[0])]
+        copies[0].start()
+        for j in range(1, n_dep):
+            down = pltpu.make_async_copy(refs[n + j - 1], ups.at[j], sems.at[j])
+            round_ = pltpu.make_async_copy(refs[n - j], ups.at[j], sems.at[j])
+            pl.when(z + j < n_dep)(down.start)
+            pl.when(z + j >= n_dep)(round_.start)
+            copies.append(down)
+        of_low.wait()
+        total = jnp.zeros((states, width), jnp.float32)
+        for j, copy in enumerate(copies):
+            copy.wait()
+            total = total + dot(lows[lax.rem(z + j, n_dep)], ups[j])
+        out[...] = total
+
+    hbm = pl.BlockSpec(memory_space=pltpu.HBM)
     return pl.pallas_call(
         body,
-        in_specs=[pl.BlockSpec(memory_space=pltpu.SMEM)] + [vmem] * (2 + 2 * n),
-        out_specs=vmem,
+        in_specs=[pl.BlockSpec(memory_space=pltpu.SMEM)] + [hbm] * (2 + 2 * n),
+        out_specs=pl.BlockSpec(memory_space=pltpu.VMEM),
         out_shape=jax.ShapeDtypeStruct((states, width), jnp.float32),
+        scratch_shapes=[
+            pltpu.VMEM((n_dep, states, k), got.dtype),
+            pltpu.VMEM((n_dep, k, width), own.dtype),
+            pltpu.SemaphoreType.DMA((n_dep + 1,)),
+        ],
         compiler_params=params(),
         cost_estimate=cost(0.01),
     )(depth.reshape(1), got, own, *forward, *backward)
 
 
 def make_local(n_low, n_up, n_dep):
-    n_owners = n_low * n_dep
     n_core = n_low // n_up
     others = range(1, n_up)
+    same_core = [[(y * n_core + c) * n_dep + z for y in range(n_up) for z in range(n_dep)] for c in range(n_core)]
 
     def shifted(x, shift):
         return lax.ppermute(x, "upper", [((u + shift) % n_up, u) for u in range(n_up)])
@@ -292,22 +278,23 @@
         for i in range(1, n_dep - 1):
             pass_on(forward[-1], backward[-1])
         sorted_tail = lax.all_to_all(tail_rows, "depth", 0, 0)
-        buffers = own_product(me, after(later_rows, turned[0]), upper_rows, n_up, per_block, 2)
+        own = rows_product(after(later_rows, turned[0]), upper_rows, 0, 4 * unit, (), per_block, 2)
         cross(turned[1])
         so_far = [rows_product(g, upper_rows, main_rows, 2 * unit, (), per_block, 2) for g in crossed[0]]
 
-        def combined(i, got, *others_first):
-            buffer = buffers[i]
-            for s in others:
-                slot = (me + s) % n_up
-                buffer = turned_product(slot, got[s - 1], upper_rows, so_far[s - 1][i], buffer)
-            buffer = after(buffer, *others_first) if others_first else buffer
-            by_owner = buffer.reshape(n_owners, half, width)
-            return buffer, jnp.sum(lax.all_to_all(by_owner, OWNERS, 0, 0), axis=0)
-
-        _, sum_a = combined(0, crossed[1], sorted_tail)
+        def reduced(i, got, *others_first):
+            mine_of, *for_others = turned_products(me, my_core, own[i], [x[i] for x in so_far], got, upper_rows, n_core)
+            total = mine_of
+            for k, leaving in enumerate(for_others, 1):
+                pairs = [(low(y, c), low(y, (c + k) % n_core)) for y in range(n_up) for c in range(n_core)]
+                total = total + lax.ppermute(leaving, "lower", pairs)
+            total = after(total, *others_first)
+            by_owner = total.reshape(n_up * n_dep, half, width)
+            return total, jnp.sum(lax.all_to_all(by_owner, OWNERS, 0, 0, axis_index_groups=same_core), axis=0)
+
+        _, sum_a = reduced(0, crossed[1], sorted_tail)
         cross(sorted_tail, sum_a)
-        last, sum_b = combined(1, crossed[2], sum_a)
+        last, sum_b = reduced(1, crossed[2], sum_a)
         main = jnp.concatenate([sum_a, sum_b], axis=0)
 
         terms = [tail_product(depth, after(g, last), up_tail, forward, backward) for g in crossed[3]]

time: 111 us -> 109 us (0.982)
  Pallas kernels: 27.7 us -> 22.1 us
  waiting for transfers between devices: 34.8 us -> 37.4 us
  starting transfers between devices: 42.2 us -> 40 us
  other arithmetic: 1.81 us -> 3.7 us
    pallas_call x3 -> x2, Pallas kernels: 16.2 us -> 6.16 us  [turned_products(): pl.pallas_call(body, in_specs=[pl.BlockSpec(memory_space=pltpu.SMEM)] * 2...]
    ppermute x3, waiting for transfers between devices: 9.3 us -> 0.01 us  [pass_on(): forward.append(lax.ppermute(held_up, 'depth', up[i:]))]
    ppermute x3, waiting for transfers between devices: 3.44 us -> 12.2 us  [pass_on(): backward.append(lax.ppermute(held_down, 'depth', down[:n_dep - 1 - i]))]
    ppermute x4, waiting for transfers between devices: 6.29 us -> 12 us  [shifted(): lax.ppermute(x, 'upper', [((u + shift) % n_up, u) for u in range(n_up)])]
    pallas_call x1 -> x2, Pallas kernels: 1.6 us -> 6.99 us  [rows_product(): pl.pallas_call(body, grid=(steps,), in_specs=[pl.BlockSpec((block, states...]
    all_to_all x2, waiting for transfers between devices: 15.7 us -> 10.4 us  [reduced(): lax.all_to_all(by_owner, OWNERS, 0, 0, axis_index_groups=same_core)]
    ppermute x0 -> x2, waiting for transfers between devices: none -> 2.83 us  [reduced(): total = total + lax.ppermute(leaving, 'lower', pairs)]
    all_to_all x1, starting transfers between devices: 6.8 us -> 4.14 us  [local(): sorted_tail = lax.all_to_all(tail_rows, 'depth', 0, 0)]
  transfers between devices with their start and end apart: 16 -> 18, of which waited for: 7 -> 7; matrix products, arithmetic and copies ran while one was open for 2% -> 4% of each run, Pallas kernels for 25% -> 20%
where the time goes in v3:
time: 109 us; the launch traced here: 108 us
  starting transfers between devices  40 us (37%)
  waiting for transfers between devices  37.4 us (34%)
  Pallas kernels  22.1 us (20%)
  local copies, waits for them, and re-layouts  4.56 us (4%)
  other arithmetic  3.7 us (3%)
    all_to_all x2, starting transfers between devices, reduced(): lax.all_to_all(by_owner, OWNERS, 0, 0, axis_index_groups=same_core)  15.4 us
    ppermute x3, waiting for transfers between devices, pass_on(): backward.append(lax.ppermute(held_down, 'depth', down[:n_dep - 1 - i]))  12.2 us
    ppermute x4, waiting for transfers between devices, shifted(): lax.ppermute(x, 'upper', [((u + shift) % n_up, u) for u in range(n_up)])  12 us
    all_to_all x2, waiting for transfers between devices, reduced(): lax.all_to_all(by_owner, OWNERS, 0, 0, axis_index_groups=same_core)  10.4 us
    ppermute x3, starting transfers between devices, pass_on(): forward.append(lax.ppermute(held_up, 'depth', up[i:]))  8.63 us
    pallas_call x2, Pallas kernels, rows_product(): pl.pallas_call(body, grid=(steps,), in_specs=[pl.BlockSpec((block, states...  6.99 us
    pallas_call x1, Pallas kernels, turn(): pl.pallas_call(body, grid=(mains + 1,), in_specs=[pl.BlockSpec((block, co...  6.9 us
    pallas_call x2, Pallas kernels, turned_products(): pl.pallas_call(body, in_specs=[pl.BlockSpec(memory_space=pltpu.SMEM)] * 2...  6.16 us
  transfers between devices with their start and end apart: 18, of which 7 were waited for; matrix products, arithmetic and copies ran while one was open for 4% of the time, Pallas kernels for 20%

profile of v3, /device:TPU:0, one launch (start us, length us, event | category | flops | bytes accessed | tf_op | source)
XLA Modules:
  0.0 108.1 jit_solution(4738780969929204448)
XLA Ops:
  0.0 1.1 slice_bitcast_fusion.1
  1.1 3.0 %collective-permute-start = (bf16[1024,256]{1,0:T(8,128)(2,1)S(1)}, bf16[1024,256]{1,0:T(8,128)(2,1)S(1)}, u32[]{:S(2)}, u32[]{:S(2)}) collective-permute-start(bf16[1024,256]{1,0:T(8,128)(2,1)S(1)} %slice_bitcast_fusion.1), channel_id=1, source_target_pairs={{4,0},{0,4},{5,1},{1,5},{6,2},{2,6},{7,3},{3,7},{12,8},{8,12},{13,... | collective-permute-start | bytes 1572872 | tf_op jit(solution)/shard_map/ppermute | solution.py:225
  4.1 6.9 %shard_map.82 = (bf16[128,6144]{1,0:T(8,128)(2,1)}, bf16[128,6144]{1,0:T(8,128)(2,1)}, bf16[4,64,1024]{2,1,0:T(8,128)(2,1)S(1)}) custom-call(bf16[8192,256]{1,0:T(8,128)(2,1)} %bitcast.21), custom_call_target="tpu_custom_call" | custom-call | bytes 30000 | tf_op jit(solution)/shard_map/pallas_call | solution.py:59
  11.0 5.0 %collective-permute-done.low = bf16[1024,256]{1,0:T(8,128)(2,1)S(1)} collective-permute-done((bf16[1024,256]{1,0:T(8,128)(2,1)S(1)}, bf16[1024,256]{1,0:T(8,128)(2,1)S(1)}, u32[]{:S(2)}, u32[]{:S(2)}) %collective-permute-start) | collective-permute-done | bytes 524320 | tf_op jit(solution)/shard_map/ppermute | solution.py:225
  16.0 1.7 %collective-permute-start.1 = (bf16[128,6144]{1,0:T(8,128)(2,1)}, bf16[128,6144]{1,0:T(8,128)(2,1)}, u32[]{:S(2)}, u32[]{:S(2)}) collective-permute-start(bf16[128,6144]{1,0:T(8,128)(2,1)} %get-tuple-element.30), channel_id=1, source_target_pairs={{4,0},{0,4},{5,1},{1,5},{6,2},{2,6},{7,3},{3,7},{12,8},{8,12},{13,... | collective-permute-start | bytes 4718600 | tf_op jit(solution)/shard_map/ppermute | solution.py:225
  17.7 1.2 %slice_bitcast_fusion.mid = bf16[1024,384]{1,0:T(8,128)(2,1)S(1)} fusion(bf16[1,8192,384]{2,1,0:T(8,128)(2,1)} %param.9), kind=kLoop, calls=%fused_computation | loop fusion | bytes 1572864 | tf_op jit(solution)/shard_map/slice | solution.py:276
  19.0 1.3 %collective-permute-start.9 = (bf16[1024,384]{1,0:T(8,128)(2,1)S(1)}, bf16[1024,384]{1,0:T(8,128)(2,1)S(1)}, u32[]{:S(2)}, u32[]{:S(2)}) collective-permute-start(bf16[1024,384]{1,0:T(8,128)(2,1)S(1)} %slice_bitcast_fusion.mid), channel_id=1, source_target_pairs={{1,0},{2,1},{3,2},{5,4},{6,5},{7,6},{9,8},{10,9},{11,10},{13,12},{... | collective-permute-start | bytes 2359304 | tf_op jit(solution)/shard_map/ppermute | solution.py:269
  20.3 5.5 %collective-permute-start.6 = (bf16[1024,384]{1,0:T(8,128)(2,1)S(1)}, bf16[1024,384]{1,0:T(8,128)(2,1)}, u32[]{:S(2)}, u32[]{:S(2)}) collective-permute-start(bf16[1024,384]{1,0:T(8,128)(2,1)S(1)} %slice_bitcast_fusion.mid), channel_id=1, source_target_pairs={{0,1},{1,2},{2,3},{4,5},{5,6},{6,7},{8,9},{9,10},{10,11},{12,13},{... | collective-permute-start | bytes 2359304 | tf_op jit(solution)/shard_map/ppermute | solution.py:268
  25.7 0.0 copy-done.2
  25.7 0.3 collective-permute-start.3
  26.0 0.0 copy-done.1
  26.0 4.1 %all-to-all-start = ((bf16[4,64,1024]{2,1,0:T(8,128)(2,1)}), bf16[4,64,1024]{2,1,0:T(8,128)(2,1)}, u32[]{:S(2)}, u32[]{:S(2)}) async-start(bf16[4,64,1024]{2,1,0:T(8,128)(2,1)} %copy-done.1), calls=%async_computation | async-start | bytes 1048576 | tf_op jit(solution)/shard_map/all_to_all | solution.py:280
  30.2 12.2 %collective-permute-done.9.refs_3_ = bf16[1024,384]{1,0:T(8,128)(2,1)S(1)} collective-permute-done((bf16[1024,384]{1,0:T(8,128)(2,1)S(1)}, bf16[1024,384]{1,0:T(8,128)(2,1)S(1)}, u32[]{:S(2)}, u32[]{:S(2)}) %collective-permute-start.9) | collective-permute-done | bytes 786464 | tf_op jit(solution)/shard_map/ppermute | solution.py:269
  42.4 1.3 %collective-permute-start.10 = (bf16[1024,384]{1,0:T(8,128)(2,1)S(1)}, bf16[1024,384]{1,0:T(8,128)(2,1)}, u32[]{:S(2)}, u32[]{:S(2)}) collective-permute-start(bf16[1024,384]{1,0:T(8,128)(2,1)S(1)} %collective-permute-done.9.refs_3_), channel_id=1, source_target_pairs={{1,0},{2,1},{5,4},{6,5},{9,8},{10,9},{13,12},{14,13},{17,16},{18,1... | collective-permute-start | bytes 2359304 | tf_op jit(solution)/shard_map/ppermute | solution.py:269
  43.7 0.0 collective-permute-done.6.refs_0_
  43.7 1.6 %collective-permute-start.7 = (bf16[1024,384]{1,0:T(8,128)(2,1)}, bf16[1024,384]{1,0:T(8,128)(2,1)}, u32[]{:S(2)}, u32[]{:S(2)}) collective-permute-start(bf16[1024,384]{1,0:T(8,128)(2,1)} %collective-permute-done.6.refs_0_), channel_id=1, source_target_pairs={{1,2},{2,3},{5,6},{6,7},{9,10},{10,11},{13,14},{14,15},{17,18},{18... | collective-permute-start | bytes 2359304 | tf_op jit(solution)/shard_map/ppermute | solution.py:268
  45.3 2.2 %copy-done = bf16[1,8192,256]{2,1,0:T(8,128)(2,1)S(1)} copy-done((bf16[1,8192,256]{2,1,0:T(8,128)(2,1)S(1)}, bf16[1,8192,256]{2,1,0:T(8,128)(2,1)}, u32[]{:S(2)}) %copy-start) | copy-done | bytes 4194328
  47.4 5.4 %shard_map.83 = (f32[128,384]{1,0:T(8,128)S(1)}, f32[128,384]{1,0:T(8,128)S(1)}) custom-call(bf16[8192,256]{1,0:T(8,128)(2,1)S(1)} %bitcast.22, bf16[8192,384]{1,0:T(8,128)(2,1)} %bitcast.23), custom_call_target="tpu_custom_call" | custom-call | bytes 30000 | tf_op jit(solution)/shard_map/pallas_call | solution.py:102
  52.8 0.0 copy-done.3
  52.8 1.6 %shard_map.84 = (f32[128,384]{1,0:T(8,128)S(1)}, f32[128,384]{1,0:T(8,128)S(1)}) custom-call(bf16[1024,256]{1,0:T(8,128)(2,1)S(1)} %copy-done.3, bf16[8192,384]{1,0:T(8,128)(2,1)} %bitcast.24), custom_call_target="tpu_custom_call" | custom-call | bytes 30000 | tf_op jit(solution)/shard_map/pallas_call | solution.py:102
  54.5 0.0 collective-permute-done.1.refs_1_
  54.5 3.3 %shard_map.85 = (f32[2,64,384]{2,1,0:T(8,128)S(1)}, f32[2,64,384]{2,1,0:T(8,128)S(1)}) custom-call(s32[1]{0:T(128)} %bitcast.me_at, s32[1]{0:T(128)} %bitcast.1.core_at, f32[128,384]{1,0:T(8,128)S(1)} %get-tuple-element.28.mine, bf16[8192,384]{1,0:T(8,128)(2,1)} %bitcast.25, f32[128,384]{1,0:T(8,128)S(1)} %get-tuple-element.29.refs_0_, ...), custom_call_target="tpu_custom_call" | custom-call | bytes 30000 | tf_op jit(solution)/shard_map/pallas_call | solution.py:163
  57.7 0.1 collective-permute-start.2
  57.8 1.4 %collective-permute-done.2 = f32[2,64,384]{2,1,0:T(8,128)S(1)} collective-permute-done((f32[2,64,384]{2,1,0:T(8,128)S(1)}, f32[2,64,384]{2,1,0:T(8,128)S(1)}, u32[]{:S(2)}, u32[]{:S(2)}) %collective-permute-start.2) | collective-permute-done | bytes 196640 | tf_op jit(solution)/shard_map/ppermute | solution.py:290
  59.3 0.7 add.75
  60.0 0.0 all-to-all-done
  60.0 9.3 %all-to-all-start.1 = ((f32[8,16,384]{2,1,0:T(8,128)}), f32[8,16,384]{2,1,0:T(8,128)}, u32[]{:S(2)}, u32[]{:S(2)}) async-start(f32[8,16,384]{2,1,0:T(8,128)} %bitcast.27), calls=%async_computation.1 | async-start | bytes 393216 | tf_op jit(solution)/shard_map/all_to_all | solution.py:293
  69.3 0.0 collective-permute-done.10.refs_4_
  69.3 1.3 %collective-permute-start.11 = (bf16[1024,384]{1,0:T(8,128)(2,1)}, bf16[1024,384]{1,0:T(8,128)(2,1)}, u32[]{:S(2)}, u32[]{:S(2)}) collective-permute-start(bf16[1024,384]{1,0:T(8,128)(2,1)} %collective-permute-done.10.refs_4_), channel_id=1, source_target_pairs={{1,0},{5,4},{9,8},{13,12},{17,16},{21,20},{25,24},{29,28}} | collective-permute-start | bytes 2359304 | tf_op jit(solution)/shard_map/ppermute | solution.py:269
  70.6 0.0 collective-permute-done.7.refs_1_
  70.6 1.6 %collective-permute-start.8 = (bf16[1024,384]{1,0:T(8,128)(2,1)}, bf16[1024,384]{1,0:T(8,128)(2,1)}, u32[]{:S(2)}, u32[]{:S(2)}) collective-permute-start(bf16[1024,384]{1,0:T(8,128)(2,1)} %collective-permute-done.7.refs_1_), channel_id=1, source_target_pairs={{2,3},{6,7},{10,11},{14,15},{18,19},{22,23},{26,27},{30,31}} | collective-permute-start | bytes 2359304 | tf_op jit(solution)/shard_map/ppermute | solution.py:268
  72.2 6.0 %all-to-all-done.1 = f32[8,16,384]{2,1,0:T(8,128)} async-done(((f32[8,16,384]{2,1,0:T(8,128)}), f32[8,16,384]{2,1,0:T(8,128)}, u32[]{:S(2)}, u32[]{:S(2)}) %all-to-all-start.1) | async-done | bytes 196640 | tf_op jit(solution)/shard_map/all_to_all | solution.py:293
  78.2 1.6 %reduce_sum.18 = f32[16,384]{1,0:T(8,128)} reduce(f32[8,16,384]{2,1,0:T(8,128)} %all-to-all-done.1, f32[]{:T(128)} %constant.88.clone.1), dimensions={0}, to_apply=%region_0.1 | reduce | flops 43008 | bytes 221188 | tf_op jit(solution)/shard_map/reduce_sum | solution.py:293
  79.8 0.5 collective-permute-start.5
  80.3 7.0 %collective-permute-done.3.refs_1_ = bf16[128,6144]{1,0:T(8,128)(2,1)S(1)} collective-permute-done((bf16[128,6144]{1,0:T(8,128)(2,1)}, bf16[128,6144]{1,0:T(8,128)(2,1)S(1)}, u32[]{:S(2)}, u32[]{:S(2)}) %collective-permute-start.3) | collective-permute-done | bytes 1572896 | tf_op jit(solution)/shard_map/ppermute | solution.py:225
  87.3 2.9 %shard_map.86 = (f32[2,64,384]{2,1,0:T(8,128)S(1)}, f32[2,64,384]{2,1,0:T(8,128)S(1)}) custom-call(s32[1]{0:T(128)} %bitcast.me_at, s32[1]{0:T(128)} %bitcast.1.core_at, f32[128,384]{1,0:T(8,128)S(1)} %get-tuple-element.35.mine, bf16[8192,384]{1,0:T(8,128)(2,1)} %bitcast.26, f32[128,384]{1,0:T(8,128)S(1)} %get-tuple-element.36.refs_0_, ...), custom_call_target="tpu_custom_call" | custom-call | bytes 30000 | tf_op jit(solution)/shard_map/pallas_call | solution.py:163
  90.2 0.0 copy-start.10
  90.2 0.0 copy-start.4
  90.2 0.0 copy-start.6
  90.2 0.0 copy-start.7
  90.2 0.0 copy-start.8
  90.2 0.0 copy-start.9
  90.2 0.1 collective-permute-start.4
  90.3 0.0 copy-done.5
  90.3 1.4 %collective-permute-done.4 = f32[2,64,384]{2,1,0:T(8,128)S(1)} collective-permute-done((f32[2,64,384]{2,1,0:T(8,128)S(1)}, f32[2,64,384]{2,1,0:T(8,128)S(1)}, u32[]{:S(2)}, u32[]{:S(2)}) %collective-permute-start.4) | collective-permute-done | bytes 196640 | tf_op jit(solution)/shard_map/ppermute | solution.py:290
  91.7 0.7 add.76
  92.4 6.1 %all-to-all-start.2 = ((f32[8,16,384]{2,1,0:T(8,128)}), f32[8,16,384]{2,1,0:T(8,128)S(1)}, u32[]{:S(2)}, u32[]{:S(2)}) async-start(f32[8,16,384]{2,1,0:T(8,128)} %bitcast.6), calls=%async_computation.2 | async-start | bytes 393216 | tf_op jit(solution)/shard_map/all_to_all | solution.py:293
  98.5 0.0 collective-permute-done.5.low
  98.5 0.0 collective-permute-done.11.refs_5_
  98.5 0.0 collective-permute-done.8.refs_2_
  98.5 2.1 %shard_map.87 = f32[64,384]{1,0:T(8,128)S(1)} custom-call(s32[1]{0:T(128)} %bitcast.7.at, bf16[4,64,1024]{2,1,0:T(8,128)(2,1)} %collective-permute-done.5.low, bf16[1024,384]{1,0:T(8,128)(2,1)S(1)} %slice_bitcast_fusion.mid, bf16[1024,384]{1,0:T(8,128)(2,1)} %collective-permute-done.6.refs_0_, bf16[1024,384]{1,0:T(8,128)(2,1)} %collective-permute-done.7.refs_1_, ...), custom_call_target="tpu_custom_call" | custom-call | bytes 30000 | tf_op jit(solution)/shard_map/pallas_call | solution.py:204
  100.7 0.1 collective-permute-start.12
  100.8 2.1 %collective-permute-start.13 = (f32[32,384]{1,0:T(8,128)S(1)}, f32[32,384]{1,0:T(8,128)S(1)}, u32[]{:S(2)}, u32[]{:S(2)}) collective-permute-start(f32[32,384]{1,0:T(8,128)S(1)} %get-tuple-element.47), channel_id=1, source_target_pairs={{0,16},{8,24},{16,0},{24,8},{1,17},{9,25},{17,1},{25,9},{2,18},{10... | collective-permute-start | bytes 147464 | tf_op jit(solution)/shard_map/ppermute | solution.py:315
  102.8 0.2 collective-permute-start.14
  103.0 0.0 copy-done.10
  103.0 4.3 %all-to-all-done.2 = f32[8,16,384]{2,1,0:T(8,128)S(1)} async-done(((f32[8,16,384]{2,1,0:T(8,128)}), f32[8,16,384]{2,1,0:T(8,128)S(1)}, u32[]{:S(2)}, u32[]{:S(2)}) %all-to-all-start.2) | async-done | bytes 196640 | tf_op jit(solution)/shard_map/all_to_all | solution.py:293
  107.3 0.0 collective-permute-done.12
  107.4 0.0 collective-permute-done.13
  107.4 0.0 collective-permute-done.14
  107.4 0.0 copy-done.4
  107.4 0.0 copy-done.6
  107.4 0.0 copy-done.7
  107.4 0.0 copy-done.8
  107.4 0.7 fusion.2
  (12 shorter events, 0.1 us)
Async XLA Ops:
  1.1 14.9 %collective-permute-start = (bf16[1024,256]{1,0:T(8,128)(2,1)S(1)}, bf16[1024,256]{1,0:T(8,128)(2,1)S(1)}, u32[]{:S(2)}, u32[]{:S(2)}) collective-permute-start(bf16[1024,256]{1,0:T(8,128)(2,1)S(1)} %slice_bitcast_fusion.1), channel_id=1, source_target_pairs={{4,0},{0,4},{5,1},{1,5},{6,2},{2,6},{7,3},{3,7},{12,8},{8,12},{13,... | collective-permute-start | bytes 1572872 | tf_op jit(solution)/shard_map/ppermute | solution.py:225
  11.0 15.1 %copy-start.1 = (bf16[4,64,1024]{2,1,0:T(8,128)(2,1)}, bf16[4,64,1024]{2,1,0:T(8,128)(2,1)S(1)}, u32[]{:S(2)}) copy-start(bf16[4,64,1024]{2,1,0:T(8,128)(2,1)S(1)} %get-tuple-element.33) | copy-start | bytes 1572868
  16.0 9.7 %copy-start.2 = (bf16[1024,256]{1,0:T(8,128)(2,1)}, bf16[1024,256]{1,0:T(8,128)(2,1)S(1)}, u32[]{:S(2)}) copy-start(bf16[1024,256]{1,0:T(8,128)(2,1)S(1)} %collective-permute-done.low) | copy-start | bytes 1572868
  16.0 38.4 %collective-permute-start.1 = (bf16[128,6144]{1,0:T(8,128)(2,1)}, bf16[128,6144]{1,0:T(8,128)(2,1)}, u32[]{:S(2)}, u32[]{:S(2)}) collective-permute-start(bf16[128,6144]{1,0:T(8,128)(2,1)} %get-tuple-element.30), channel_id=1, source_target_pairs={{4,0},{0,4},{5,1},{1,5},{6,2},{2,6},{7,3},{3,7},{12,8},{8,12},{13,... | collective-permute-start | bytes 4718600 | tf_op jit(solution)/shard_map/ppermute | solution.py:225
  19.0 23.4 %collective-permute-start.9 = (bf16[1024,384]{1,0:T(8,128)(2,1)S(1)}, bf16[1024,384]{1,0:T(8,128)(2,1)S(1)}, u32[]{:S(2)}, u32[]{:S(2)}) collective-permute-start(bf16[1024,384]{1,0:T(8,128)(2,1)S(1)} %slice_bitcast_fusion.mid), channel_id=1, source_target_pairs={{1,0},{2,1},{3,2},{5,4},{6,5},{7,6},{9,8},{10,9},{11,10},{13,12},{... | collective-permute-start | bytes 2359304 | tf_op jit(solution)/shard_map/ppermute | solution.py:269
  20.3 23.4 %collective-permute-start.6 = (bf16[1024,384]{1,0:T(8,128)(2,1)S(1)}, bf16[1024,384]{1,0:T(8,128)(2,1)}, u32[]{:S(2)}, u32[]{:S(2)}) collective-permute-start(bf16[1024,384]{1,0:T(8,128)(2,1)S(1)} %slice_bitcast_fusion.mid), channel_id=1, source_target_pairs={{0,1},{1,2},{2,3},{4,5},{5,6},{6,7},{8,9},{9,10},{10,11},{12,13},{... | collective-permute-start | bytes 2359304 | tf_op jit(solution)/shard_map/ppermute | solution.py:268
  25.7 61.5 %collective-permute-start.3 = (bf16[128,6144]{1,0:T(8,128)(2,1)}, bf16[128,6144]{1,0:T(8,128)(2,1)S(1)}, u32[]{:S(2)}, u32[]{:S(2)}) collective-permute-start(bf16[128,6144]{1,0:T(8,128)(2,1)} %get-tuple-element.38), channel_id=1, source_target_pairs={{4,0},{0,4},{5,1},{1,5},{6,2},{2,6},{7,3},{3,7},{12,8},{8,12},{13,... | collective-permute-start | bytes 4718600 | tf_op jit(solution)/shard_map/ppermute | solution.py:225
  26.0 33.9 %all-to-all-start = ((bf16[4,64,1024]{2,1,0:T(8,128)(2,1)}), bf16[4,64,1024]{2,1,0:T(8,128)(2,1)}, u32[]{:S(2)}, u32[]{:S(2)}) async-start(bf16[4,64,1024]{2,1,0:T(8,128)(2,1)} %copy-done.1), calls=%async_computation | async-start | bytes 1048576 | tf_op jit(solution)/shard_map/all_to_all | solution.py:280
  42.4 26.9 %collective-permute-start.10 = (bf16[1024,384]{1,0:T(8,128)(2,1)S(1)}, bf16[1024,384]{1,0:T(8,128)(2,1)}, u32[]{:S(2)}, u32[]{:S(2)}) collective-permute-start(bf16[1024,384]{1,0:T(8,128)(2,1)S(1)} %collective-permute-done.9.refs_3_), channel_id=1, source_target_pairs={{1,0},{2,1},{5,4},{6,5},{9,8},{10,9},{13,12},{14,13},{17,16},{18,1... | collective-permute-start | bytes 2359304 | tf_op jit(solution)/shard_map/ppermute | solution.py:269
  43.7 26.9 %collective-permute-start.7 = (bf16[1024,384]{1,0:T(8,128)(2,1)}, bf16[1024,384]{1,0:T(8,128)(2,1)}, u32[]{:S(2)}, u32[]{:S(2)}) collective-permute-start(bf16[1024,384]{1,0:T(8,128)(2,1)} %collective-permute-done.6.refs_0_), channel_id=1, source_target_pairs={{1,2},{2,3},{5,6},{6,7},{9,10},{10,11},{13,14},{14,15},{17,18},{18... | collective-permute-start | bytes 2359304 | tf_op jit(solution)/shard_map/ppermute | solution.py:268
  45.2 2.2 %copy-start = (bf16[1,8192,256]{2,1,0:T(8,128)(2,1)S(1)}, bf16[1,8192,256]{2,1,0:T(8,128)(2,1)}, u32[]{:S(2)}) copy-start(bf16[1,8192,256]{2,1,0:T(8,128)(2,1)} %param.8) | copy-start | bytes 12582916
  47.4 5.4 %copy-start.3 = (bf16[1024,256]{1,0:T(8,128)(2,1)S(1)}, bf16[1024,256]{1,0:T(8,128)(2,1)}, u32[]{:S(2)}) copy-start(bf16[1024,256]{1,0:T(8,128)(2,1)} %copy-done.2) | copy-start | bytes 1572868
  57.7 1.5 %collective-permute-start.2 = (f32[2,64,384]{2,1,0:T(8,128)S(1)}, f32[2,64,384]{2,1,0:T(8,128)S(1)}, u32[]{:S(2)}, u32[]{:S(2)}) collective-permute-start(f32[2,64,384]{2,1,0:T(8,128)S(1)} %get-tuple-element.32), channel_id=1, source_target_pairs={{0,8},{8,0},{16,24},{24,16},{1,9},{9,1},{17,25},{25,17},{2,10},{10... | collective-permute-start | bytes 589832 | tf_op jit(solution)/shard_map/ppermute | solution.py:290
  60.0 18.2 %all-to-all-start.1 = ((f32[8,16,384]{2,1,0:T(8,128)}), f32[8,16,384]{2,1,0:T(8,128)}, u32[]{:S(2)}, u32[]{:S(2)}) async-start(f32[8,16,384]{2,1,0:T(8,128)} %bitcast.27), calls=%async_computation.1 | async-start | bytes 393216 | tf_op jit(solution)/shard_map/all_to_all | solution.py:293
  69.3 29.2 %collective-permute-start.11 = (bf16[1024,384]{1,0:T(8,128)(2,1)}, bf16[1024,384]{1,0:T(8,128)(2,1)}, u32[]{:S(2)}, u32[]{:S(2)}) collective-permute-start(bf16[1024,384]{1,0:T(8,128)(2,1)} %collective-permute-done.10.refs_4_), channel_id=1, source_target_pairs={{1,0},{5,4},{9,8},{13,12},{17,16},{21,20},{25,24},{29,28}} | collective-permute-start | bytes 2359304 | tf_op jit(solution)/shard_map/ppermute | solution.py:269
  70.6 27.9 %collective-permute-start.8 = (bf16[1024,384]{1,0:T(8,128)(2,1)}, bf16[1024,384]{1,0:T(8,128)(2,1)}, u32[]{:S(2)}, u32[]{:S(2)}) collective-permute-start(bf16[1024,384]{1,0:T(8,128)(2,1)} %collective-permute-done.7.refs_1_), channel_id=1, source_target_pairs={{2,3},{6,7},{10,11},{14,15},{18,19},{22,23},{26,27},{30,31}} | collective-permute-start | bytes 2359304 | tf_op jit(solution)/shard_map/ppermute | solution.py:268
  79.8 18.7 %collective-permute-start.5 = (bf16[4,64,1024]{2,1,0:T(8,128)(2,1)}, bf16[4,64,1024]{2,1,0:T(8,128)(2,1)}, u32[]{:S(2)}, u32[]{:S(2)}) collective-permute-start(bf16[4,64,1024]{2,1,0:T(8,128)(2,1)} %all-to-all-done), channel_id=1, source_target_pairs={{4,0},{0,4},{5,1},{1,5},{6,2},{2,6},{7,3},{3,7},{12,8},{8,12},{13,... | collective-permute-start | bytes 1572872 | tf_op jit(solution)/shard_map/ppermute | solution.py:225
  80.3 10.0 %copy-start.5 = (s32[384]{0:T(512)S(1)}, s32[384]{0:T(512)}, u32[]{:S(2)}) copy-start(s32[384]{0:T(512)} %param.15) | copy-start | bytes 4612
  90.2 12.9 %copy-start.10 = (s32[32]{0:T(128)S(1)}, s32[32]{0:T(128)}, u32[]{:S(2)}) copy-start(s32[32]{0:T(128)} %param.12) | copy-start | bytes 388
  90.2 17.2 %copy-start.4 = (f32[16,384]{1,0:T(8,128)S(1)}, f32[16,384]{1,0:T(8,128)}, u32[]{:S(2)}) copy-start(f32[16,384]{1,0:T(8,128)} %reduce_sum.18) | copy-start | bytes 73732
  90.2 17.2 %copy-start.6 = (f32[384]{0:T(512)S(1)}, f32[384]{0:T(512)}, u32[]{:S(2)}) copy-start(f32[384]{0:T(512)} %param.11) | copy-start | bytes 4612
  90.2 17.2 %copy-start.7 = (s32[384]{0:T(512)S(1)}, s32[384]{0:T(512)}, u32[]{:S(2)}) copy-start(s32[384]{0:T(512)} %param.13) | copy-start | bytes 4612
  90.2 17.2 %copy-start.8 = (f32[32]{0:T(128)S(1)}, f32[32]{0:T(128)}, u32[]{:S(2)}) copy-start(f32[32]{0:T(128)} %param.10) | copy-start | bytes 388
  90.2 17.2 %copy-start.9 = (s32[32]{0:T(128)S(1)}, s32[32]{0:T(128)}, u32[]{:S(2)}) copy-start(s32[32]{0:T(128)} %param.14) | copy-start | bytes 388
  90.2 1.5 %collective-permute-start.4 = (f32[2,64,384]{2,1,0:T(8,128)S(1)}, f32[2,64,384]{2,1,0:T(8,128)S(1)}, u32[]{:S(2)}, u32[]{:S(2)}) collective-permute-start(f32[2,64,384]{2,1,0:T(8,128)S(1)} %get-tuple-element.40), channel_id=1, source_target_pairs={{0,8},{8,0},{16,24},{24,16},{1,9},{9,1},{17,25},{25,17},{2,10},{10... | collective-permute-start | bytes 589832 | tf_op jit(solution)/shard_map/ppermute | solution.py:290
  92.4 14.9 %all-to-all-start.2 = ((f32[8,16,384]{2,1,0:T(8,128)}), f32[8,16,384]{2,1,0:T(8,128)S(1)}, u32[]{:S(2)}, u32[]{:S(2)}) async-start(f32[8,16,384]{2,1,0:T(8,128)} %bitcast.6), calls=%async_computation.2 | async-start | bytes 393216 | tf_op jit(solution)/shard_map/all_to_all | solution.py:293
  100.7 6.7 %collective-permute-start.12 = (f32[32,384]{1,0:T(8,128)S(1)}, f32[32,384]{1,0:T(8,128)S(1)}, u32[]{:S(2)}, u32[]{:S(2)}) collective-permute-start(f32[32,384]{1,0:T(8,128)S(1)} %dynamic-slice_bitcast_fusion.2), channel_id=1, source_target_pairs={{0,8},{8,0},{16,24},{24,16},{1,9},{9,1},{17,25},{25,17},{2,10},{10... | collective-permute-start | bytes 147464 | tf_op jit(solution)/shard_map/ppermute | solution.py:315
  100.8 6.6 %collective-permute-start.13 = (f32[32,384]{1,0:T(8,128)S(1)}, f32[32,384]{1,0:T(8,128)S(1)}, u32[]{:S(2)}, u32[]{:S(2)}) collective-permute-start(f32[32,384]{1,0:T(8,128)S(1)} %get-tuple-element.47), channel_id=1, source_target_pairs={{0,16},{8,24},{16,0},{24,8},{1,17},{9,25},{17,1},{25,9},{2,18},{10... | collective-permute-start | bytes 147464 | tf_op jit(solution)/shard_map/ppermute | solution.py:315
  102.8 4.5 %collective-permute-start.14 = (f32[32,384]{1,0:T(8,128)S(1)}, f32[32,384]{1,0:T(8,128)S(1)}, u32[]{:S(2)}, u32[]{:S(2)}) collective-permute-start(f32[32,384]{1,0:T(8,128)S(1)} %get-tuple-element.48), channel_id=1, source_target_pairs={{0,24},{8,16},{16,8},{24,0},{1,25},{9,17},{17,9},{25,1},{2,26},{10... | collective-permute-start | bytes 147464 | tf_op jit(solution)/shard_map/ppermute | solution.py:315

commit v4 on v3

--- a/solution.py
+++ b/solution.py
@@ -272,7 +272,7 @@
         cross(first)
         later_rows = after(lower_rows, first)
         *turned, tail_rows = turn(later_rows, 2, unit, mine, n_dep)
-        cross(after(turned[0], *crossed[0]))
+        cross(turned[0])
         up_tail = after(upper_rows[main_rows + 2 * unit :], *crossed[0])
         pass_on(up_tail, up_tail)
         for i in range(1, n_dep - 1):

time: 109 us -> 106 us (0.972)
  waiting for transfers between devices: 37.4 us -> 29.4 us
  starting transfers between devices: 40 us -> 44.3 us
    ppermute x4, waiting for transfers between devices: 12 us -> 4.44 us  [shifted(): lax.ppermute(x, 'upper', [((u + shift) % n_up, u) for u in range(n_up)])]
    all_to_all x2, starting transfers between devices: 15.4 us -> 18.7 us  [reduced(): lax.all_to_all(by_owner, OWNERS, 0, 0, axis_index_groups=same_core)]
  transfers between devices with their start and end apart: 18 -> 18, of which waited for: 7 -> 6; matrix products, arithmetic and copies ran while one was open for 4% -> 4% of each run, Pallas kernels for 20% -> 21%
where the time goes in v4:
time: 106 us; the launch traced here: 105 us
  starting transfers between devices  44.3 us (42%)
  waiting for transfers between devices  29.4 us (28%)
  Pallas kernels  22.1 us (21%)
  local copies, waits for them, and re-layouts  5.57 us (5%)
  other arithmetic  3.7 us (3%)
    all_to_all x2, starting transfers between devices, reduced(): lax.all_to_all(by_owner, OWNERS, 0, 0, axis_index_groups=same_core)  18.7 us
    ppermute x3, waiting for transfers between devices, pass_on(): backward.append(lax.ppermute(held_down, 'depth', down[:n_dep - 1 - i]))  11.8 us
    all_to_all x2, waiting for transfers between devices, reduced(): lax.all_to_all(by_owner, OWNERS, 0, 0, axis_index_groups=same_core)  10.4 us
    ppermute x3, starting transfers between devices, pass_on(): forward.append(lax.ppermute(held_up, 'depth', up[i:]))  8.76 us
    pallas_call x2, Pallas kernels, rows_product(): pl.pallas_call(body, grid=(steps,), in_specs=[pl.BlockSpec((block, states...  6.98 us
    pallas_call x1, Pallas kernels, turn(): pl.pallas_call(body, grid=(mains + 1,), in_specs=[pl.BlockSpec((block, co...  6.9 us
    ppermute x4, starting transfers between devices, shifted(): lax.ppermute(x, 'upper', [((u + shift) % n_up, u) for u in range(n_up)])  6.45 us
    pallas_call x2, Pallas kernels, turned_products(): pl.pallas_call(body, in_specs=[pl.BlockSpec(memory_space=pltpu.SMEM)] * 2...  6.17 us
  transfers between devices with their start and end apart: 18, of which 6 were waited for; matrix products, arithmetic and copies ran while one was open for 4% of the time, Pallas kernels for 21%

profile of v4, /device:TPU:0, one launch (start us, length us, event | category | flops | bytes accessed | tf_op | source)
XLA Modules:
  0.0 105.5 jit_solution(985425203888606555)
XLA Ops:
  0.0 1.1 %slice_bitcast_fusion.1 = bf16[1024,256]{1,0:T(8,128)(2,1)S(1)} fusion(bf16[1,8192,256]{2,1,0:T(8,128)(2,1)} %param.8), kind=kLoop, calls=%fused_computation.1 | loop fusion | bytes 1048576 | tf_op jit(solution)/shard_map/slice | solution.py:271
  1.1 3.0 %collective-permute-start = (bf16[1024,256]{1,0:T(8,128)(2,1)S(1)}, bf16[1024,256]{1,0:T(8,128)(2,1)S(1)}, u32[]{:S(2)}, u32[]{:S(2)}) collective-permute-start(bf16[1024,256]{1,0:T(8,128)(2,1)S(1)} %slice_bitcast_fusion.1), channel_id=1, source_target_pairs={{4,0},{0,4},{5,1},{1,5},{6,2},{2,6},{7,3},{3,7},{12,8},{8,12},{13,... | collective-permute-start | bytes 1572872 | tf_op jit(solution)/shard_map/ppermute | solution.py:225
  4.1 6.9 %shard_map.82 = (bf16[128,6144]{1,0:T(8,128)(2,1)}, bf16[128,6144]{1,0:T(8,128)(2,1)}, bf16[4,64,1024]{2,1,0:T(8,128)(2,1)S(1)}) custom-call(bf16[8192,256]{1,0:T(8,128)(2,1)} %bitcast.21), custom_call_target="tpu_custom_call" | custom-call | bytes 30000 | tf_op jit(solution)/shard_map/pallas_call | solution.py:59
  11.0 0.0 collective-permute-start.1
  11.0 1.4 %slice_bitcast_fusion.mid = bf16[1024,384]{1,0:T(8,128)(2,1)S(1)} fusion(bf16[1,8192,384]{2,1,0:T(8,128)(2,1)} %param.9), kind=kLoop, calls=%fused_computation | loop fusion | bytes 1572864 | tf_op jit(solution)/shard_map/slice | solution.py:276
  12.4 4.4 %collective-permute-done.low = bf16[1024,256]{1,0:T(8,128)(2,1)S(1)} collective-permute-done((bf16[1024,256]{1,0:T(8,128)(2,1)S(1)}, bf16[1024,256]{1,0:T(8,128)(2,1)S(1)}, u32[]{:S(2)}, u32[]{:S(2)}) %collective-permute-start) | collective-permute-done | bytes 524320 | tf_op jit(solution)/shard_map/ppermute | solution.py:225
  16.8 0.8 copy-done.2
  17.7 1.3 %collective-permute-start.9 = (bf16[1024,384]{1,0:T(8,128)(2,1)S(1)}, bf16[1024,384]{1,0:T(8,128)(2,1)S(1)}, u32[]{:S(2)}, u32[]{:S(2)}) collective-permute-start(bf16[1024,384]{1,0:T(8,128)(2,1)S(1)} %slice_bitcast_fusion.mid), channel_id=1, source_target_pairs={{1,0},{2,1},{3,2},{5,4},{6,5},{7,6},{9,8},{10,9},{11,10},{13,12},{... | collective-permute-start | bytes 2359304 | tf_op jit(solution)/shard_map/ppermute | solution.py:269
  19.0 5.6 %collective-permute-start.6 = (bf16[1024,384]{1,0:T(8,128)(2,1)S(1)}, bf16[1024,384]{1,0:T(8,128)(2,1)}, u32[]{:S(2)}, u32[]{:S(2)}) collective-permute-start(bf16[1024,384]{1,0:T(8,128)(2,1)S(1)} %slice_bitcast_fusion.mid), channel_id=1, source_target_pairs={{0,1},{1,2},{2,3},{4,5},{5,6},{6,7},{8,9},{9,10},{10,11},{12,13},{... | collective-permute-start | bytes 2359304 | tf_op jit(solution)/shard_map/ppermute | solution.py:268
  24.6 1.9 %collective-permute-start.3 = (bf16[128,6144]{1,0:T(8,128)(2,1)}, bf16[128,6144]{1,0:T(8,128)(2,1)S(1)}, u32[]{:S(2)}, u32[]{:S(2)}) collective-permute-start(bf16[128,6144]{1,0:T(8,128)(2,1)} %get-tuple-element.36), channel_id=1, source_target_pairs={{4,0},{0,4},{5,1},{1,5},{6,2},{2,6},{7,3},{3,7},{12,8},{8,12},{13,... | collective-permute-start | bytes 4718600 | tf_op jit(solution)/shard_map/ppermute | solution.py:225
  26.5 0.0 copy-done.1
  26.5 4.1 %all-to-all-start = ((bf16[4,64,1024]{2,1,0:T(8,128)(2,1)}), bf16[4,64,1024]{2,1,0:T(8,128)(2,1)}, u32[]{:S(2)}, u32[]{:S(2)}) async-start(bf16[4,64,1024]{2,1,0:T(8,128)(2,1)} %copy-done.1), calls=%async_computation | async-start | bytes 1048576 | tf_op jit(solution)/shard_map/all_to_all | solution.py:280
  30.7 11.7 %collective-permute-done.9.refs_3_ = bf16[1024,384]{1,0:T(8,128)(2,1)S(1)} collective-permute-done((bf16[1024,384]{1,0:T(8,128)(2,1)S(1)}, bf16[1024,384]{1,0:T(8,128)(2,1)S(1)}, u32[]{:S(2)}, u32[]{:S(2)}) %collective-permute-start.9) | collective-permute-done | bytes 786464 | tf_op jit(solution)/shard_map/ppermute | solution.py:269
  42.4 1.3 %collective-permute-start.10 = (bf16[1024,384]{1,0:T(8,128)(2,1)S(1)}, bf16[1024,384]{1,0:T(8,128)(2,1)}, u32[]{:S(2)}, u32[]{:S(2)}) collective-permute-start(bf16[1024,384]{1,0:T(8,128)(2,1)S(1)} %collective-permute-done.9.refs_3_), channel_id=1, source_target_pairs={{1,0},{2,1},{5,4},{6,5},{9,8},{10,9},{13,12},{14,13},{17,16},{18,1... | collective-permute-start | bytes 2359304 | tf_op jit(solution)/shard_map/ppermute | solution.py:269
  43.7 0.0 collective-permute-done.6.refs_0_
  43.7 1.6 %collective-permute-start.7 = (bf16[1024,384]{1,0:T(8,128)(2,1)}, bf16[1024,384]{1,0:T(8,128)(2,1)}, u32[]{:S(2)}, u32[]{:S(2)}) collective-permute-start(bf16[1024,384]{1,0:T(8,128)(2,1)} %collective-permute-done.6.refs_0_), channel_id=1, source_target_pairs={{1,2},{2,3},{5,6},{6,7},{9,10},{10,11},{13,14},{14,15},{17,18},{18... | collective-permute-start | bytes 2359304 | tf_op jit(solution)/shard_map/ppermute | solution.py:268
  45.3 2.2 %copy-done = bf16[1,8192,256]{2,1,0:T(8,128)(2,1)S(1)} copy-done((bf16[1,8192,256]{2,1,0:T(8,128)(2,1)S(1)}, bf16[1,8192,256]{2,1,0:T(8,128)(2,1)}, u32[]{:S(2)}) %copy-start) | copy-done | bytes 4194328
  47.5 5.4 %shard_map.83 = (f32[128,384]{1,0:T(8,128)S(1)}, f32[128,384]{1,0:T(8,128)S(1)}) custom-call(bf16[8192,256]{1,0:T(8,128)(2,1)S(1)} %bitcast.22, bf16[8192,384]{1,0:T(8,128)(2,1)} %bitcast.23), custom_call_target="tpu_custom_call" | custom-call | bytes 30000 | tf_op jit(solution)/shard_map/pallas_call | solution.py:102
  52.9 0.0 copy-done.3
  52.9 1.6 %shard_map.84 = (f32[128,384]{1,0:T(8,128)S(1)}, f32[128,384]{1,0:T(8,128)S(1)}) custom-call(bf16[1024,256]{1,0:T(8,128)(2,1)S(1)} %copy-done.3, bf16[8192,384]{1,0:T(8,128)(2,1)} %bitcast.24), custom_call_target="tpu_custom_call" | custom-call | bytes 30000 | tf_op jit(solution)/shard_map/pallas_call | solution.py:102
  54.5 0.0 collective-permute-done.1.refs_1_
  54.5 3.3 %shard_map.85 = (f32[2,64,384]{2,1,0:T(8,128)S(1)}, f32[2,64,384]{2,1,0:T(8,128)S(1)}) custom-call(s32[1]{0:T(128)} %bitcast.me_at, s32[1]{0:T(128)} %bitcast.1.core_at, f32[128,384]{1,0:T(8,128)S(1)} %get-tuple-element.27.mine, bf16[8192,384]{1,0:T(8,128)(2,1)} %bitcast.25, f32[128,384]{1,0:T(8,128)S(1)} %get-tuple-element.28.refs_0_, ...), custom_call_target="tpu_custom_call" | custom-call | bytes 30000 | tf_op jit(solution)/shard_map/pallas_call | solution.py:163
  57.8 0.1 collective-permute-start.2
  57.9 1.4 %collective-permute-done.2 = f32[2,64,384]{2,1,0:T(8,128)S(1)} collective-permute-done((f32[2,64,384]{2,1,0:T(8,128)S(1)}, f32[2,64,384]{2,1,0:T(8,128)S(1)}, u32[]{:S(2)}, u32[]{:S(2)}) %collective-permute-start.2) | collective-permute-done | bytes 196640 | tf_op jit(solution)/shard_map/ppermute | solution.py:290
  59.3 0.7 add.75
  60.0 0.0 all-to-all-done
  60.0 11.6 %all-to-all-start.1 = ((f32[8,16,384]{2,1,0:T(8,128)}), f32[8,16,384]{2,1,0:T(8,128)}, u32[]{:S(2)}, u32[]{:S(2)}) async-start(f32[8,16,384]{2,1,0:T(8,128)} %bitcast.27), calls=%async_computation.1 | async-start | bytes 393216 | tf_op jit(solution)/shard_map/all_to_all | solution.py:293
  71.6 0.0 collective-permute-done.10.refs_4_
  71.6 1.3 %collective-permute-start.11 = (bf16[1024,384]{1,0:T(8,128)(2,1)}, bf16[1024,384]{1,0:T(8,128)(2,1)}, u32[]{:S(2)}, u32[]{:S(2)}) collective-permute-start(bf16[1024,384]{1,0:T(8,128)(2,1)} %collective-permute-done.10.refs_4_), channel_id=1, source_target_pairs={{1,0},{5,4},{9,8},{13,12},{17,16},{21,20},{25,24},{29,28}} | collective-permute-start | bytes 2359304 | tf_op jit(solution)/shard_map/ppermute | solution.py:269
  72.9 0.0 collective-permute-done.7.refs_1_
  72.9 1.6 %collective-permute-start.8 = (bf16[1024,384]{1,0:T(8,128)(2,1)}, bf16[1024,384]{1,0:T(8,128)(2,1)}, u32[]{:S(2)}, u32[]{:S(2)}) collective-permute-start(bf16[1024,384]{1,0:T(8,128)(2,1)} %collective-permute-done.7.refs_1_), channel_id=1, source_target_pairs={{2,3},{6,7},{10,11},{14,15},{18,19},{22,23},{26,27},{30,31}} | collective-permute-start | bytes 2359304 | tf_op jit(solution)/shard_map/ppermute | solution.py:268
  74.5 6.0 %all-to-all-done.1 = f32[8,16,384]{2,1,0:T(8,128)} async-done(((f32[8,16,384]{2,1,0:T(8,128)}), f32[8,16,384]{2,1,0:T(8,128)}, u32[]{:S(2)}, u32[]{:S(2)}) %all-to-all-start.1) | async-done | bytes 196640 | tf_op jit(solution)/shard_map/all_to_all | solution.py:293
  80.5 1.6 %reduce_sum.18 = f32[16,384]{1,0:T(8,128)} reduce(f32[8,16,384]{2,1,0:T(8,128)} %all-to-all-done.1, f32[]{:T(128)} %constant.88.clone.1), dimensions={0}, to_apply=%region_0.1 | reduce | flops 43008 | bytes 221188 | tf_op jit(solution)/shard_map/reduce_sum | solution.py:293
  82.1 1.5 %collective-permute-start.5 = (bf16[4,64,1024]{2,1,0:T(8,128)(2,1)}, bf16[4,64,1024]{2,1,0:T(8,128)(2,1)}, u32[]{:S(2)}, u32[]{:S(2)}) collective-permute-start(bf16[4,64,1024]{2,1,0:T(8,128)(2,1)} %all-to-all-done), channel_id=1, source_target_pairs={{4,0},{0,4},{5,1},{1,5},{6,2},{2,6},{7,3},{3,7},{12,8},{8,12},{13,... | collective-permute-start | bytes 1572872 | tf_op jit(solution)/shard_map/ppermute | solution.py:225
  83.6 0.0 collective-permute-done.3.refs_1_
  83.6 2.9 %shard_map.86 = (f32[2,64,384]{2,1,0:T(8,128)S(1)}, f32[2,64,384]{2,1,0:T(8,128)S(1)}) custom-call(s32[1]{0:T(128)} %bitcast.me_at, s32[1]{0:T(128)} %bitcast.1.core_at, f32[128,384]{1,0:T(8,128)S(1)} %get-tuple-element.33.mine, bf16[8192,384]{1,0:T(8,128)(2,1)} %bitcast.26, f32[128,384]{1,0:T(8,128)S(1)} %get-tuple-element.34.refs_0_, ...), custom_call_target="tpu_custom_call" | custom-call | bytes 30000 | tf_op jit(solution)/shard_map/pallas_call | solution.py:163
  86.5 0.0 copy-start.10
  86.5 0.0 copy-start.4
  86.5 0.0 copy-start.6
  86.5 0.0 copy-start.7
  86.5 0.0 copy-start.8
  86.5 0.0 copy-start.9
  86.6 0.1 collective-permute-start.4
  86.6 0.0 copy-done.5
  86.7 1.4 %collective-permute-done.4 = f32[2,64,384]{2,1,0:T(8,128)S(1)} collective-permute-done((f32[2,64,384]{2,1,0:T(8,128)S(1)}, f32[2,64,384]{2,1,0:T(8,128)S(1)}, u32[]{:S(2)}, u32[]{:S(2)}) %collective-permute-start.4) | collective-permute-done | bytes 196640 | tf_op jit(solution)/shard_map/ppermute | solution.py:290
  88.1 0.7 add.76
  88.7 7.1 %all-to-all-start.2 = ((f32[8,16,384]{2,1,0:T(8,128)}), f32[8,16,384]{2,1,0:T(8,128)S(1)}, u32[]{:S(2)}, u32[]{:S(2)}) async-start(f32[8,16,384]{2,1,0:T(8,128)} %bitcast.6), calls=%async_computation.2 | async-start | bytes 393216 | tf_op jit(solution)/shard_map/all_to_all | solution.py:293
  95.8 0.0 collective-permute-done.5.low
  95.8 0.0 collective-permute-done.11.refs_5_
  95.8 0.0 collective-permute-done.8.refs_2_
  95.8 2.1 %shard_map.87 = f32[64,384]{1,0:T(8,128)S(1)} custom-call(s32[1]{0:T(128)} %bitcast.7.at, bf16[4,64,1024]{2,1,0:T(8,128)(2,1)} %collective-permute-done.5.low, bf16[1024,384]{1,0:T(8,128)(2,1)S(1)} %slice_bitcast_fusion.mid, bf16[1024,384]{1,0:T(8,128)(2,1)} %collective-permute-done.6.refs_0_, bf16[1024,384]{1,0:T(8,128)(2,1)} %collective-permute-done.7.refs_1_, ...), custom_call_target="tpu_custom_call" | custom-call | bytes 30000 | tf_op jit(solution)/shard_map/pallas_call | solution.py:204
  98.0 0.1 collective-permute-start.12
  98.1 2.1 %collective-permute-start.13 = (f32[32,384]{1,0:T(8,128)S(1)}, f32[32,384]{1,0:T(8,128)S(1)}, u32[]{:S(2)}, u32[]{:S(2)}) collective-permute-start(f32[32,384]{1,0:T(8,128)S(1)} %get-tuple-element.45), channel_id=1, source_target_pairs={{0,16},{8,24},{16,0},{24,8},{1,17},{9,25},{17,1},{25,9},{2,18},{10... | collective-permute-start | bytes 147464 | tf_op jit(solution)/shard_map/ppermute | solution.py:315
  100.1 0.2 collective-permute-start.14
  100.3 0.0 copy-done.10
  100.3 4.3 %all-to-all-done.2 = f32[8,16,384]{2,1,0:T(8,128)S(1)} async-done(((f32[8,16,384]{2,1,0:T(8,128)}), f32[8,16,384]{2,1,0:T(8,128)S(1)}, u32[]{:S(2)}, u32[]{:S(2)}) %all-to-all-start.2) | async-done | bytes 196640 | tf_op jit(solution)/shard_map/all_to_all | solution.py:293
  104.7 0.0 collective-permute-done.12
  104.7 0.0 collective-permute-done.13
  104.7 0.0 collective-permute-done.14
  104.7 0.0 copy-done.4
  104.7 0.0 copy-done.6
  104.7 0.0 copy-done.7
  104.7 0.0 copy-done.8
  104.7 0.7 fusion.2
  (12 shorter events, 0.1 us)
Async XLA Ops:
  1.1 15.8 %collective-permute-start = (bf16[1024,256]{1,0:T(8,128)(2,1)S(1)}, bf16[1024,256]{1,0:T(8,128)(2,1)S(1)}, u32[]{:S(2)}, u32[]{:S(2)}) collective-permute-start(bf16[1024,256]{1,0:T(8,128)(2,1)S(1)} %slice_bitcast_fusion.1), channel_id=1, source_target_pairs={{4,0},{0,4},{5,1},{1,5},{6,2},{2,6},{7,3},{3,7},{12,8},{8,12},{13,... | collective-permute-start | bytes 1572872 | tf_op jit(solution)/shard_map/ppermute | solution.py:225
  11.0 15.5 %copy-start.1 = (bf16[4,64,1024]{2,1,0:T(8,128)(2,1)}, bf16[4,64,1024]{2,1,0:T(8,128)(2,1)S(1)}, u32[]{:S(2)}) copy-start(bf16[4,64,1024]{2,1,0:T(8,128)(2,1)S(1)} %get-tuple-element.31) | copy-start | bytes 1572868
  11.0 43.5 %collective-permute-start.1 = (bf16[128,6144]{1,0:T(8,128)(2,1)}, bf16[128,6144]{1,0:T(8,128)(2,1)}, u32[]{:S(2)}, u32[]{:S(2)}) collective-permute-start(bf16[128,6144]{1,0:T(8,128)(2,1)} %get-tuple-element.25), channel_id=1, source_target_pairs={{4,0},{0,4},{5,1},{1,5},{6,2},{2,6},{7,3},{3,7},{12,8},{8,12},{13,... | collective-permute-start | bytes 4718600 | tf_op jit(solution)/shard_map/ppermute | solution.py:225
  16.8 0.8 copy-start.2
  17.7 24.7 %collective-permute-start.9 = (bf16[1024,384]{1,0:T(8,128)(2,1)S(1)}, bf16[1024,384]{1,0:T(8,128)(2,1)S(1)}, u32[]{:S(2)}, u32[]{:S(2)}) collective-permute-start(bf16[1024,384]{1,0:T(8,128)(2,1)S(1)} %slice_bitcast_fusion.mid), channel_id=1, source_target_pairs={{1,0},{2,1},{3,2},{5,4},{6,5},{7,6},{9,8},{10,9},{11,10},{13,12},{... | collective-permute-start | bytes 2359304 | tf_op jit(solution)/shard_map/ppermute | solution.py:269
  19.0 24.7 %collective-permute-start.6 = (bf16[1024,384]{1,0:T(8,128)(2,1)S(1)}, bf16[1024,384]{1,0:T(8,128)(2,1)}, u32[]{:S(2)}, u32[]{:S(2)}) collective-permute-start(bf16[1024,384]{1,0:T(8,128)(2,1)S(1)} %slice_bitcast_fusion.mid), channel_id=1, source_target_pairs={{0,1},{1,2},{2,3},{4,5},{5,6},{6,7},{8,9},{9,10},{10,11},{12,13},{... | collective-permute-start | bytes 2359304 | tf_op jit(solution)/shard_map/ppermute | solution.py:268
  24.6 59.0 %collective-permute-start.3 = (bf16[128,6144]{1,0:T(8,128)(2,1)}, bf16[128,6144]{1,0:T(8,128)(2,1)S(1)}, u32[]{:S(2)}, u32[]{:S(2)}) collective-permute-start(bf16[128,6144]{1,0:T(8,128)(2,1)} %get-tuple-element.36), channel_id=1, source_target_pairs={{4,0},{0,4},{5,1},{1,5},{6,2},{2,6},{7,3},{3,7},{12,8},{8,12},{13,... | collective-permute-start | bytes 4718600 | tf_op jit(solution)/shard_map/ppermute | solution.py:225
  26.5 33.5 %all-to-all-start = ((bf16[4,64,1024]{2,1,0:T(8,128)(2,1)}), bf16[4,64,1024]{2,1,0:T(8,128)(2,1)}, u32[]{:S(2)}, u32[]{:S(2)}) async-start(bf16[4,64,1024]{2,1,0:T(8,128)(2,1)} %copy-done.1), calls=%async_computation | async-start | bytes 1048576 | tf_op jit(solution)/shard_map/all_to_all | solution.py:280
  42.4 29.2 %collective-permute-start.10 = (bf16[1024,384]{1,0:T(8,128)(2,1)S(1)}, bf16[1024,384]{1,0:T(8,128)(2,1)}, u32[]{:S(2)}, u32[]{:S(2)}) collective-permute-start(bf16[1024,384]{1,0:T(8,128)(2,1)S(1)} %collective-permute-done.9.refs_3_), channel_id=1, source_target_pairs={{1,0},{2,1},{5,4},{6,5},{9,8},{10,9},{13,12},{14,13},{17,16},{18,1... | collective-permute-start | bytes 2359304 | tf_op jit(solution)/shard_map/ppermute | solution.py:269
  43.7 29.2 %collective-permute-start.7 = (bf16[1024,384]{1,0:T(8,128)(2,1)}, bf16[1024,384]{1,0:T(8,128)(2,1)}, u32[]{:S(2)}, u32[]{:S(2)}) collective-permute-start(bf16[1024,384]{1,0:T(8,128)(2,1)} %collective-permute-done.6.refs_0_), channel_id=1, source_target_pairs={{1,2},{2,3},{5,6},{6,7},{9,10},{10,11},{13,14},{14,15},{17,18},{18... | collective-permute-start | bytes 2359304 | tf_op jit(solution)/shard_map/ppermute | solution.py:268
  45.3 2.2 %copy-start = (bf16[1,8192,256]{2,1,0:T(8,128)(2,1)S(1)}, bf16[1,8192,256]{2,1,0:T(8,128)(2,1)}, u32[]{:S(2)}) copy-start(bf16[1,8192,256]{2,1,0:T(8,128)(2,1)} %param.8) | copy-start | bytes 12582916
  47.5 5.4 %copy-start.3 = (bf16[1024,256]{1,0:T(8,128)(2,1)S(1)}, bf16[1024,256]{1,0:T(8,128)(2,1)}, u32[]{:S(2)}) copy-start(bf16[1024,256]{1,0:T(8,128)(2,1)} %copy-done.2) | copy-start | bytes 1572868
  57.8 1.5 %collective-permute-start.2 = (f32[2,64,384]{2,1,0:T(8,128)S(1)}, f32[2,64,384]{2,1,0:T(8,128)S(1)}, u32[]{:S(2)}, u32[]{:S(2)}) collective-permute-start(f32[2,64,384]{2,1,0:T(8,128)S(1)} %get-tuple-element.30), channel_id=1, source_target_pairs={{0,8},{8,0},{16,24},{24,16},{1,9},{9,1},{17,25},{25,17},{2,10},{10... | collective-permute-start | bytes 589832 | tf_op jit(solution)/shard_map/ppermute | solution.py:290
  60.0 20.6 %all-to-all-start.1 = ((f32[8,16,384]{2,1,0:T(8,128)}), f32[8,16,384]{2,1,0:T(8,128)}, u32[]{:S(2)}, u32[]{:S(2)}) async-start(f32[8,16,384]{2,1,0:T(8,128)} %bitcast.27), calls=%async_computation.1 | async-start | bytes 393216 | tf_op jit(solution)/shard_map/all_to_all | solution.py:293
  71.6 24.2 %collective-permute-start.11 = (bf16[1024,384]{1,0:T(8,128)(2,1)}, bf16[1024,384]{1,0:T(8,128)(2,1)}, u32[]{:S(2)}, u32[]{:S(2)}) collective-permute-start(bf16[1024,384]{1,0:T(8,128)(2,1)} %collective-permute-done.10.refs_4_), channel_id=1, source_target_pairs={{1,0},{5,4},{9,8},{13,12},{17,16},{21,20},{25,24},{29,28}} | collective-permute-start | bytes 2359304 | tf_op jit(solution)/shard_map/ppermute | solution.py:269
  72.9 22.9 %collective-permute-start.8 = (bf16[1024,384]{1,0:T(8,128)(2,1)}, bf16[1024,384]{1,0:T(8,128)(2,1)}, u32[]{:S(2)}, u32[]{:S(2)}) collective-permute-start(bf16[1024,384]{1,0:T(8,128)(2,1)} %collective-permute-done.7.refs_1_), channel_id=1, source_target_pairs={{2,3},{6,7},{10,11},{14,15},{18,19},{22,23},{26,27},{30,31}} | collective-permute-start | bytes 2359304 | tf_op jit(solution)/shard_map/ppermute | solution.py:268
  82.1 13.7 %collective-permute-start.5 = (bf16[4,64,1024]{2,1,0:T(8,128)(2,1)}, bf16[4,64,1024]{2,1,0:T(8,128)(2,1)}, u32[]{:S(2)}, u32[]{:S(2)}) collective-permute-start(bf16[4,64,1024]{2,1,0:T(8,128)(2,1)} %all-to-all-done), channel_id=1, source_target_pairs={{4,0},{0,4},{5,1},{1,5},{6,2},{2,6},{7,3},{3,7},{12,8},{8,12},{13,... | collective-permute-start | bytes 1572872 | tf_op jit(solution)/shard_map/ppermute | solution.py:225
  83.6 3.1 %copy-start.5 = (s32[384]{0:T(512)S(1)}, s32[384]{0:T(512)}, u32[]{:S(2)}) copy-start(s32[384]{0:T(512)} %param.15) | copy-start | bytes 4612
  86.5 13.8 %copy-start.10 = (s32[32]{0:T(128)S(1)}, s32[32]{0:T(128)}, u32[]{:S(2)}) copy-start(s32[32]{0:T(128)} %param.12) | copy-start | bytes 388
  86.5 18.2 %copy-start.4 = (f32[16,384]{1,0:T(8,128)S(1)}, f32[16,384]{1,0:T(8,128)}, u32[]{:S(2)}) copy-start(f32[16,384]{1,0:T(8,128)} %reduce_sum.18) | copy-start | bytes 73732
  86.5 18.2 %copy-start.6 = (f32[384]{0:T(512)S(1)}, f32[384]{0:T(512)}, u32[]{:S(2)}) copy-start(f32[384]{0:T(512)} %param.11) | copy-start | bytes 4612
  86.5 18.2 %copy-start.7 = (s32[384]{0:T(512)S(1)}, s32[384]{0:T(512)}, u32[]{:S(2)}) copy-start(s32[384]{0:T(512)} %param.13) | copy-start | bytes 4612
  86.5 18.2 %copy-start.8 = (f32[32]{0:T(128)S(1)}, f32[32]{0:T(128)}, u32[]{:S(2)}) copy-start(f32[32]{0:T(128)} %param.10) | copy-start | bytes 388
  86.5 18.2 %copy-start.9 = (s32[32]{0:T(128)S(1)}, s32[32]{0:T(128)}, u32[]{:S(2)}) copy-start(s32[32]{0:T(128)} %param.14) | copy-start | bytes 388
  86.6 1.5 %collective-permute-start.4 = (f32[2,64,384]{2,1,0:T(8,128)S(1)}, f32[2,64,384]{2,1,0:T(8,128)S(1)}, u32[]{:S(2)}, u32[]{:S(2)}) collective-permute-start(f32[2,64,384]{2,1,0:T(8,128)S(1)} %get-tuple-element.38), channel_id=1, source_target_pairs={{0,8},{8,0},{16,24},{24,16},{1,9},{9,1},{17,25},{25,17},{2,10},{10... | collective-permute-start | bytes 589832 | tf_op jit(solution)/shard_map/ppermute | solution.py:290
  88.7 15.9 %all-to-all-start.2 = ((f32[8,16,384]{2,1,0:T(8,128)}), f32[8,16,384]{2,1,0:T(8,128)S(1)}, u32[]{:S(2)}, u32[]{:S(2)}) async-start(f32[8,16,384]{2,1,0:T(8,128)} %bitcast.6), calls=%async_computation.2 | async-start | bytes 393216 | tf_op jit(solution)/shard_map/all_to_all | solution.py:293
  98.0 6.7 %collective-permute-start.12 = (f32[32,384]{1,0:T(8,128)S(1)}, f32[32,384]{1,0:T(8,128)S(1)}, u32[]{:S(2)}, u32[]{:S(2)}) collective-permute-start(f32[32,384]{1,0:T(8,128)S(1)} %dynamic-slice_bitcast_fusion.2), channel_id=1, source_target_pairs={{0,8},{8,0},{16,24},{24,16},{1,9},{9,1},{17,25},{25,17},{2,10},{10... | collective-permute-start | bytes 147464 | tf_op jit(solution)/shard_map/ppermute | solution.py:315
  98.1 6.6 %collective-permute-start.13 = (f32[32,384]{1,0:T(8,128)S(1)}, f32[32,384]{1,0:T(8,128)S(1)}, u32[]{:S(2)}, u32[]{:S(2)}) collective-permute-start(f32[32,384]{1,0:T(8,128)S(1)} %get-tuple-element.45), channel_id=1, source_target_pairs={{0,16},{8,24},{16,0},{24,8},{1,17},{9,25},{17,1},{25,9},{2,18},{10... | collective-permute-start | bytes 147464 | tf_op jit(solution)/shard_map/ppermute | solution.py:315
  100.1 4.5 %collective-permute-start.14 = (f32[32,384]{1,0:T(8,128)S(1)}, f32[32,384]{1,0:T(8,128)S(1)}, u32[]{:S(2)}, u32[]{:S(2)}) collective-permute-start(f32[32,384]{1,0:T(8,128)S(1)} %get-tuple-element.46), channel_id=1, source_target_pairs={{0,24},{8,16},{16,8},{24,0},{1,25},{9,17},{17,9},{25,1},{2,26},{10... | collective-permute-start | bytes 147464 | tf_op jit(solution)/shard_map/ppermute | solution.py:315

commit v5 on v4

--- a/solution.py
+++ b/solution.py
@@ -27,6 +27,10 @@
 
 def in_hbm(x):
     return pltpu.with_memory_space_constraint(x, pltpu.HBM)
+
+
+def in_vmem(x):
+    return pltpu.with_memory_space_constraint(x, pltpu.VMEM)
 
 
 def whole(shape):
@@ -115,10 +119,29 @@
     )(got, in_hbm(upper_rows), *so_far)
 
 
-def turned_products(me, core, own, so_far, got, upper_rows, n_core):
+def held_rows(upper_rows, k):
+    width = upper_rows.shape[1]
+
+    def body(up, out, sem):
+        copy = pltpu.make_async_copy(up.at[pl.ds(0, k)], out, sem)
+        copy.start()
+        copy.wait()
+
+    return pl.pallas_call(
+        body,
+        in_specs=[pl.BlockSpec(memory_space=pltpu.HBM)],
+        out_specs=pl.BlockSpec(memory_space=pltpu.VMEM),
+        out_shape=pltpu.VMEM((k, width), upper_rows.dtype),
+        scratch_shapes=[pltpu.SemaphoreType.DMA],
+        compiler_params=params(),
+        cost_estimate=cost(0.01),
+    )(in_hbm(upper_rows))
+
+
+def turned_products(me, core, own, so_far, got, rows, n_core):
     n_up = 1 + len(got)
     states, k = got[0].shape
-    width = upper_rows.shape[1]
+    width = rows.shape[1]
     steps = 3
     block = k // steps
     share = states // n_core
@@ -126,7 +149,7 @@
     def body(me_at, core_at, mine, up, *refs):
         befores, lows_at = refs[: n_up - 1], refs[n_up - 1 : 2 * n_up - 2]
         outs = refs[2 * n_up - 2 : 2 * n_up - 2 + n_core]
-        lows, ups, sems = refs[2 * n_up - 2 + n_core :]
+        lows, sems = refs[2 * n_up - 2 + n_core :]
 
         def start(source, target, sem):
             copy = pltpu.make_async_copy(source, target, sem)
@@ -137,8 +160,7 @@
         for j in range(steps):
             span = pl.ds(j * block, block)
             copies.append(
-                [start(up.at[span], ups.at[j], sems.at[0, j])]
-                + [start(low.at[:, span], lows.at[i, j], sems.at[i + 1, j]) for i, low in enumerate(lows_at)]
+                [start(low.at[:, span], lows.at[i, j], sems.at[i, j]) for i, low in enumerate(lows_at)]
             )
 
         def put(slot, product):
@@ -155,24 +177,23 @@
         for j, group in enumerate(copies):
             for copy in group:
                 copy.wait()
-            totals = [total + dot(lows[i, j], ups[j]) for i, total in enumerate(totals)]
+            totals = [total + dot(lows[i, j], up[j * block : (j + 1) * block]) for i, total in enumerate(totals)]
         for i, total in enumerate(totals):
             put(lax.rem(me_at[0] + 1 + i, n_up), total)
 
     vmem, hbm = pl.BlockSpec(memory_space=pltpu.VMEM), pl.BlockSpec(memory_space=pltpu.HBM)
     return pl.pallas_call(
         body,
-        in_specs=[pl.BlockSpec(memory_space=pltpu.SMEM)] * 2 + [vmem, hbm] + [vmem] * (n_up - 1) + [hbm] * (n_up - 1),
+        in_specs=[pl.BlockSpec(memory_space=pltpu.SMEM)] * 2 + [vmem] * (n_up + 1) + [hbm] * (n_up - 1),
         out_specs=[vmem] * n_core,
         out_shape=[jax.ShapeDtypeStruct((n_up, share, width), jnp.float32)] * n_core,
         scratch_shapes=[
             pltpu.VMEM((n_up - 1, steps, states, block), got[0].dtype),
-            pltpu.VMEM((steps, block, width), upper_rows.dtype),
-            pltpu.SemaphoreType.DMA((n_up, steps)),
+            pltpu.SemaphoreType.DMA((n_up - 1, steps)),
         ],
         compiler_params=params(),
         cost_estimate=cost(0.01),
-    )(me.reshape(1), core.reshape(1), own, in_hbm(upper_rows), *so_far, *got)
+    )(me.reshape(1), core.reshape(1), own, in_vmem(rows), *so_far, *got)
 
 
 def tail_product(depth, got, own, forward, backward):
@@ -275,15 +296,16 @@
         cross(turned[0])
         up_tail = after(upper_rows[main_rows + 2 * unit :], *crossed[0])
         pass_on(up_tail, up_tail)
-        for i in range(1, n_dep - 1):
-            pass_on(forward[-1], backward[-1])
         sorted_tail = lax.all_to_all(tail_rows, "depth", 0, 0)
         own = rows_product(after(later_rows, turned[0]), upper_rows, 0, 4 * unit, (), per_block, 2)
         cross(turned[1])
         so_far = [rows_product(g, upper_rows, main_rows, 2 * unit, (), per_block, 2) for g in crossed[0]]
-
-        def reduced(i, got, *others_first):
-            mine_of, *for_others = turned_products(me, my_core, own[i], [x[i] for x in so_far], got, upper_rows, n_core)
+        for i in range(1, n_dep - 1):
+            held = (forward[-1], backward[-1])
+            pass_on(*(after(held, *own, *so_far[0]) if i == 1 else held))
+
+        def reduced(i, got, main_held, *others_first):
+            mine_of, *for_others = turned_products(me, my_core, own[i], [x[i] for x in so_far], got, main_held, n_core)
             total = mine_of
             for k, leaving in enumerate(for_others, 1):
                 pairs = [(low(y, c), low(y, (c + k) % n_core)) for y in range(n_up) for c in range(n_core)]
@@ -292,9 +314,9 @@
             by_owner = total.reshape(n_up * n_dep, half, width)
             return total, jnp.sum(lax.all_to_all(by_owner, OWNERS, 0, 0, axis_index_groups=same_core), axis=0)
 
-        _, sum_a = reduced(0, crossed[1], sorted_tail)
+        _, sum_a = reduced(0, crossed[1], held_rows(after(upper_rows, *so_far[0]), main_rows), sorted_tail)
         cross(sorted_tail, sum_a)
-        last, sum_b = reduced(1, crossed[2], sum_a)
+        last, sum_b = reduced(1, crossed[2], held_rows(after(upper_rows, sum_a), main_rows), sum_a)
         main = jnp.concatenate([sum_a, sum_b], axis=0)
 
         terms = [tail_product(depth, after(g, last), up_tail, forward, backward) for g in crossed[3]]

time: 106 us -> 105 us (level)
  Pallas kernels: 22.1 us -> 24.8 us
  waiting for transfers between devices: 29.4 us -> 26.9 us
  starting transfers between devices: 44.3 us -> 42.1 us
    ppermute x3, waiting for transfers between devices: 11.8 us -> 3.34 us  [pass_on(): backward.append(lax.ppermute(held_down, 'depth', down[:n_dep - 1 - i]))]
    ppermute x4, waiting for transfers between devices: 4.44 us -> 9.34 us  [shifted(): lax.ppermute(x, 'upper', [((u + shift) % n_up, u) for u in range(n_up)])]
    pallas_call x0 -> x2, Pallas kernels: none -> 4.74 us  [held_rows(): pl.pallas_call(body, in_specs=[pl.BlockSpec(memory_space=pltpu.HBM)], out...]
    all_to_all x2, starting transfers between devices: 18.7 us -> 16.1 us  [reduced(): lax.all_to_all(by_owner, OWNERS, 0, 0, axis_index_groups=same_core)]
    all_to_all x1, starting transfers between devices: 4.14 us -> 6.74 us  [local(): sorted_tail = lax.all_to_all(tail_rows, 'depth', 0, 0)]
    pallas_call x2, Pallas kernels: 6.17 us -> 3.82 us  [turned_products(): pl.pallas_call(body, in_specs=[pl.BlockSpec(memory_space=pltpu.SMEM)] * 2...]
    ppermute x3, starting transfers between devices: 8.76 us -> 7.2 us  [pass_on(): forward.append(lax.ppermute(held_up, 'depth', up[i:]))]
    unnamed x22 -> x30, local copies, waits for them, and re-layouts: 3.08 us -> 3.74 us
  transfers between devices with their start and end apart: 18 -> 18, of which waited for: 6 -> 10; matrix products, arithmetic and copies ran while one was open for 4% -> 4% of each run, Pallas kernels for 21% -> 24%
where the time goes in v5:
time: 105 us; the launch traced here: 104 us
  starting transfers between devices  42.1 us (40%)
  waiting for transfers between devices  26.9 us (26%)
  Pallas kernels  24.8 us (24%)
  local copies, waits for them, and re-layouts  6.22 us (6%)
  other arithmetic  3.71 us (4%)
    all_to_all x2, starting transfers between devices, reduced(): lax.all_to_all(by_owner, OWNERS, 0, 0, axis_index_groups=same_core)  16.1 us
    all_to_all x2, waiting for transfers between devices, reduced(): lax.all_to_all(by_owner, OWNERS, 0, 0, axis_index_groups=same_core)  10.6 us
    ppermute x4, waiting for transfers between devices, shifted(): lax.ppermute(x, 'upper', [((u + shift) % n_up, u) for u in range(n_up)])  9.34 us
    ppermute x3, starting transfers between devices, pass_on(): forward.append(lax.ppermute(held_up, 'depth', up[i:]))  7.2 us
    pallas_call x2, Pallas kernels, rows_product(): pl.pallas_call(body, grid=(steps,), in_specs=[pl.BlockSpec((block, states...  7.06 us
    pallas_call x1, Pallas kernels, turn(): pl.pallas_call(body, grid=(mains + 1,), in_specs=[pl.BlockSpec((block, co...  6.89 us
    all_to_all x1, starting transfers between devices, local(): sorted_tail = lax.all_to_all(tail_rows, 'depth', 0, 0)  6.74 us
    ppermute x4, starting transfers between devices, shifted(): lax.ppermute(x, 'upper', [((u + shift) % n_up, u) for u in range(n_up)])  6.08 us
  transfers between devices with their start and end apart: 18, of which 10 were waited for; matrix products, arithmetic and copies ran while one was open for 4% of the time, Pallas kernels for 24%

profile of v5, /device:TPU:0, one launch (start us, length us, event | category | flops | bytes accessed | tf_op | source)
XLA Modules:
  0.0 104.1 jit_solution(18059417404603939991)
XLA Ops:
  0.0 1.1 %slice_bitcast_fusion.1 = bf16[1024,256]{1,0:T(8,128)(2,1)S(1)} fusion(bf16[1,8192,256]{2,1,0:T(8,128)(2,1)} %param.8), kind=kLoop, calls=%fused_computation.1 | loop fusion | bytes 1048576 | tf_op jit(solution)/shard_map/slice | solution.py:292
  1.1 3.0 %collective-permute-start = (bf16[1024,256]{1,0:T(8,128)(2,1)S(1)}, bf16[1024,256]{1,0:T(8,128)(2,1)S(1)}, u32[]{:S(2)}, u32[]{:S(2)}) collective-permute-start(bf16[1024,256]{1,0:T(8,128)(2,1)S(1)} %slice_bitcast_fusion.1), channel_id=1, source_target_pairs={{4,0},{0,4},{5,1},{1,5},{6,2},{2,6},{7,3},{3,7},{12,8},{8,12},{13,... | collective-permute-start | bytes 1572872 | tf_op jit(solution)/shard_map/ppermute | solution.py:246
  4.1 6.9 %shard_map.82 = (bf16[128,6144]{1,0:T(8,128)(2,1)}, bf16[128,6144]{1,0:T(8,128)(2,1)}, bf16[4,64,1024]{2,1,0:T(8,128)(2,1)S(1)}) custom-call(bf16[8192,256]{1,0:T(8,128)(2,1)} %bitcast.21), custom_call_target="tpu_custom_call" | custom-call | bytes 30000 | tf_op jit(solution)/shard_map/pallas_call | solution.py:63
  11.0 0.0 collective-permute-start.1
  11.0 1.4 %slice_bitcast_fusion.mid = bf16[1024,384]{1,0:T(8,128)(2,1)S(1)} fusion(bf16[1,8192,384]{2,1,0:T(8,128)(2,1)} %param.9), kind=kLoop, calls=%fused_computation | loop fusion | bytes 1572864 | tf_op jit(solution)/shard_map/slice | solution.py:297
  12.4 4.4 %collective-permute-done.low = bf16[1024,256]{1,0:T(8,128)(2,1)S(1)} collective-permute-done((bf16[1024,256]{1,0:T(8,128)(2,1)S(1)}, bf16[1024,256]{1,0:T(8,128)(2,1)S(1)}, u32[]{:S(2)}, u32[]{:S(2)}) %collective-permute-start) | collective-permute-done | bytes 524320 | tf_op jit(solution)/shard_map/ppermute | solution.py:246
  16.8 0.8 copy-done.2
  17.6 4.1 %collective-permute-start.6 = (bf16[1024,384]{1,0:T(8,128)(2,1)S(1)}, bf16[1024,384]{1,0:T(8,128)(2,1)S(1)}, u32[]{:S(2)}, u32[]{:S(2)}) collective-permute-start(bf16[1024,384]{1,0:T(8,128)(2,1)S(1)} %slice_bitcast_fusion.mid), channel_id=1, source_target_pairs={{0,1},{1,2},{2,3},{4,5},{5,6},{6,7},{8,9},{9,10},{10,11},{12,13},{... | collective-permute-start | bytes 2359304 | tf_op jit(solution)/shard_map/ppermute | solution.py:289
  21.7 1.3 %collective-permute-start.7 = (bf16[1024,384]{1,0:T(8,128)(2,1)S(1)}, bf16[1024,384]{1,0:T(8,128)(2,1)}, u32[]{:S(2)}, u32[]{:S(2)}) collective-permute-start(bf16[1024,384]{1,0:T(8,128)(2,1)S(1)} %slice_bitcast_fusion.mid), channel_id=1, source_target_pairs={{1,0},{2,1},{3,2},{5,4},{6,5},{7,6},{9,8},{10,9},{11,10},{13,12},{... | collective-permute-start | bytes 2359304 | tf_op jit(solution)/shard_map/ppermute | solution.py:290
  23.0 1.6 %collective-permute-start.3 = (bf16[128,6144]{1,0:T(8,128)(2,1)}, bf16[128,6144]{1,0:T(8,128)(2,1)S(1)}, u32[]{:S(2)}, u32[]{:S(2)}) collective-permute-start(bf16[128,6144]{1,0:T(8,128)(2,1)} %get-tuple-element.42), channel_id=1, source_target_pairs={{4,0},{0,4},{5,1},{1,5},{6,2},{2,6},{7,3},{3,7},{12,8},{8,12},{13,... | collective-permute-start | bytes 4718600 | tf_op jit(solution)/shard_map/ppermute | solution.py:246
  24.6 6.7 %all-to-all-start = ((bf16[4,64,1024]{2,1,0:T(8,128)(2,1)}), bf16[4,64,1024]{2,1,0:T(8,128)(2,1)}, u32[]{:S(2)}, u32[]{:S(2)}) async-start(bf16[4,64,1024]{2,1,0:T(8,128)(2,1)} %copy-done.1), calls=%async_computation | async-start | bytes 1048576 | tf_op jit(solution)/shard_map/all_to_all | solution.py:299
  31.3 2.2 %copy-done = bf16[1,8192,256]{2,1,0:T(8,128)(2,1)S(1)} copy-done((bf16[1,8192,256]{2,1,0:T(8,128)(2,1)S(1)}, bf16[1,8192,256]{2,1,0:T(8,128)(2,1)}, u32[]{:S(2)}) %copy-start) | copy-done | bytes 4194328
  33.5 5.4 %shard_map.83 = (f32[128,384]{1,0:T(8,128)S(1)}, f32[128,384]{1,0:T(8,128)S(1)}) custom-call(bf16[8192,256]{1,0:T(8,128)(2,1)S(1)} %bitcast.22, bf16[8192,384]{1,0:T(8,128)(2,1)} %bitcast.23), custom_call_target="tpu_custom_call" | custom-call | bytes 30000 | tf_op jit(solution)/shard_map/pallas_call | solution.py:106
  38.9 1.7 %shard_map.84 = (f32[128,384]{1,0:T(8,128)S(1)}, f32[128,384]{1,0:T(8,128)S(1)}) custom-call(bf16[1024,256]{1,0:T(8,128)(2,1)S(1)} %copy-done.3, bf16[8192,384]{1,0:T(8,128)(2,1)} %bitcast.24), custom_call_target="tpu_custom_call" | custom-call | bytes 30000 | tf_op jit(solution)/shard_map/pallas_call | solution.py:106
  40.6 0.0 copy-start.6
  40.6 0.7 copy-done.6
  41.3 0.0 collective-permute-done.6.refs_0_
  41.3 3.3 %collective-permute-done.7.refs_3_ = bf16[1024,384]{1,0:T(8,128)(2,1)} collective-permute-done((bf16[1024,384]{1,0:T(8,128)(2,1)S(1)}, bf16[1024,384]{1,0:T(8,128)(2,1)}, u32[]{:S(2)}, u32[]{:S(2)}) %collective-permute-start.7) | collective-permute-done | bytes 786464 | tf_op jit(solution)/shard_map/ppermute | solution.py:290
  44.7 1.6 %collective-permute-start.8 = (bf16[1024,384]{1,0:T(8,128)(2,1)S(1)}, bf16[1024,384]{1,0:T(8,128)(2,1)}, u32[]{:S(2)}, u32[]{:S(2)}) collective-permute-start(bf16[1024,384]{1,0:T(8,128)(2,1)S(1)} %collective-permute-done.6.refs_0_), channel_id=1, source_target_pairs={{1,2},{2,3},{5,6},{6,7},{9,10},{10,11},{13,14},{14,15},{17,18},{18... | collective-permute-start | bytes 2359304 | tf_op jit(solution)/shard_map/ppermute | solution.py:289
  46.2 1.3 %collective-permute-start.10 = (bf16[1024,384]{1,0:T(8,128)(2,1)}, bf16[1024,384]{1,0:T(8,128)(2,1)}, u32[]{:S(2)}, u32[]{:S(2)}) collective-permute-start(bf16[1024,384]{1,0:T(8,128)(2,1)} %collective-permute-done.7.refs_3_), channel_id=1, source_target_pairs={{1,0},{2,1},{5,4},{6,5},{9,8},{10,9},{13,12},{14,13},{17,16},{18,1... | collective-permute-start | bytes 2359304 | tf_op jit(solution)/shard_map/ppermute | solution.py:290
  47.5 0.0 copy-start.5
  47.5 0.0 copy-start.7
  47.5 2.4 %shard_map.85.up = bf16[6144,384]{1,0:T(8,128)(2,1)S(1)} custom-call(bf16[8192,384]{1,0:T(8,128)(2,1)} %bitcast.25), custom_call_target="tpu_custom_call" | custom-call | bytes 30000 | tf_op jit(solution)/shard_map/pallas_call | solution.py:130
  49.9 0.7 collective-permute-done.1.refs_1_
  50.7 2.3 %shard_map.86 = (f32[2,64,384]{2,1,0:T(8,128)S(1)}, f32[2,64,384]{2,1,0:T(8,128)S(1)}) custom-call(s32[1]{0:T(128)} %bitcast.me_at, s32[1]{0:T(128)} %bitcast.1.core_at, f32[128,384]{1,0:T(8,128)S(1)} %copy-done.5, bf16[6144,384]{1,0:T(8,128)(2,1)S(1)} %shard_map.85.up, f32[128,384]{1,0:T(8,128)S(1)} %copy-done.7, ...), custom_call_target="tpu_custom_call" | custom-call | bytes 30000 | tf_op jit(solution)/shard_map/pallas_call | solution.py:185
  53.0 0.1 collective-permute-start.2
  53.1 1.4 %collective-permute-done.2 = f32[2,64,384]{2,1,0:T(8,128)S(1)} collective-permute-done((f32[2,64,384]{2,1,0:T(8,128)S(1)}, f32[2,64,384]{2,1,0:T(8,128)S(1)}, u32[]{:S(2)}, u32[]{:S(2)}) %collective-permute-start.2) | collective-permute-done | bytes 196640 | tf_op jit(solution)/shard_map/ppermute | solution.py:312
  54.5 0.7 add.75
  55.2 0.8 all-to-all-done
  56.0 9.7 %all-to-all-start.1 = ((f32[8,16,384]{2,1,0:T(8,128)}), f32[8,16,384]{2,1,0:T(8,128)}, u32[]{:S(2)}, u32[]{:S(2)}) async-start(f32[8,16,384]{2,1,0:T(8,128)} %bitcast.27), calls=%async_computation.1 | async-start | bytes 393216 | tf_op jit(solution)/shard_map/all_to_all | solution.py:315
  65.6 0.0 collective-permute-done.8.refs_1_
  65.6 1.6 %collective-permute-start.9 = (bf16[1024,384]{1,0:T(8,128)(2,1)}, bf16[1024,384]{1,0:T(8,128)(2,1)}, u32[]{:S(2)}, u32[]{:S(2)}) collective-permute-start(bf16[1024,384]{1,0:T(8,128)(2,1)} %collective-permute-done.8.refs_1_), channel_id=1, source_target_pairs={{2,3},{6,7},{10,11},{14,15},{18,19},{22,23},{26,27},{30,31}} | collective-permute-start | bytes 2359304 | tf_op jit(solution)/shard_map/ppermute | solution.py:289
  67.2 0.0 collective-permute-done.10.refs_4_
  67.2 1.3 %collective-permute-start.11 = (bf16[1024,384]{1,0:T(8,128)(2,1)}, bf16[1024,384]{1,0:T(8,128)(2,1)}, u32[]{:S(2)}, u32[]{:S(2)}) collective-permute-start(bf16[1024,384]{1,0:T(8,128)(2,1)} %collective-permute-done.10.refs_4_), channel_id=1, source_target_pairs={{1,0},{5,4},{9,8},{13,12},{17,16},{21,20},{25,24},{29,28}} | collective-permute-start | bytes 2359304 | tf_op jit(solution)/shard_map/ppermute | solution.py:290
  68.5 6.5 %all-to-all-done.1 = f32[8,16,384]{2,1,0:T(8,128)} async-done(((f32[8,16,384]{2,1,0:T(8,128)}), f32[8,16,384]{2,1,0:T(8,128)}, u32[]{:S(2)}, u32[]{:S(2)}) %all-to-all-start.1) | async-done | bytes 196640 | tf_op jit(solution)/shard_map/all_to_all | solution.py:315
  75.0 1.6 %reduce_sum.18 = f32[16,384]{1,0:T(8,128)} reduce(f32[8,16,384]{2,1,0:T(8,128)} %all-to-all-done.1, f32[]{:T(128)} %constant.88.clone.1), dimensions={0}, to_apply=%region_0.1 | reduce | flops 43008 | bytes 221188 | tf_op jit(solution)/shard_map/reduce_sum | solution.py:315
  76.6 1.5 %collective-permute-start.5 = (bf16[4,64,1024]{2,1,0:T(8,128)(2,1)}, bf16[4,64,1024]{2,1,0:T(8,128)(2,1)}, u32[]{:S(2)}, u32[]{:S(2)}) collective-permute-start(bf16[4,64,1024]{2,1,0:T(8,128)(2,1)} %all-to-all-done), channel_id=1, source_target_pairs={{4,0},{0,4},{5,1},{1,5},{6,2},{2,6},{7,3},{3,7},{12,8},{8,12},{13,... | collective-permute-start | bytes 1572872 | tf_op jit(solution)/shard_map/ppermute | solution.py:246
  78.0 2.3 %shard_map.87.up = bf16[6144,384]{1,0:T(8,128)(2,1)S(1)} custom-call(bf16[8192,384]{1,0:T(8,128)(2,1)} %bitcast.26), custom_call_target="tpu_custom_call" | custom-call | bytes 30000 | tf_op jit(solution)/shard_map/pallas_call | solution.py:130
  80.4 0.0 copy-start.9
  80.4 3.8 %collective-permute-done.3.refs_1_ = bf16[128,6144]{1,0:T(8,128)(2,1)S(1)} collective-permute-done((bf16[128,6144]{1,0:T(8,128)(2,1)}, bf16[128,6144]{1,0:T(8,128)(2,1)S(1)}, u32[]{:S(2)}, u32[]{:S(2)}) %collective-permute-start.3) | collective-permute-done | bytes 1572896 | tf_op jit(solution)/shard_map/ppermute | solution.py:246
  84.2 1.5 %shard_map.88 = (f32[2,64,384]{2,1,0:T(8,128)S(1)}, f32[2,64,384]{2,1,0:T(8,128)S(1)}) custom-call(s32[1]{0:T(128)} %bitcast.me_at, s32[1]{0:T(128)} %bitcast.1.core_at, f32[128,384]{1,0:T(8,128)S(1)} %get-tuple-element.39.mine, bf16[6144,384]{1,0:T(8,128)(2,1)S(1)} %shard_map.87.up, f32[128,384]{1,0:T(8,128)S(1)} %get-tuple-element.33.refs_0_, ...), custom_call_target="tpu_custom_call" | custom-call | bytes 30000 | tf_op jit(solution)/shard_map/pallas_call | solution.py:185
  85.7 0.0 copy-start.14
  85.7 0.0 copy-start.8
  85.8 0.0 copy-start.10
  85.8 0.0 copy-start.11
  85.8 0.0 copy-start.12
  85.8 0.0 copy-start.13
  85.8 0.1 collective-permute-start.4
  85.9 1.4 %collective-permute-done.4 = f32[2,64,384]{2,1,0:T(8,128)S(1)} collective-permute-done((f32[2,64,384]{2,1,0:T(8,128)S(1)}, f32[2,64,384]{2,1,0:T(8,128)S(1)}, u32[]{:S(2)}, u32[]{:S(2)}) %collective-permute-start.4) | collective-permute-done | bytes 196640 | tf_op jit(solution)/shard_map/ppermute | solution.py:312
  87.3 0.7 add.76
  88.0 6.4 %all-to-all-start.2 = ((f32[8,16,384]{2,1,0:T(8,128)}), f32[8,16,384]{2,1,0:T(8,128)S(1)}, u32[]{:S(2)}, u32[]{:S(2)}) async-start(f32[8,16,384]{2,1,0:T(8,128)} %bitcast.6), calls=%async_computation.2 | async-start | bytes 393216 | tf_op jit(solution)/shard_map/all_to_all | solution.py:315
  94.4 0.4 collective-permute-done.5.low
  94.8 0.0 collective-permute-done.9.refs_2_
  94.8 0.0 collective-permute-done.11.refs_5_
  94.8 2.3 %shard_map.89 = f32[64,384]{1,0:T(8,128)S(1)} custom-call(s32[1]{0:T(128)} %bitcast.7.at, bf16[4,64,1024]{2,1,0:T(8,128)(2,1)} %collective-permute-done.5.low, bf16[1024,384]{1,0:T(8,128)(2,1)S(1)} %slice_bitcast_fusion.mid, bf16[1024,384]{1,0:T(8,128)(2,1)S(1)} %collective-permute-done.6.refs_0_, bf16[1024,384]{1,0:T(8,128)(2,1)} %collective-permute-done.8.refs_1_, ...), custom_call_target="tpu_custom_call" | custom-call | bytes 30000 | tf_op jit(solution)/shard_map/pallas_call | solution.py:225
  97.1 0.9 collective-permute-start.14
  98.0 1.0 collective-permute-start.13
  99.0 0.1 collective-permute-start.12
  99.1 4.1 %all-to-all-done.2 = f32[8,16,384]{2,1,0:T(8,128)S(1)} async-done(((f32[8,16,384]{2,1,0:T(8,128)}), f32[8,16,384]{2,1,0:T(8,128)S(1)}, u32[]{:S(2)}, u32[]{:S(2)}) %all-to-all-start.2) | async-done | bytes 196640 | tf_op jit(solution)/shard_map/all_to_all | solution.py:315
  103.3 0.0 collective-permute-done.14
  103.3 0.0 collective-permute-done.13
  103.3 0.0 collective-permute-done.12
  103.3 0.0 copy-done.8
  103.3 0.7 fusion.2
  (22 shorter events, 0.1 us)
Async XLA Ops:
  1.1 15.8 %collective-permute-start = (bf16[1024,256]{1,0:T(8,128)(2,1)S(1)}, bf16[1024,256]{1,0:T(8,128)(2,1)S(1)}, u32[]{:S(2)}, u32[]{:S(2)}) collective-permute-start(bf16[1024,256]{1,0:T(8,128)(2,1)S(1)} %slice_bitcast_fusion.1), channel_id=1, source_target_pairs={{4,0},{0,4},{5,1},{1,5},{6,2},{2,6},{7,3},{3,7},{12,8},{8,12},{13,... | collective-permute-start | bytes 1572872 | tf_op jit(solution)/shard_map/ppermute | solution.py:246
  11.0 13.6 %copy-start.1 = (bf16[4,64,1024]{2,1,0:T(8,128)(2,1)}, bf16[4,64,1024]{2,1,0:T(8,128)(2,1)S(1)}, u32[]{:S(2)}) copy-start(bf16[4,64,1024]{2,1,0:T(8,128)(2,1)S(1)} %get-tuple-element.37) | copy-start | bytes 1572868
  11.0 39.7 %collective-permute-start.1 = (bf16[128,6144]{1,0:T(8,128)(2,1)}, bf16[128,6144]{1,0:T(8,128)(2,1)}, u32[]{:S(2)}, u32[]{:S(2)}) collective-permute-start(bf16[128,6144]{1,0:T(8,128)(2,1)} %get-tuple-element.29), channel_id=1, source_target_pairs={{4,0},{0,4},{5,1},{1,5},{6,2},{2,6},{7,3},{3,7},{12,8},{8,12},{13,... | collective-permute-start | bytes 4718600 | tf_op jit(solution)/shard_map/ppermute | solution.py:246
  16.8 0.8 copy-start.2
  17.6 23.7 %collective-permute-start.6 = (bf16[1024,384]{1,0:T(8,128)(2,1)S(1)}, bf16[1024,384]{1,0:T(8,128)(2,1)S(1)}, u32[]{:S(2)}, u32[]{:S(2)}) collective-permute-start(bf16[1024,384]{1,0:T(8,128)(2,1)S(1)} %slice_bitcast_fusion.mid), channel_id=1, source_target_pairs={{0,1},{1,2},{2,3},{4,5},{5,6},{6,7},{8,9},{9,10},{10,11},{12,13},{... | collective-permute-start | bytes 2359304 | tf_op jit(solution)/shard_map/ppermute | solution.py:289
  21.7 22.9 %collective-permute-start.7 = (bf16[1024,384]{1,0:T(8,128)(2,1)S(1)}, bf16[1024,384]{1,0:T(8,128)(2,1)}, u32[]{:S(2)}, u32[]{:S(2)}) collective-permute-start(bf16[1024,384]{1,0:T(8,128)(2,1)S(1)} %slice_bitcast_fusion.mid), channel_id=1, source_target_pairs={{1,0},{2,1},{3,2},{5,4},{6,5},{7,6},{9,8},{10,9},{11,10},{13,12},{... | collective-permute-start | bytes 2359304 | tf_op jit(solution)/shard_map/ppermute | solution.py:290
  23.0 61.2 %collective-permute-start.3 = (bf16[128,6144]{1,0:T(8,128)(2,1)}, bf16[128,6144]{1,0:T(8,128)(2,1)S(1)}, u32[]{:S(2)}, u32[]{:S(2)}) collective-permute-start(bf16[128,6144]{1,0:T(8,128)(2,1)} %get-tuple-element.42), channel_id=1, source_target_pairs={{4,0},{0,4},{5,1},{1,5},{6,2},{2,6},{7,3},{3,7},{12,8},{8,12},{13,... | collective-permute-start | bytes 4718600 | tf_op jit(solution)/shard_map/ppermute | solution.py:246
  24.6 31.4 %all-to-all-start = ((bf16[4,64,1024]{2,1,0:T(8,128)(2,1)}), bf16[4,64,1024]{2,1,0:T(8,128)(2,1)}, u32[]{:S(2)}, u32[]{:S(2)}) async-start(bf16[4,64,1024]{2,1,0:T(8,128)(2,1)} %copy-done.1), calls=%async_computation | async-start | bytes 1048576 | tf_op jit(solution)/shard_map/all_to_all | solution.py:299
  31.3 2.2 %copy-start = (bf16[1,8192,256]{2,1,0:T(8,128)(2,1)S(1)}, bf16[1,8192,256]{2,1,0:T(8,128)(2,1)}, u32[]{:S(2)}) copy-start(bf16[1,8192,256]{2,1,0:T(8,128)(2,1)} %param.8) | copy-start | bytes 12582916
  33.5 5.4 %copy-start.3 = (bf16[1024,256]{1,0:T(8,128)(2,1)S(1)}, bf16[1024,256]{1,0:T(8,128)(2,1)}, u32[]{:S(2)}) copy-start(bf16[1024,256]{1,0:T(8,128)(2,1)} %copy-done.2) | copy-start | bytes 1572868
  38.9 5.7 %copy-start.4 = (f32[128,384]{1,0:T(8,128)}, f32[128,384]{1,0:T(8,128)S(1)}, u32[]{:S(2)}) copy-start(f32[128,384]{1,0:T(8,128)S(1)} %get-tuple-element.31.mine) | copy-start | bytes 589828
  40.6 0.7 copy-start.6
  44.7 21.0 %collective-permute-start.8 = (bf16[1024,384]{1,0:T(8,128)(2,1)S(1)}, bf16[1024,384]{1,0:T(8,128)(2,1)}, u32[]{:S(2)}, u32[]{:S(2)}) collective-permute-start(bf16[1024,384]{1,0:T(8,128)(2,1)S(1)} %collective-permute-done.6.refs_0_), channel_id=1, source_target_pairs={{1,2},{2,3},{5,6},{6,7},{9,10},{10,11},{13,14},{14,15},{17,18},{18... | collective-permute-start | bytes 2359304 | tf_op jit(solution)/shard_map/ppermute | solution.py:289
  46.2 21.0 %collective-permute-start.10 = (bf16[1024,384]{1,0:T(8,128)(2,1)}, bf16[1024,384]{1,0:T(8,128)(2,1)}, u32[]{:S(2)}, u32[]{:S(2)}) collective-permute-start(bf16[1024,384]{1,0:T(8,128)(2,1)} %collective-permute-done.7.refs_3_), channel_id=1, source_target_pairs={{1,0},{2,1},{5,4},{6,5},{9,8},{10,9},{13,12},{14,13},{17,16},{18,1... | collective-permute-start | bytes 2359304 | tf_op jit(solution)/shard_map/ppermute | solution.py:290
  47.5 3.1 %copy-start.5 = (f32[128,384]{1,0:T(8,128)S(1)}, f32[128,384]{1,0:T(8,128)}, u32[]{:S(2)}) copy-start(f32[128,384]{1,0:T(8,128)} %copy-done.4) | copy-start | bytes 589828
  47.5 3.1 %copy-start.7 = (f32[128,384]{1,0:T(8,128)S(1)}, f32[128,384]{1,0:T(8,128)}, u32[]{:S(2)}) copy-start(f32[128,384]{1,0:T(8,128)} %copy-done.6) | copy-start | bytes 589828
  53.0 1.5 %collective-permute-start.2 = (f32[2,64,384]{2,1,0:T(8,128)S(1)}, f32[2,64,384]{2,1,0:T(8,128)S(1)}, u32[]{:S(2)}, u32[]{:S(2)}) collective-permute-start(f32[2,64,384]{2,1,0:T(8,128)S(1)} %get-tuple-element.36), channel_id=1, source_target_pairs={{0,8},{8,0},{16,24},{24,16},{1,9},{9,1},{17,25},{25,17},{2,10},{10... | collective-permute-start | bytes 589832 | tf_op jit(solution)/shard_map/ppermute | solution.py:312
  56.0 19.0 %all-to-all-start.1 = ((f32[8,16,384]{2,1,0:T(8,128)}), f32[8,16,384]{2,1,0:T(8,128)}, u32[]{:S(2)}, u32[]{:S(2)}) async-start(f32[8,16,384]{2,1,0:T(8,128)} %bitcast.27), calls=%async_computation.1 | async-start | bytes 393216 | tf_op jit(solution)/shard_map/all_to_all | solution.py:315
  65.6 29.1 %collective-permute-start.9 = (bf16[1024,384]{1,0:T(8,128)(2,1)}, bf16[1024,384]{1,0:T(8,128)(2,1)}, u32[]{:S(2)}, u32[]{:S(2)}) collective-permute-start(bf16[1024,384]{1,0:T(8,128)(2,1)} %collective-permute-done.8.refs_1_), channel_id=1, source_target_pairs={{2,3},{6,7},{10,11},{14,15},{18,19},{22,23},{26,27},{30,31}} | collective-permute-start | bytes 2359304 | tf_op jit(solution)/shard_map/ppermute | solution.py:289
  67.2 27.6 %collective-permute-start.11 = (bf16[1024,384]{1,0:T(8,128)(2,1)}, bf16[1024,384]{1,0:T(8,128)(2,1)}, u32[]{:S(2)}, u32[]{:S(2)}) collective-permute-start(bf16[1024,384]{1,0:T(8,128)(2,1)} %collective-permute-done.10.refs_4_), channel_id=1, source_target_pairs={{1,0},{5,4},{9,8},{13,12},{17,16},{21,20},{25,24},{29,28}} | collective-permute-start | bytes 2359304 | tf_op jit(solution)/shard_map/ppermute | solution.py:290
  76.6 18.2 %collective-permute-start.5 = (bf16[4,64,1024]{2,1,0:T(8,128)(2,1)}, bf16[4,64,1024]{2,1,0:T(8,128)(2,1)}, u32[]{:S(2)}, u32[]{:S(2)}) collective-permute-start(bf16[4,64,1024]{2,1,0:T(8,128)(2,1)} %all-to-all-done), channel_id=1, source_target_pairs={{4,0},{0,4},{5,1},{1,5},{6,2},{2,6},{7,3},{3,7},{12,8},{8,12},{13,... | collective-permute-start | bytes 1572872 | tf_op jit(solution)/shard_map/ppermute | solution.py:246
  80.4 5.5 %copy-start.9 = (s32[384]{0:T(512)S(1)}, s32[384]{0:T(512)}, u32[]{:S(2)}) copy-start(s32[384]{0:T(512)} %param.15) | copy-start | bytes 4612
  85.7 13.4 %copy-start.14 = (s32[32]{0:T(128)S(1)}, s32[32]{0:T(128)}, u32[]{:S(2)}) copy-start(s32[32]{0:T(128)} %param.12) | copy-start | bytes 388
  85.7 17.5 %copy-start.8 = (f32[16,384]{1,0:T(8,128)S(1)}, f32[16,384]{1,0:T(8,128)}, u32[]{:S(2)}) copy-start(f32[16,384]{1,0:T(8,128)} %reduce_sum.18) | copy-start | bytes 73732
  85.8 17.5 %copy-start.10 = (f32[384]{0:T(512)S(1)}, f32[384]{0:T(512)}, u32[]{:S(2)}) copy-start(f32[384]{0:T(512)} %param.11) | copy-start | bytes 4612
  85.8 17.5 %copy-start.11 = (s32[384]{0:T(512)S(1)}, s32[384]{0:T(512)}, u32[]{:S(2)}) copy-start(s32[384]{0:T(512)} %param.13) | copy-start | bytes 4612
  85.8 17.5 %copy-start.12 = (f32[32]{0:T(128)S(1)}, f32[32]{0:T(128)}, u32[]{:S(2)}) copy-start(f32[32]{0:T(128)} %param.10) | copy-start | bytes 388
  85.8 17.5 %copy-start.13 = (s32[32]{0:T(128)S(1)}, s32[32]{0:T(128)}, u32[]{:S(2)}) copy-start(s32[32]{0:T(128)} %param.14) | copy-start | bytes 388
  85.8 1.5 %collective-permute-start.4 = (f32[2,64,384]{2,1,0:T(8,128)S(1)}, f32[2,64,384]{2,1,0:T(8,128)S(1)}, u32[]{:S(2)}, u32[]{:S(2)}) collective-permute-start(f32[2,64,384]{2,1,0:T(8,128)S(1)} %get-tuple-element.44), channel_id=1, source_target_pairs={{0,8},{8,0},{16,24},{24,16},{1,9},{9,1},{17,25},{25,17},{2,10},{10... | collective-permute-start | bytes 589832 | tf_op jit(solution)/shard_map/ppermute | solution.py:312
  88.0 15.2 %all-to-all-start.2 = ((f32[8,16,384]{2,1,0:T(8,128)}), f32[8,16,384]{2,1,0:T(8,128)S(1)}, u32[]{:S(2)}, u32[]{:S(2)}) async-start(f32[8,16,384]{2,1,0:T(8,128)} %bitcast.6), calls=%async_computation.2 | async-start | bytes 393216 | tf_op jit(solution)/shard_map/all_to_all | solution.py:315
  97.1 6.2 %collective-permute-start.14 = (f32[32,384]{1,0:T(8,128)S(1)}, f32[32,384]{1,0:T(8,128)S(1)}, u32[]{:S(2)}, u32[]{:S(2)}) collective-permute-start(f32[32,384]{1,0:T(8,128)S(1)} %get-tuple-element.54), channel_id=1, source_target_pairs={{0,24},{8,16},{16,8},{24,0},{1,25},{9,17},{17,9},{25,1},{2,26},{10... | collective-permute-start | bytes 147464 | tf_op jit(solution)/shard_map/ppermute | solution.py:337
  98.0 5.2 %collective-permute-start.13 = (f32[32,384]{1,0:T(8,128)S(1)}, f32[32,384]{1,0:T(8,128)S(1)}, u32[]{:S(2)}, u32[]{:S(2)}) collective-permute-start(f32[32,384]{1,0:T(8,128)S(1)} %get-tuple-element.53), channel_id=1, source_target_pairs={{0,16},{8,24},{16,0},{24,8},{1,17},{9,25},{17,1},{25,9},{2,18},{10... | collective-permute-start | bytes 147464 | tf_op jit(solution)/shard_map/ppermute | solution.py:337
  99.0 4.3 %collective-permute-start.12 = (f32[32,384]{1,0:T(8,128)S(1)}, f32[32,384]{1,0:T(8,128)S(1)}, u32[]{:S(2)}, u32[]{:S(2)}) collective-permute-start(f32[32,384]{1,0:T(8,128)S(1)} %dynamic-slice_bitcast_fusion.2), channel_id=1, source_target_pairs={{0,8},{8,0},{16,24},{24,16},{1,9},{9,1},{17,25},{25,17},{2,10},{10... | collective-permute-start | bytes 147464 | tf_op jit(solution)/shard_map/ppermute | solution.py:337

commit v6 on v5

--- a/solution.py
+++ b/solution.py
@@ -37,40 +37,39 @@
     return pl.BlockSpec(shape, lambda *_: (0,) * len(shape))
 
 
-def turn(lower_rows, parts, unit, mine, n_dep):
+def turn(lower_rows, n_tail, n_main, parts, mine, n_dep):
     rows, cols = lower_rows.shape
     per_block = cols // mine
     kind = lower_rows.dtype
-    block = 2 * unit
-    mains = rows // block - 2
-
-    def body(low, *outs):
-        i = pl.program_id(0)
+    steps = 6
+    block = n_main // steps
+    skipped = (rows - n_main) // block
+
+    def body(low, low_tail, *outs):
         flipped = low[...].astype(jnp.float32).T
-
-        @pl.when(i < mains)
+        for out, part in zip(outs, split_states(flipped, per_block, parts)):
+            out[...] = part.astype(kind)
+
+        @pl.when(pl.program_id(0) == steps - 1)
         def _():
-            for out, part in zip(outs, split_states(flipped, per_block, parts)):
-                out[...] = part.astype(kind)
-
-        @pl.when(i == mains)
-        def _():
-            by_depth = flipped.reshape(per_block // n_dep, n_dep, mine, block)
+            by_depth = low_tail[...].astype(jnp.float32).T.reshape(per_block // n_dep, n_dep, mine, n_tail)
             for z in range(n_dep):
-                outs[-1][z] = by_depth[:, z].reshape(cols // n_dep, block).astype(kind)
-
-    tail_shape = (n_dep, cols // n_dep, block)
-    return pl.pallas_call(
-        body,
-        grid=(mains + 1,),
-        in_specs=[pl.BlockSpec((block, cols), lambda i: (jnp.where(i < mains, i, i + 1), 0))],
-        out_specs=[pl.BlockSpec((cols // parts, block), lambda i: (0, jnp.minimum(i, mains - 1)))] * parts
-        + [whole(tail_shape)],
-        out_shape=[jax.ShapeDtypeStruct((cols // parts, mains * block), kind)] * parts
+                outs[-1][z] = by_depth[:, z].reshape(cols // n_dep, n_tail).astype(kind)
+
+    tail_shape = (n_dep, cols // n_dep, n_tail)
+    return pl.pallas_call(
+        body,
+        grid=(steps,),
+        in_specs=[
+            pl.BlockSpec((block, cols), lambda i: (i + skipped, 0)),
+            pl.BlockSpec((n_tail, cols), lambda i: (0, 0)),
+        ],
+        out_specs=[pl.BlockSpec((cols // parts, block), lambda i: (0, i))] * parts + [whole(tail_shape)],
+        out_shape=[jax.ShapeDtypeStruct((cols // parts, n_main), kind)] * parts
         + [jax.ShapeDtypeStruct(tail_shape, kind)],
         compiler_params=params(),
         cost_estimate=cost(0.01),
-    )(in_hbm(lower_rows))
+    )(in_hbm(lower_rows), in_hbm(lower_rows))
 
 
 def split_states(product, per_block, parts):
@@ -119,11 +118,11 @@
     )(got, in_hbm(upper_rows), *so_far)
 
 
-def held_rows(upper_rows, k):
-    width = upper_rows.shape[1]
+def held_rows(rows, first, k):
+    width = rows.shape[1]
 
     def body(up, out, sem):
-        copy = pltpu.make_async_copy(up.at[pl.ds(0, k)], out, sem)
+        copy = pltpu.make_async_copy(up.at[pl.ds(first, k)], out, sem)
         copy.start()
         copy.wait()
 
@@ -131,11 +130,11 @@
         body,
         in_specs=[pl.BlockSpec(memory_space=pltpu.HBM)],
         out_specs=pl.BlockSpec(memory_space=pltpu.VMEM),
-        out_shape=pltpu.VMEM((k, width), upper_rows.dtype),
+        out_shape=pltpu.VMEM((k, width), rows.dtype),
         scratch_shapes=[pltpu.SemaphoreType.DMA],
         compiler_params=params(),
         cost_estimate=cost(0.01),
-    )(in_hbm(upper_rows))
+    )(in_hbm(rows))
 
 
 def turned_products(me, core, own, so_far, got, rows, n_core):
@@ -257,8 +256,8 @@
         width = upper_rows.shape[1]
         mine = energy_lower.shape[0]
         per_block = cols // mine
-        unit = rows // 16
-        main_rows = 12 * unit
+        unit = rows // 64
+        n_tail, n_head, n_main = 9 * unit, 7 * unit, 48 * unit
         half = mine // 2
         me = lax.axis_index("upper")
         depth = lax.axis_index("depth")
@@ -289,17 +288,18 @@
             forward.append(lax.ppermute(held_up, "depth", up[i:]))
             backward.append(lax.ppermute(held_down, "depth", down[: n_dep - 1 - i]))
 
-        first = lower_rows[main_rows : main_rows + 2 * unit]
+        first = lower_rows[n_tail : n_tail + n_head]
         cross(first)
         later_rows = after(lower_rows, first)
-        *turned, tail_rows = turn(later_rows, 2, unit, mine, n_dep)
+        *turned, tail_rows = turn(later_rows, n_tail, n_main, 2, mine, n_dep)
         cross(turned[0])
-        up_tail = after(upper_rows[main_rows + 2 * unit :], *crossed[0])
+        up_tail = after(upper_rows[:n_tail], *crossed[0])
         pass_on(up_tail, up_tail)
         sorted_tail = lax.all_to_all(tail_rows, "depth", 0, 0)
-        own = rows_product(after(later_rows, turned[0]), upper_rows, 0, 4 * unit, (), per_block, 2)
+        own = rows_product(after(later_rows, turned[0]), upper_rows, 0, rows // 4, (), per_block, 2)
         cross(turned[1])
-        so_far = [rows_product(g, upper_rows, main_rows, 2 * unit, (), per_block, 2) for g in crossed[0]]
+        head_rows = upper_rows[n_tail : n_tail + n_head]
+        so_far = [rows_product(g, head_rows, 0, n_head, (), per_block, 2) for g in crossed[0]]
         for i in range(1, n_dep - 1):
             held = (forward[-1], backward[-1])
             pass_on(*(after(held, *own, *so_far[0]) if i == 1 else held))
@@ -312,11 +312,15 @@
                 total = total + lax.ppermute(leaving, "lower", pairs)
             total = after(total, *others_first)
             by_owner = total.reshape(n_up * n_dep, half, width)
-            return total, jnp.sum(lax.all_to_all(by_owner, OWNERS, 0, 0, axis_index_groups=same_core), axis=0)
-
-        _, sum_a = reduced(0, crossed[1], held_rows(after(upper_rows, *so_far[0]), main_rows), sorted_tail)
-        cross(sorted_tail, sum_a)
-        last, sum_b = reduced(1, crossed[2], held_rows(after(upper_rows, sum_a), main_rows), sum_a)
+            return total, lax.all_to_all(by_owner, OWNERS, 0, 0, axis_index_groups=same_core)
+
+        held_a = held_rows(after(upper_rows, *so_far[0]), rows - n_main, n_main)
+        sent_a, from_a = reduced(0, crossed[1], held_a, sorted_tail)
+        sum_a = jnp.sum(from_a, axis=0)
+        held_b = held_rows(after(upper_rows, sum_a), rows - n_main, n_main)
+        cross(sorted_tail, from_a)
+        last, from_b = reduced(1, crossed[2], held_b, sum_a)
+        sum_b = jnp.sum(from_b, axis=0)
         main = jnp.concatenate([sum_a, sum_b], axis=0)
 
         terms = [tail_product(depth, after(g, last), up_tail, forward, backward) for g in crossed[3]]
@@ -328,9 +332,9 @@
             return block
 
         total = main
-        for t in range(n_up):
+        for t in reversed(range(n_up)):
             by_core = term_for(my_y + t).reshape(n_core, mine, width)
-            for k in range(n_core):
+            for k in reversed(range(n_core)):
                 term = lax.dynamic_index_in_dim(by_core, (my_core + k) % n_core, 0, keepdims=False)
                 if t or k:
                     pairs = [(low(y, c), low(y + t, (c + k) % n_core)) for y in range(n_up) for c in range(n_core)]

time: 105 us -> 105 us (level)
  local copies, waits for them, and re-layouts: 6.22 us -> 9.29 us
  starting transfers between devices: 42.1 us -> 39.4 us
    ppermute x4, waiting for transfers between devices: 9.34 us -> 5.1 us  [shifted(): lax.ppermute(x, 'upper', [((u + shift) % n_up, u) for u in range(n_up)])]
    all_to_all x2, starting transfers between devices: 16.1 us -> 13.2 us  [reduced(): lax.all_to_all(by_owner, OWNERS, 0, 0, axis_index_groups=same_core)]
    slice x2 -> x3, local copies, waits for them, and re-layouts: 2.46 us -> 4.88 us  [the longest x1 2.03 us: local(): head_rows = upper_rows[n_tail:n_tail + n_head]]
    all_to_all x1, waiting for transfers between devices: 0.76 us -> 3.08 us  [local(): sorted_tail = lax.all_to_all(tail_rows, 'depth', 0, 0)]
    unnamed x30 -> x34, local copies, waits for them, and re-layouts: 3.74 us -> 4.38 us
  transfers between devices with their start and end apart: 18 -> 18, of which waited for: 10 -> 9; matrix products, arithmetic and copies ran while one was open for 4% -> 8% of each run, Pallas kernels for 24% -> 23%
where the time goes in v6:
time: 105 us; the launch traced here: 104 us
  starting transfers between devices  39.4 us (38%)
  waiting for transfers between devices  26 us (25%)
  Pallas kernels  24.1 us (23%)
  local copies, waits for them, and re-layouts  9.29 us (9%)
  other arithmetic  4.65 us (4%)
    all_to_all x2, starting transfers between devices, reduced(): lax.all_to_all(by_owner, OWNERS, 0, 0, axis_index_groups=same_core)  13.2 us
    all_to_all x2, waiting for transfers between devices, reduced(): lax.all_to_all(by_owner, OWNERS, 0, 0, axis_index_groups=same_core)  10.8 us
    ppermute x3, starting transfers between devices, pass_on(): forward.append(lax.ppermute(held_up, 'depth', up[i:]))  7.25 us
    pallas_call x2, Pallas kernels, rows_product(): pl.pallas_call(body, grid=(steps,), in_specs=[pl.BlockSpec((block, states...  7 us
    all_to_all x1, starting transfers between devices, local(): sorted_tail = lax.all_to_all(tail_rows, 'depth', 0, 0)  6.84 us
    pallas_call x1, Pallas kernels, turn(): pl.pallas_call(body, grid=(steps,), in_specs=[pl.BlockSpec((block, cols),...  6.06 us
    ppermute x4, starting transfers between devices, shifted(): lax.ppermute(x, 'upper', [((u + shift) % n_up, u) for u in range(n_up)])  6.03 us
    ppermute x4, waiting for transfers between devices, shifted(): lax.ppermute(x, 'upper', [((u + shift) % n_up, u) for u in range(n_up)])  5.1 us
  transfers between devices with their start and end apart: 18, of which 9 were waited for; matrix products, arithmetic and copies ran while one was open for 8% of the time, Pallas kernels for 23%

profile of v6, /device:TPU:0, one launch (start us, length us, event | category | flops | bytes accessed | tf_op | source)
XLA Modules:
  0.0 103.8 jit_solution(13258698943347895324)
XLA Ops:
  0.0 1.0 %slice_bitcast_fusion.2 = bf16[896,256]{1,0:T(8,128)(2,1)S(1)} fusion(bf16[1,8192,256]{2,1,0:T(8,128)(2,1)} %param.8), kind=kLoop, calls=%fused_computation.2 | loop fusion | bytes 917504 | tf_op jit(solution)/shard_map/slice | solution.py:291
  1.1 3.0 %collective-permute-start = (bf16[896,256]{1,0:T(8,128)(2,1)S(1)}, bf16[896,256]{1,0:T(8,128)(2,1)S(1)}, u32[]{:S(2)}, u32[]{:S(2)}) collective-permute-start(bf16[896,256]{1,0:T(8,128)(2,1)S(1)} %slice_bitcast_fusion.2), channel_id=1, source_target_pairs={{4,0},{0,4},{5,1},{1,5},{6,2},{2,6},{7,3},{3,7},{12,8},{8,12},{13,... | collective-permute-start | bytes 1376264 | tf_op jit(solution)/shard_map/ppermute | solution.py:245
  4.1 6.1 %shard_map.82 = (bf16[128,6144]{1,0:T(8,128)(2,1)}, bf16[128,6144]{1,0:T(8,128)(2,1)S(1)}, bf16[4,64,1152]{2,1,0:T(8,128)(2,1)}) custom-call(bf16[8192,256]{1,0:T(8,128)(2,1)} %bitcast.23, bf16[8192,256]{1,0:T(8,128)(2,1)} %bitcast.24), custom_call_target="tpu_custom_call" | custom-call | bytes 30000 | tf_op jit(solution)/shard_map/pallas_call | solution.py:60
  10.1 0.0 collective-permute-start.1
  10.2 1.8 %slice_bitcast_fusion.mid = bf16[1152,384]{1,0:T(8,128)(2,1)S(1)} fusion(bf16[1,8192,384]{2,1,0:T(8,128)(2,1)} %param.9), kind=kLoop, calls=%fused_computation | loop fusion | bytes 1769472 | tf_op jit(solution)/shard_map/slice | solution.py:296
  12.0 3.4 %collective-permute-done.low = bf16[896,256]{1,0:T(8,128)(2,1)S(1)} collective-permute-done((bf16[896,256]{1,0:T(8,128)(2,1)S(1)}, bf16[896,256]{1,0:T(8,128)(2,1)S(1)}, u32[]{:S(2)}, u32[]{:S(2)}) %collective-permute-start) | collective-permute-done | bytes 458784 | tf_op jit(solution)/shard_map/ppermute | solution.py:245
  15.4 0.0 copy-done.9
  15.4 0.8 copy-done.1
  16.2 4.1 %collective-permute-start.6 = (bf16[1152,384]{1,0:T(8,128)(2,1)S(1)}, bf16[1152,384]{1,0:T(8,128)(2,1)S(1)}, u32[]{:S(2)}, u32[]{:S(2)}) collective-permute-start(bf16[1152,384]{1,0:T(8,128)(2,1)S(1)} %slice_bitcast_fusion.mid), channel_id=1, source_target_pairs={{0,1},{1,2},{2,3},{4,5},{5,6},{6,7},{8,9},{9,10},{10,11},{12,13},{... | collective-permute-start | bytes 2654216 | tf_op jit(solution)/shard_map/ppermute | solution.py:288
  20.3 1.3 %collective-permute-start.7 = (bf16[1152,384]{1,0:T(8,128)(2,1)S(1)}, bf16[1152,384]{1,0:T(8,128)(2,1)}, u32[]{:S(2)}, u32[]{:S(2)}) collective-permute-start(bf16[1152,384]{1,0:T(8,128)(2,1)S(1)} %slice_bitcast_fusion.mid), channel_id=1, source_target_pairs={{1,0},{2,1},{3,2},{5,4},{6,5},{7,6},{9,8},{10,9},{11,10},{13,12},{... | collective-permute-start | bytes 2654216 | tf_op jit(solution)/shard_map/ppermute | solution.py:289
  21.6 6.8 %all-to-all-start = ((bf16[4,64,1152]{2,1,0:T(8,128)(2,1)}), bf16[4,64,1152]{2,1,0:T(8,128)(2,1)}, u32[]{:S(2)}, u32[]{:S(2)}) async-start(bf16[4,64,1152]{2,1,0:T(8,128)(2,1)} %get-tuple-element.37), calls=%async_computation | async-start | bytes 1179648 | tf_op jit(solution)/shard_map/all_to_all | solution.py:298
  28.4 1.5 %collective-permute-start.3 = (bf16[128,6144]{1,0:T(8,128)(2,1)}, bf16[128,6144]{1,0:T(8,128)(2,1)S(1)}, u32[]{:S(2)}, u32[]{:S(2)}) collective-permute-start(bf16[128,6144]{1,0:T(8,128)(2,1)} %copy-done.9), channel_id=1, source_target_pairs={{4,0},{0,4},{5,1},{1,5},{6,2},{2,6},{7,3},{3,7},{12,8},{8,12},{13,... | collective-permute-start | bytes 4718600 | tf_op jit(solution)/shard_map/ppermute | solution.py:245
  29.9 2.0 %slice_bitcast_fusion.1.up = bf16[896,384]{1,0:T(8,128)(2,1)} fusion(bf16[1,8192,384]{2,1,0:T(8,128)(2,1)} %param.9), kind=kLoop, calls=%fused_computation.1 | loop fusion | bytes 1376256 | tf_op jit(solution)/shard_map/slice | solution.py:301
  32.0 2.2 %copy-done = bf16[1,8192,256]{2,1,0:T(8,128)(2,1)S(1)} copy-done((bf16[1,8192,256]{2,1,0:T(8,128)(2,1)S(1)}, bf16[1,8192,256]{2,1,0:T(8,128)(2,1)}, u32[]{:S(2)}) %copy-start) | copy-done | bytes 4194328
  34.2 5.4 %shard_map.83 = (f32[128,384]{1,0:T(8,128)S(1)}, f32[128,384]{1,0:T(8,128)S(1)}) custom-call(bf16[8192,256]{1,0:T(8,128)(2,1)S(1)} %bitcast.25, bf16[8192,384]{1,0:T(8,128)(2,1)} %bitcast.26), custom_call_target="tpu_custom_call" | custom-call | bytes 30000 | tf_op jit(solution)/shard_map/pallas_call | solution.py:105
  39.5 0.0 copy-done.2
  39.6 0.0 copy-start.5
  39.6 1.6 %shard_map.84 = (f32[128,384]{1,0:T(8,128)S(1)}, f32[128,384]{1,0:T(8,128)S(1)}) custom-call(bf16[896,256]{1,0:T(8,128)(2,1)S(1)} %copy-done.2, bf16[896,384]{1,0:T(8,128)(2,1)} %slice_bitcast_fusion.1.up), custom_call_target="tpu_custom_call" | custom-call | bytes 30000 | tf_op jit(solution)/shard_map/pallas_call | solution.py:105
  41.2 0.0 copy-start.3
  41.2 0.7 copy-done.3
  41.9 0.7 copy-done.7
  42.5 0.0 collective-permute-done.6.refs_0_
  42.6 2.9 %collective-permute-done.7.refs_3_ = bf16[1152,384]{1,0:T(8,128)(2,1)} collective-permute-done((bf16[1152,384]{1,0:T(8,128)(2,1)S(1)}, bf16[1152,384]{1,0:T(8,128)(2,1)}, u32[]{:S(2)}, u32[]{:S(2)}) %collective-permute-start.7) | collective-permute-done | bytes 884768 | tf_op jit(solution)/shard_map/ppermute | solution.py:289
  45.5 1.6 %collective-permute-start.8 = (bf16[1152,384]{1,0:T(8,128)(2,1)S(1)}, bf16[1152,384]{1,0:T(8,128)(2,1)}, u32[]{:S(2)}, u32[]{:S(2)}) collective-permute-start(bf16[1152,384]{1,0:T(8,128)(2,1)S(1)} %collective-permute-done.6.refs_0_), channel_id=1, source_target_pairs={{1,2},{2,3},{5,6},{6,7},{9,10},{10,11},{13,14},{14,15},{17,18},{18... | collective-permute-start | bytes 2654216 | tf_op jit(solution)/shard_map/ppermute | solution.py:288
  47.1 1.3 %collective-permute-start.10 = (bf16[1152,384]{1,0:T(8,128)(2,1)}, bf16[1152,384]{1,0:T(8,128)(2,1)}, u32[]{:S(2)}, u32[]{:S(2)}) collective-permute-start(bf16[1152,384]{1,0:T(8,128)(2,1)} %collective-permute-done.7.refs_3_), channel_id=1, source_target_pairs={{1,0},{2,1},{5,4},{6,5},{9,8},{10,9},{13,12},{14,13},{17,16},{18,1... | collective-permute-start | bytes 2654216 | tf_op jit(solution)/shard_map/ppermute | solution.py:289
  48.4 2.4 %shard_map.85.up = bf16[6144,384]{1,0:T(8,128)(2,1)S(1)} custom-call(bf16[8192,384]{1,0:T(8,128)(2,1)} %bitcast.27), custom_call_target="tpu_custom_call" | custom-call | bytes 30000 | tf_op jit(solution)/shard_map/pallas_call | solution.py:129
  50.8 0.0 collective-permute-done.1.refs_1_
  50.8 2.4 %shard_map.86 = (f32[2,64,384]{2,1,0:T(8,128)S(1)}, f32[2,64,384]{2,1,0:T(8,128)S(1)}) custom-call(s32[1]{0:T(128)} %bitcast.me_at, s32[1]{0:T(128)} %bitcast.1.core_at, f32[128,384]{1,0:T(8,128)S(1)} %copy-done.6, bf16[6144,384]{1,0:T(8,128)(2,1)S(1)} %shard_map.85.up, f32[128,384]{1,0:T(8,128)S(1)} %copy-done.8, ...), custom_call_target="tpu_custom_call" | custom-call | bytes 30000 | tf_op jit(solution)/shard_map/pallas_call | solution.py:184
  53.2 0.1 collective-permute-start.2
  53.3 1.4 %collective-permute-done.2 = f32[2,64,384]{2,1,0:T(8,128)S(1)} collective-permute-done((f32[2,64,384]{2,1,0:T(8,128)S(1)}, f32[2,64,384]{2,1,0:T(8,128)S(1)}, u32[]{:S(2)}, u32[]{:S(2)}) %collective-permute-start.2) | collective-permute-done | bytes 196640 | tf_op jit(solution)/shard_map/ppermute | solution.py:312
  54.7 0.7 add.75
  55.4 3.1 %all-to-all-done = bf16[4,64,1152]{2,1,0:T(8,128)(2,1)} async-done(((bf16[4,64,1152]{2,1,0:T(8,128)(2,1)}), bf16[4,64,1152]{2,1,0:T(8,128)(2,1)}, u32[]{:S(2)}, u32[]{:S(2)}) %all-to-all-start) | async-done | bytes 589856 | tf_op jit(solution)/shard_map/all_to_all | solution.py:298
  58.5 8.6 %all-to-all-start.1 = ((f32[8,16,384]{2,1,0:T(8,128)}), f32[8,16,384]{2,1,0:T(8,128)}, u32[]{:S(2)}, u32[]{:S(2)}) async-start(f32[8,16,384]{2,1,0:T(8,128)} %bitcast.29), calls=%async_computation.1 | async-start | bytes 393216 | tf_op jit(solution)/shard_map/all_to_all | solution.py:315
  67.1 0.0 collective-permute-done.8.refs_1_
  67.1 1.6 %collective-permute-start.9 = (bf16[1152,384]{1,0:T(8,128)(2,1)}, bf16[1152,384]{1,0:T(8,128)(2,1)}, u32[]{:S(2)}, u32[]{:S(2)}) collective-permute-start(bf16[1152,384]{1,0:T(8,128)(2,1)} %collective-permute-done.8.refs_1_), channel_id=1, source_target_pairs={{2,3},{6,7},{10,11},{14,15},{18,19},{22,23},{26,27},{30,31}} | collective-permute-start | bytes 2654216 | tf_op jit(solution)/shard_map/ppermute | solution.py:288
  68.7 1.2 %collective-permute-done.10.refs_4_ = bf16[1152,384]{1,0:T(8,128)(2,1)} collective-permute-done((bf16[1152,384]{1,0:T(8,128)(2,1)}, bf16[1152,384]{1,0:T(8,128)(2,1)}, u32[]{:S(2)}, u32[]{:S(2)}) %collective-permute-start.10) | collective-permute-done | bytes 884768 | tf_op jit(solution)/shard_map/ppermute | solution.py:289
  69.8 1.3 %collective-permute-start.11 = (bf16[1152,384]{1,0:T(8,128)(2,1)}, bf16[1152,384]{1,0:T(8,128)(2,1)}, u32[]{:S(2)}, u32[]{:S(2)}) collective-permute-start(bf16[1152,384]{1,0:T(8,128)(2,1)} %collective-permute-done.10.refs_4_), channel_id=1, source_target_pairs={{1,0},{5,4},{9,8},{13,12},{17,16},{21,20},{25,24},{29,28}} | collective-permute-start | bytes 2654216 | tf_op jit(solution)/shard_map/ppermute | solution.py:289
  71.1 8.1 %all-to-all-done.1 = f32[8,16,384]{2,1,0:T(8,128)} async-done(((f32[8,16,384]{2,1,0:T(8,128)}), f32[8,16,384]{2,1,0:T(8,128)}, u32[]{:S(2)}, u32[]{:S(2)}) %all-to-all-start.1) | async-done | bytes 196640 | tf_op jit(solution)/shard_map/all_to_all | solution.py:315
  79.2 1.5 %collective-permute-start.5 = (bf16[4,64,1152]{2,1,0:T(8,128)(2,1)}, bf16[4,64,1152]{2,1,0:T(8,128)(2,1)}, u32[]{:S(2)}, u32[]{:S(2)}) collective-permute-start(bf16[4,64,1152]{2,1,0:T(8,128)(2,1)} %all-to-all-done), channel_id=1, source_target_pairs={{4,0},{0,4},{5,1},{1,5},{6,2},{2,6},{7,3},{3,7},{12,8},{8,12},{13,... | collective-permute-start | bytes 1769480 | tf_op jit(solution)/shard_map/ppermute | solution.py:245
  80.7 1.5 %reduce_sum.18 = f32[16,384]{1,0:T(8,128)} reduce(f32[8,16,384]{2,1,0:T(8,128)} %all-to-all-done.1, f32[]{:T(128)} %constant.88.clone.1), dimensions={0}, to_apply=%region_0.1 | reduce | flops 43008 | bytes 221188 | tf_op jit(solution)/shard_map/reduce_sum | solution.py:319
  82.3 2.4 %shard_map.87.up = bf16[6144,384]{1,0:T(8,128)(2,1)S(1)} custom-call(bf16[8192,384]{1,0:T(8,128)(2,1)} %bitcast.28), custom_call_target="tpu_custom_call" | custom-call | bytes 30000 | tf_op jit(solution)/shard_map/pallas_call | solution.py:129
  84.7 0.0 copy-start.11
  84.7 0.0 collective-permute-done.3.refs_1_
  84.7 1.5 %shard_map.88 = (f32[2,64,384]{2,1,0:T(8,128)S(1)}, f32[2,64,384]{2,1,0:T(8,128)S(1)}) custom-call(s32[1]{0:T(128)} %bitcast.me_at, s32[1]{0:T(128)} %bitcast.1.core_at, f32[128,384]{1,0:T(8,128)S(1)} %get-tuple-element.39.mine, bf16[6144,384]{1,0:T(8,128)(2,1)S(1)} %shard_map.87.up, f32[128,384]{1,0:T(8,128)S(1)} %copy-done.4, ...), custom_call_target="tpu_custom_call" | custom-call | bytes 30000 | tf_op jit(solution)/shard_map/pallas_call | solution.py:184
  86.2 0.1 collective-permute-start.4
  86.3 0.0 copy-done.11
  86.3 1.4 %collective-permute-done.4 = f32[2,64,384]{2,1,0:T(8,128)S(1)} collective-permute-done((f32[2,64,384]{2,1,0:T(8,128)S(1)}, f32[2,64,384]{2,1,0:T(8,128)S(1)}, u32[]{:S(2)}, u32[]{:S(2)}) %collective-permute-start.4) | collective-permute-done | bytes 196640 | tf_op jit(solution)/shard_map/ppermute | solution.py:312
  87.7 0.7 add.76
  88.4 0.0 copy-start.15
  88.4 4.7 %all-to-all-start.2 = ((f32[8,16,384]{2,1,0:T(8,128)}), f32[8,16,384]{2,1,0:T(8,128)}, u32[]{:S(2)}, u32[]{:S(2)}) async-start(f32[8,16,384]{2,1,0:T(8,128)} %bitcast.7), calls=%async_computation.2 | async-start | bytes 393216 | tf_op jit(solution)/shard_map/all_to_all | solution.py:315
  93.1 1.7 %collective-permute-done.5.low = bf16[4,64,1152]{2,1,0:T(8,128)(2,1)} collective-permute-done((bf16[4,64,1152]{2,1,0:T(8,128)(2,1)}, bf16[4,64,1152]{2,1,0:T(8,128)(2,1)}, u32[]{:S(2)}, u32[]{:S(2)}) %collective-permute-start.5) | collective-permute-done | bytes 589856 | tf_op jit(solution)/shard_map/ppermute | solution.py:245
  94.7 0.0 collective-permute-done.9.refs_2_
  94.7 0.0 collective-permute-done.11.refs_5_
  94.7 2.4 %shard_map.89 = f32[64,384]{1,0:T(8,128)S(1)} custom-call(s32[1]{0:T(128)} %bitcast.8.at, bf16[4,64,1152]{2,1,0:T(8,128)(2,1)} %collective-permute-done.5.low, bf16[1152,384]{1,0:T(8,128)(2,1)S(1)} %slice_bitcast_fusion.mid, bf16[1152,384]{1,0:T(8,128)(2,1)S(1)} %collective-permute-done.6.refs_0_, bf16[1152,384]{1,0:T(8,128)(2,1)} %collective-permute-done.8.refs_1_, ...), custom_call_target="tpu_custom_call" | custom-call | bytes 30000 | tf_op jit(solution)/shard_map/pallas_call | solution.py:224
  97.2 0.1 collective-permute-start.14
  97.3 1.8 %collective-permute-start.13 = (f32[32,384]{1,0:T(8,128)S(1)}, f32[32,384]{1,0:T(8,128)S(1)}, u32[]{:S(2)}, u32[]{:S(2)}) collective-permute-start(f32[32,384]{1,0:T(8,128)S(1)} %get-tuple-element.52), channel_id=1, source_target_pairs={{0,16},{8,24},{16,0},{24,8},{1,17},{9,25},{17,1},{25,9},{2,18},{10... | collective-permute-start | bytes 147464 | tf_op jit(solution)/shard_map/ppermute | solution.py:341
  99.1 0.2 collective-permute-start.12
  99.3 0.0 copy-done.16
  99.3 2.7 %all-to-all-done.2 = f32[8,16,384]{2,1,0:T(8,128)} async-done(((f32[8,16,384]{2,1,0:T(8,128)}), f32[8,16,384]{2,1,0:T(8,128)}, u32[]{:S(2)}, u32[]{:S(2)}) %all-to-all-start.2) | async-done | bytes 196640 | tf_op jit(solution)/shard_map/all_to_all | solution.py:315
  102.0 0.9 reduce_sum.19
  103.0 0.0 collective-permute-done.14
  103.0 0.0 collective-permute-done.13
  103.0 0.0 collective-permute-done.12
  103.0 0.7 fusion.2
  (27 shorter events, 0.1 us)
Async XLA Ops:
  1.1 14.4 %collective-permute-start = (bf16[896,256]{1,0:T(8,128)(2,1)S(1)}, bf16[896,256]{1,0:T(8,128)(2,1)S(1)}, u32[]{:S(2)}, u32[]{:S(2)}) collective-permute-start(bf16[896,256]{1,0:T(8,128)(2,1)S(1)} %slice_bitcast_fusion.2), channel_id=1, source_target_pairs={{4,0},{0,4},{5,1},{1,5},{6,2},{2,6},{7,3},{3,7},{12,8},{8,12},{13,... | collective-permute-start | bytes 1376264 | tf_op jit(solution)/shard_map/ppermute | solution.py:245
  10.1 5.3 %copy-start.9 = (bf16[128,6144]{1,0:T(8,128)(2,1)}, bf16[128,6144]{1,0:T(8,128)(2,1)S(1)}, u32[]{:S(2)}) copy-start(bf16[128,6144]{1,0:T(8,128)(2,1)S(1)} %get-tuple-element.42) | copy-start | bytes 4718596
  10.1 40.7 %collective-permute-start.1 = (bf16[128,6144]{1,0:T(8,128)(2,1)}, bf16[128,6144]{1,0:T(8,128)(2,1)}, u32[]{:S(2)}, u32[]{:S(2)}) collective-permute-start(bf16[128,6144]{1,0:T(8,128)(2,1)} %get-tuple-element.29), channel_id=1, source_target_pairs={{4,0},{0,4},{5,1},{1,5},{6,2},{2,6},{7,3},{3,7},{12,8},{8,12},{13,... | collective-permute-start | bytes 4718600 | tf_op jit(solution)/shard_map/ppermute | solution.py:245
  15.4 0.8 copy-start.1
  16.2 26.4 %collective-permute-start.6 = (bf16[1152,384]{1,0:T(8,128)(2,1)S(1)}, bf16[1152,384]{1,0:T(8,128)(2,1)S(1)}, u32[]{:S(2)}, u32[]{:S(2)}) collective-permute-start(bf16[1152,384]{1,0:T(8,128)(2,1)S(1)} %slice_bitcast_fusion.mid), channel_id=1, source_target_pairs={{0,1},{1,2},{2,3},{4,5},{5,6},{6,7},{8,9},{9,10},{10,11},{12,13},{... | collective-permute-start | bytes 2654216 | tf_op jit(solution)/shard_map/ppermute | solution.py:288
  20.3 25.2 %collective-permute-start.7 = (bf16[1152,384]{1,0:T(8,128)(2,1)S(1)}, bf16[1152,384]{1,0:T(8,128)(2,1)}, u32[]{:S(2)}, u32[]{:S(2)}) collective-permute-start(bf16[1152,384]{1,0:T(8,128)(2,1)S(1)} %slice_bitcast_fusion.mid), channel_id=1, source_target_pairs={{1,0},{2,1},{3,2},{5,4},{6,5},{7,6},{9,8},{10,9},{11,10},{13,12},{... | collective-permute-start | bytes 2654216 | tf_op jit(solution)/shard_map/ppermute | solution.py:289
  21.6 36.9 %all-to-all-start = ((bf16[4,64,1152]{2,1,0:T(8,128)(2,1)}), bf16[4,64,1152]{2,1,0:T(8,128)(2,1)}, u32[]{:S(2)}, u32[]{:S(2)}) async-start(bf16[4,64,1152]{2,1,0:T(8,128)(2,1)} %get-tuple-element.37), calls=%async_computation | async-start | bytes 1179648 | tf_op jit(solution)/shard_map/all_to_all | solution.py:298
  28.4 56.2 %collective-permute-start.3 = (bf16[128,6144]{1,0:T(8,128)(2,1)}, bf16[128,6144]{1,0:T(8,128)(2,1)S(1)}, u32[]{:S(2)}, u32[]{:S(2)}) collective-permute-start(bf16[128,6144]{1,0:T(8,128)(2,1)} %copy-done.9), channel_id=1, source_target_pairs={{4,0},{0,4},{5,1},{1,5},{6,2},{2,6},{7,3},{3,7},{12,8},{8,12},{13,... | collective-permute-start | bytes 4718600 | tf_op jit(solution)/shard_map/ppermute | solution.py:245
  32.0 2.2 %copy-start = (bf16[1,8192,256]{2,1,0:T(8,128)(2,1)S(1)}, bf16[1,8192,256]{2,1,0:T(8,128)(2,1)}, u32[]{:S(2)}) copy-start(bf16[1,8192,256]{2,1,0:T(8,128)(2,1)} %param.8) | copy-start | bytes 12582916
  34.1 5.4 %copy-start.2 = (bf16[896,256]{1,0:T(8,128)(2,1)S(1)}, bf16[896,256]{1,0:T(8,128)(2,1)}, u32[]{:S(2)}) copy-start(bf16[896,256]{1,0:T(8,128)(2,1)} %copy-done.1) | copy-start | bytes 1376260
  39.6 5.9 %copy-start.5 = (f32[128,384]{1,0:T(8,128)}, f32[128,384]{1,0:T(8,128)S(1)}, u32[]{:S(2)}) copy-start(f32[128,384]{1,0:T(8,128)S(1)} %get-tuple-element.31.mine) | copy-start | bytes 589828
  41.2 0.7 copy-start.3
  41.9 0.7 copy-start.7
  45.5 21.6 %collective-permute-start.8 = (bf16[1152,384]{1,0:T(8,128)(2,1)S(1)}, bf16[1152,384]{1,0:T(8,128)(2,1)}, u32[]{:S(2)}, u32[]{:S(2)}) collective-permute-start(bf16[1152,384]{1,0:T(8,128)(2,1)S(1)} %collective-permute-done.6.refs_0_), channel_id=1, source_target_pairs={{1,2},{2,3},{5,6},{6,7},{9,10},{10,11},{13,14},{14,15},{17,18},{18... | collective-permute-start | bytes 2654216 | tf_op jit(solution)/shard_map/ppermute | solution.py:288
  47.1 22.8 %collective-permute-start.10 = (bf16[1152,384]{1,0:T(8,128)(2,1)}, bf16[1152,384]{1,0:T(8,128)(2,1)}, u32[]{:S(2)}, u32[]{:S(2)}) collective-permute-start(bf16[1152,384]{1,0:T(8,128)(2,1)} %collective-permute-done.7.refs_3_), channel_id=1, source_target_pairs={{1,0},{2,1},{5,4},{6,5},{9,8},{10,9},{13,12},{14,13},{17,16},{18,1... | collective-permute-start | bytes 2654216 | tf_op jit(solution)/shard_map/ppermute | solution.py:289
  48.4 2.4 %copy-start.6 = (f32[128,384]{1,0:T(8,128)S(1)}, f32[128,384]{1,0:T(8,128)}, u32[]{:S(2)}) copy-start(f32[128,384]{1,0:T(8,128)} %copy-done.5) | copy-start | bytes 589828
  48.4 2.4 %copy-start.8 = (f32[128,384]{1,0:T(8,128)S(1)}, f32[128,384]{1,0:T(8,128)}, u32[]{:S(2)}) copy-start(f32[128,384]{1,0:T(8,128)} %copy-done.7) | copy-start | bytes 589828
  53.2 1.5 %collective-permute-start.2 = (f32[2,64,384]{2,1,0:T(8,128)S(1)}, f32[2,64,384]{2,1,0:T(8,128)S(1)}, u32[]{:S(2)}, u32[]{:S(2)}) collective-permute-start(f32[2,64,384]{2,1,0:T(8,128)S(1)} %get-tuple-element.36), channel_id=1, source_target_pairs={{0,8},{8,0},{16,24},{24,16},{1,9},{9,1},{17,25},{25,17},{2,10},{10... | collective-permute-start | bytes 589832 | tf_op jit(solution)/shard_map/ppermute | solution.py:312
  58.5 20.7 %all-to-all-start.1 = ((f32[8,16,384]{2,1,0:T(8,128)}), f32[8,16,384]{2,1,0:T(8,128)}, u32[]{:S(2)}, u32[]{:S(2)}) async-start(f32[8,16,384]{2,1,0:T(8,128)} %bitcast.29), calls=%async_computation.1 | async-start | bytes 393216 | tf_op jit(solution)/shard_map/all_to_all | solution.py:315
  67.1 27.7 %collective-permute-start.9 = (bf16[1152,384]{1,0:T(8,128)(2,1)}, bf16[1152,384]{1,0:T(8,128)(2,1)}, u32[]{:S(2)}, u32[]{:S(2)}) collective-permute-start(bf16[1152,384]{1,0:T(8,128)(2,1)} %collective-permute-done.8.refs_1_), channel_id=1, source_target_pairs={{2,3},{6,7},{10,11},{14,15},{18,19},{22,23},{26,27},{30,31}} | collective-permute-start | bytes 2654216 | tf_op jit(solution)/shard_map/ppermute | solution.py:288
  69.8 24.9 %collective-permute-start.11 = (bf16[1152,384]{1,0:T(8,128)(2,1)}, bf16[1152,384]{1,0:T(8,128)(2,1)}, u32[]{:S(2)}, u32[]{:S(2)}) collective-permute-start(bf16[1152,384]{1,0:T(8,128)(2,1)} %collective-permute-done.10.refs_4_), channel_id=1, source_target_pairs={{1,0},{5,4},{9,8},{13,12},{17,16},{21,20},{25,24},{29,28}} | collective-permute-start | bytes 2654216 | tf_op jit(solution)/shard_map/ppermute | solution.py:289
  79.2 15.5 %collective-permute-start.5 = (bf16[4,64,1152]{2,1,0:T(8,128)(2,1)}, bf16[4,64,1152]{2,1,0:T(8,128)(2,1)}, u32[]{:S(2)}, u32[]{:S(2)}) collective-permute-start(bf16[4,64,1152]{2,1,0:T(8,128)(2,1)} %all-to-all-done), channel_id=1, source_target_pairs={{4,0},{0,4},{5,1},{1,5},{6,2},{2,6},{7,3},{3,7},{12,8},{8,12},{13,... | collective-permute-start | bytes 1769480 | tf_op jit(solution)/shard_map/ppermute | solution.py:245
  82.3 2.4 %copy-start.4 = (f32[128,384]{1,0:T(8,128)S(1)}, f32[128,384]{1,0:T(8,128)}, u32[]{:S(2)}) copy-start(f32[128,384]{1,0:T(8,128)} %copy-done.3) | copy-start | bytes 589828
  84.7 1.6 %copy-start.11 = (s32[384]{0:T(512)S(1)}, s32[384]{0:T(512)}, u32[]{:S(2)}) copy-start(s32[384]{0:T(512)} %param.15) | copy-start | bytes 4612
  86.2 1.5 %collective-permute-start.4 = (f32[2,64,384]{2,1,0:T(8,128)S(1)}, f32[2,64,384]{2,1,0:T(8,128)S(1)}, u32[]{:S(2)}, u32[]{:S(2)}) collective-permute-start(f32[2,64,384]{2,1,0:T(8,128)S(1)} %get-tuple-element.44), channel_id=1, source_target_pairs={{0,8},{8,0},{16,24},{24,16},{1,9},{9,1},{17,25},{25,17},{2,10},{10... | collective-permute-start | bytes 589832 | tf_op jit(solution)/shard_map/ppermute | solution.py:312
  87.7 11.6 %copy-start.16 = (s32[32]{0:T(128)S(1)}, s32[32]{0:T(128)}, u32[]{:S(2)}) copy-start(s32[32]{0:T(128)} %param.12) | copy-start | bytes 388
  88.4 14.6 %copy-start.10 = (f32[16,384]{1,0:T(8,128)S(1)}, f32[16,384]{1,0:T(8,128)}, u32[]{:S(2)}) copy-start(f32[16,384]{1,0:T(8,128)} %reduce_sum.18) | copy-start | bytes 73732
  88.4 14.6 %copy-start.12 = (f32[384]{0:T(512)S(1)}, f32[384]{0:T(512)}, u32[]{:S(2)}) copy-start(f32[384]{0:T(512)} %param.11) | copy-start | bytes 4612
  88.4 14.6 %copy-start.13 = (s32[384]{0:T(512)S(1)}, s32[384]{0:T(512)}, u32[]{:S(2)}) copy-start(s32[384]{0:T(512)} %param.13) | copy-start | bytes 4612
  88.4 14.6 %copy-start.14 = (f32[32]{0:T(128)S(1)}, f32[32]{0:T(128)}, u32[]{:S(2)}) copy-start(f32[32]{0:T(128)} %param.10) | copy-start | bytes 388
  88.4 14.6 %copy-start.15 = (s32[32]{0:T(128)S(1)}, s32[32]{0:T(128)}, u32[]{:S(2)}) copy-start(s32[32]{0:T(128)} %param.14) | copy-start | bytes 388
  88.4 13.6 %all-to-all-start.2 = ((f32[8,16,384]{2,1,0:T(8,128)}), f32[8,16,384]{2,1,0:T(8,128)}, u32[]{:S(2)}, u32[]{:S(2)}) async-start(f32[8,16,384]{2,1,0:T(8,128)} %bitcast.7), calls=%async_computation.2 | async-start | bytes 393216 | tf_op jit(solution)/shard_map/all_to_all | solution.py:315
  97.2 5.8 %collective-permute-start.14 = (f32[32,384]{1,0:T(8,128)S(1)}, f32[32,384]{1,0:T(8,128)S(1)}, u32[]{:S(2)}, u32[]{:S(2)}) collective-permute-start(f32[32,384]{1,0:T(8,128)S(1)} %dynamic-slice_bitcast_fusion), channel_id=1, source_target_pairs={{0,8},{8,0},{16,24},{24,16},{1,9},{9,1},{17,25},{25,17},{2,10},{10... | collective-permute-start | bytes 147464 | tf_op jit(solution)/shard_map/ppermute | solution.py:341
  97.3 5.7 %collective-permute-start.13 = (f32[32,384]{1,0:T(8,128)S(1)}, f32[32,384]{1,0:T(8,128)S(1)}, u32[]{:S(2)}, u32[]{:S(2)}) collective-permute-start(f32[32,384]{1,0:T(8,128)S(1)} %get-tuple-element.52), channel_id=1, source_target_pairs={{0,16},{8,24},{16,0},{24,8},{1,17},{9,25},{17,1},{25,9},{2,18},{10... | collective-permute-start | bytes 147464 | tf_op jit(solution)/shard_map/ppermute | solution.py:341
  99.1 3.9 %collective-permute-start.12 = (f32[32,384]{1,0:T(8,128)S(1)}, f32[32,384]{1,0:T(8,128)S(1)}, u32[]{:S(2)}, u32[]{:S(2)}) collective-permute-start(f32[32,384]{1,0:T(8,128)S(1)} %get-tuple-element.51), channel_id=1, source_target_pairs={{0,24},{8,16},{16,8},{24,0},{1,25},{9,17},{17,9},{25,1},{2,26},{10... | collective-permute-start | bytes 147464 | tf_op jit(solution)/shard_map/ppermute | solution.py:341

commit v7 on v6

--- a/solution.py
+++ b/solution.py
@@ -13,8 +13,8 @@
     return pltpu.CompilerParams(vmem_limit_bytes=VMEM_LIMIT)
 
 
-def cost(microseconds):
-    return pl.CostEstimate(flops=0, bytes_accessed=int(microseconds * 3.0e6), transcendentals=0)
+def cost():
+    return pl.CostEstimate(flops=0, bytes_accessed=30000, transcendentals=0)
 
 
 def dot(a, b):
@@ -68,7 +68,7 @@
         out_shape=[jax.ShapeDtypeStruct((cols // parts, n_main), kind)] * parts
         + [jax.ShapeDtypeStruct(tail_shape, kind)],
         compiler_params=params(),
-        cost_estimate=cost(0.01),
+        cost_estimate=cost(),
     )(in_hbm(lower_rows), in_hbm(lower_rows))
 
 
@@ -114,7 +114,7 @@
         out_shape=[jax.ShapeDtypeStruct(shape, jnp.float32)] * parts,
         scratch_shapes=[pltpu.VMEM((states, width), jnp.float32)],
         compiler_params=params(),
-        cost_estimate=cost(0.01),
+        cost_estimate=cost(),
     )(got, in_hbm(upper_rows), *so_far)
 
 
@@ -133,7 +133,7 @@
         out_shape=pltpu.VMEM((k, width), rows.dtype),
         scratch_shapes=[pltpu.SemaphoreType.DMA],
         compiler_params=params(),
-        cost_estimate=cost(0.01),
+        cost_estimate=cost(),
     )(in_hbm(rows))
 
 
@@ -141,7 +141,7 @@
     n_up = 1 + len(got)
     states, k = got[0].shape
     width = rows.shape[1]
-    steps = 3
+    steps = 1
     block = k // steps
     share = states // n_core
 
@@ -191,7 +191,7 @@
             pltpu.SemaphoreType.DMA((n_up - 1, steps)),
         ],
         compiler_params=params(),
-        cost_estimate=cost(0.01),
+        cost_estimate=cost(),
     )(me.reshape(1), core.reshape(1), own, in_vmem(rows), *so_far, *got)
 
 
@@ -232,7 +232,7 @@
             pltpu.SemaphoreType.DMA((n_dep + 1,)),
         ],
         compiler_params=params(),
-        cost_estimate=cost(0.01),
+        cost_estimate=cost(),
     )(depth.reshape(1), got, own, *forward, *backward)
 
 
@@ -316,11 +316,10 @@
 
         held_a = held_rows(after(upper_rows, *so_far[0]), rows - n_main, n_main)
         sent_a, from_a = reduced(0, crossed[1], held_a, sorted_tail)
-        sum_a = jnp.sum(from_a, axis=0)
-        held_b = held_rows(after(upper_rows, sum_a), rows - n_main, n_main)
+        held_b = held_rows(after(upper_rows, sent_a), rows - n_main, n_main)
         cross(sorted_tail, from_a)
-        last, from_b = reduced(1, crossed[2], held_b, sum_a)
-        sum_b = jnp.sum(from_b, axis=0)
+        last, from_b = reduced(1, crossed[2], held_b, from_a)
+        sum_a, sum_b = jnp.sum(from_a, axis=0), jnp.sum(from_b, axis=0)
         main = jnp.concatenate([sum_a, sum_b], axis=0)
 
         terms = [tail_product(depth, after(g, last), up_tail, forward, backward) for g in crossed[3]]

time: 105 us -> 105 us (level)
  starting transfers between devices: 39.4 us -> 41.1 us
    all_to_all x2, starting transfers between devices: 13.2 us -> 14.9 us  [reduced(): lax.all_to_all(by_owner, OWNERS, 0, 0, axis_index_groups=same_core)]
    all_to_all x2, waiting for transfers between devices: 10.8 us -> 9.58 us  [reduced(): lax.all_to_all(by_owner, OWNERS, 0, 0, axis_index_groups=same_core)]
    unnamed x34 -> x32, local copies, waits for them, and re-layouts: 4.38 us -> 4.37 us
  transfers between devices with their start and end apart: 18 -> 18, of which waited for: 9 -> 10; matrix products, arithmetic and copies ran while one was open for 8% -> 7% of each run, Pallas kernels for 23% -> 23%
where the time goes in v7:
time: 105 us; the launch traced here: 104 us
  starting transfers between devices  41.1 us (39%)
  waiting for transfers between devices  25 us (24%)
  Pallas kernels  23.8 us (23%)
  local copies, waits for them, and re-layouts  9.28 us (9%)
  other arithmetic  4.08 us (4%)
    all_to_all x2, starting transfers between devices, reduced(): lax.all_to_all(by_owner, OWNERS, 0, 0, axis_index_groups=same_core)  14.9 us
    all_to_all x2, waiting for transfers between devices, reduced(): lax.all_to_all(by_owner, OWNERS, 0, 0, axis_index_groups=same_core)  9.58 us
    ppermute x3, starting transfers between devices, pass_on(): forward.append(lax.ppermute(held_up, 'depth', up[i:]))  7.25 us
    pallas_call x2, Pallas kernels, rows_product(): pl.pallas_call(body, grid=(steps,), in_specs=[pl.BlockSpec((block, states...  7 us
    all_to_all x1, starting transfers between devices, local(): sorted_tail = lax.all_to_all(tail_rows, 'depth', 0, 0)  6.85 us
    pallas_call x1, Pallas kernels, turn(): pl.pallas_call(body, grid=(steps,), in_specs=[pl.BlockSpec((block, cols),...  6.05 us
    ppermute x4, starting transfers between devices, shifted(): lax.ppermute(x, 'upper', [((u + shift) % n_up, u) for u in range(n_up)])  6.03 us
    ppermute x4, waiting for transfers between devices, shifted(): lax.ppermute(x, 'upper', [((u + shift) % n_up, u) for u in range(n_up)])  5.41 us
  transfers between devices with their start and end apart: 18, of which 10 were waited for; matrix products, arithmetic and copies ran while one was open for 7% of the time, Pallas kernels for 23%

profile of v7, /device:TPU:0, one launch (start us, length us, event | category | flops | bytes accessed | tf_op | source)
XLA Modules:
  0.0 103.6 jit_solution(552133330748134430)
XLA Ops:
  0.0 1.0 %slice_bitcast_fusion.2 = bf16[896,256]{1,0:T(8,128)(2,1)S(1)} fusion(bf16[1,8192,256]{2,1,0:T(8,128)(2,1)} %param.8), kind=kLoop, calls=%fused_computation.2 | loop fusion | bytes 917504 | tf_op jit(solution)/shard_map/slice | solution.py:291
  1.1 3.0 %collective-permute-start = (bf16[896,256]{1,0:T(8,128)(2,1)S(1)}, bf16[896,256]{1,0:T(8,128)(2,1)S(1)}, u32[]{:S(2)}, u32[]{:S(2)}) collective-permute-start(bf16[896,256]{1,0:T(8,128)(2,1)S(1)} %slice_bitcast_fusion.2), channel_id=1, source_target_pairs={{4,0},{0,4},{5,1},{1,5},{6,2},{2,6},{7,3},{3,7},{12,8},{8,12},{13,... | collective-permute-start | bytes 1376264 | tf_op jit(solution)/shard_map/ppermute | solution.py:245
  4.1 6.0 %shard_map.82 = (bf16[128,6144]{1,0:T(8,128)(2,1)}, bf16[128,6144]{1,0:T(8,128)(2,1)S(1)}, bf16[4,64,1152]{2,1,0:T(8,128)(2,1)}) custom-call(bf16[8192,256]{1,0:T(8,128)(2,1)} %bitcast.23, bf16[8192,256]{1,0:T(8,128)(2,1)} %bitcast.24), custom_call_target="tpu_custom_call" | custom-call | bytes 30000 | tf_op jit(solution)/shard_map/pallas_call | solution.py:60
  10.1 0.0 collective-permute-start.1
  10.1 1.8 %slice_bitcast_fusion.mid = bf16[1152,384]{1,0:T(8,128)(2,1)S(1)} fusion(bf16[1,8192,384]{2,1,0:T(8,128)(2,1)} %param.9), kind=kLoop, calls=%fused_computation | loop fusion | bytes 1769472 | tf_op jit(solution)/shard_map/slice | solution.py:296
  12.0 3.5 %collective-permute-done.low = bf16[896,256]{1,0:T(8,128)(2,1)S(1)} collective-permute-done((bf16[896,256]{1,0:T(8,128)(2,1)S(1)}, bf16[896,256]{1,0:T(8,128)(2,1)S(1)}, u32[]{:S(2)}, u32[]{:S(2)}) %collective-permute-start) | collective-permute-done | bytes 458784 | tf_op jit(solution)/shard_map/ppermute | solution.py:245
  15.4 0.0 copy-done.9
  15.4 0.8 copy-done.1
  16.2 4.1 %collective-permute-start.6 = (bf16[1152,384]{1,0:T(8,128)(2,1)S(1)}, bf16[1152,384]{1,0:T(8,128)(2,1)S(1)}, u32[]{:S(2)}, u32[]{:S(2)}) collective-permute-start(bf16[1152,384]{1,0:T(8,128)(2,1)S(1)} %slice_bitcast_fusion.mid), channel_id=1, source_target_pairs={{0,1},{1,2},{2,3},{4,5},{5,6},{6,7},{8,9},{9,10},{10,11},{12,13},{... | collective-permute-start | bytes 2654216 | tf_op jit(solution)/shard_map/ppermute | solution.py:288
  20.3 1.3 %collective-permute-start.7 = (bf16[1152,384]{1,0:T(8,128)(2,1)S(1)}, bf16[1152,384]{1,0:T(8,128)(2,1)}, u32[]{:S(2)}, u32[]{:S(2)}) collective-permute-start(bf16[1152,384]{1,0:T(8,128)(2,1)S(1)} %slice_bitcast_fusion.mid), channel_id=1, source_target_pairs={{1,0},{2,1},{3,2},{5,4},{6,5},{7,6},{9,8},{10,9},{11,10},{13,12},{... | collective-permute-start | bytes 2654216 | tf_op jit(solution)/shard_map/ppermute | solution.py:289
  21.6 6.8 %all-to-all-start = ((bf16[4,64,1152]{2,1,0:T(8,128)(2,1)}), bf16[4,64,1152]{2,1,0:T(8,128)(2,1)}, u32[]{:S(2)}, u32[]{:S(2)}) async-start(bf16[4,64,1152]{2,1,0:T(8,128)(2,1)} %get-tuple-element.37), calls=%async_computation | async-start | bytes 1179648 | tf_op jit(solution)/shard_map/all_to_all | solution.py:298
  28.4 1.5 %collective-permute-start.3 = (bf16[128,6144]{1,0:T(8,128)(2,1)}, bf16[128,6144]{1,0:T(8,128)(2,1)S(1)}, u32[]{:S(2)}, u32[]{:S(2)}) collective-permute-start(bf16[128,6144]{1,0:T(8,128)(2,1)} %copy-done.9), channel_id=1, source_target_pairs={{4,0},{0,4},{5,1},{1,5},{6,2},{2,6},{7,3},{3,7},{12,8},{8,12},{13,... | collective-permute-start | bytes 4718600 | tf_op jit(solution)/shard_map/ppermute | solution.py:245
  29.9 2.0 %slice_bitcast_fusion.1.up = bf16[896,384]{1,0:T(8,128)(2,1)} fusion(bf16[1,8192,384]{2,1,0:T(8,128)(2,1)} %param.9), kind=kLoop, calls=%fused_computation.1 | loop fusion | bytes 1376256 | tf_op jit(solution)/shard_map/slice | solution.py:301
  32.0 2.2 %copy-done = bf16[1,8192,256]{2,1,0:T(8,128)(2,1)S(1)} copy-done((bf16[1,8192,256]{2,1,0:T(8,128)(2,1)S(1)}, bf16[1,8192,256]{2,1,0:T(8,128)(2,1)}, u32[]{:S(2)}) %copy-start) | copy-done | bytes 4194328
  34.2 5.4 %shard_map.83 = (f32[128,384]{1,0:T(8,128)S(1)}, f32[128,384]{1,0:T(8,128)S(1)}) custom-call(bf16[8192,256]{1,0:T(8,128)(2,1)S(1)} %bitcast.25, bf16[8192,384]{1,0:T(8,128)(2,1)} %bitcast.26), custom_call_target="tpu_custom_call" | custom-call | bytes 30000 | tf_op jit(solution)/shard_map/pallas_call | solution.py:105
  39.5 0.0 copy-done.2
  39.5 0.0 copy-start.5
  39.6 1.6 %shard_map.84 = (f32[128,384]{1,0:T(8,128)S(1)}, f32[128,384]{1,0:T(8,128)S(1)}) custom-call(bf16[896,256]{1,0:T(8,128)(2,1)S(1)} %copy-done.2, bf16[896,384]{1,0:T(8,128)(2,1)} %slice_bitcast_fusion.1.up), custom_call_target="tpu_custom_call" | custom-call | bytes 30000 | tf_op jit(solution)/shard_map/pallas_call | solution.py:105
  41.2 0.0 copy-start.3
  41.2 0.7 copy-done.3
  41.9 0.7 copy-done.7
  42.6 0.0 collective-permute-done.6.refs_0_
  42.6 2.9 %collective-permute-done.7.refs_3_ = bf16[1152,384]{1,0:T(8,128)(2,1)} collective-permute-done((bf16[1152,384]{1,0:T(8,128)(2,1)S(1)}, bf16[1152,384]{1,0:T(8,128)(2,1)}, u32[]{:S(2)}, u32[]{:S(2)}) %collective-permute-start.7) | collective-permute-done | bytes 884768 | tf_op jit(solution)/shard_map/ppermute | solution.py:289
  45.5 0.0 copy-done.5
  45.5 1.6 %collective-permute-start.8 = (bf16[1152,384]{1,0:T(8,128)(2,1)S(1)}, bf16[1152,384]{1,0:T(8,128)(2,1)}, u32[]{:S(2)}, u32[]{:S(2)}) collective-permute-start(bf16[1152,384]{1,0:T(8,128)(2,1)S(1)} %collective-permute-done.6.refs_0_), channel_id=1, source_target_pairs={{1,2},{2,3},{5,6},{6,7},{9,10},{10,11},{13,14},{14,15},{17,18},{18... | collective-permute-start | bytes 2654216 | tf_op jit(solution)/shard_map/ppermute | solution.py:288
  47.1 1.3 %collective-permute-start.10 = (bf16[1152,384]{1,0:T(8,128)(2,1)}, bf16[1152,384]{1,0:T(8,128)(2,1)}, u32[]{:S(2)}, u32[]{:S(2)}) collective-permute-start(bf16[1152,384]{1,0:T(8,128)(2,1)} %collective-permute-done.7.refs_3_), channel_id=1, source_target_pairs={{1,0},{2,1},{5,4},{6,5},{9,8},{10,9},{13,12},{14,13},{17,16},{18,1... | collective-permute-start | bytes 2654216 | tf_op jit(solution)/shard_map/ppermute | solution.py:289
  48.4 0.0 copy-start.6
  48.4 2.4 %shard_map.85.up = bf16[6144,384]{1,0:T(8,128)(2,1)S(1)} custom-call(bf16[8192,384]{1,0:T(8,128)(2,1)} %bitcast.27), custom_call_target="tpu_custom_call" | custom-call | bytes 30000 | tf_op jit(solution)/shard_map/pallas_call | solution.py:129
  50.8 0.0 collective-permute-done.1.refs_1_
  50.8 2.4 %shard_map.86 = (f32[2,64,384]{2,1,0:T(8,128)S(1)}, f32[2,64,384]{2,1,0:T(8,128)S(1)}) custom-call(s32[1]{0:T(128)} %bitcast.me_at, s32[1]{0:T(128)} %bitcast.1.core_at, f32[128,384]{1,0:T(8,128)S(1)} %copy-done.6, bf16[6144,384]{1,0:T(8,128)(2,1)S(1)} %shard_map.85.up, f32[128,384]{1,0:T(8,128)S(1)} %copy-done.8, ...), custom_call_target="tpu_custom_call" | custom-call | bytes 30000 | tf_op jit(solution)/shard_map/pallas_call | solution.py:184
  53.2 0.1 collective-permute-start.2
  53.3 1.4 %collective-permute-done.2 = f32[2,64,384]{2,1,0:T(8,128)S(1)} collective-permute-done((f32[2,64,384]{2,1,0:T(8,128)S(1)}, f32[2,64,384]{2,1,0:T(8,128)S(1)}, u32[]{:S(2)}, u32[]{:S(2)}) %collective-permute-start.2) | collective-permute-done | bytes 196640 | tf_op jit(solution)/shard_map/ppermute | solution.py:312
  54.8 0.7 add.75
  55.5 3.0 %all-to-all-done = bf16[4,64,1152]{2,1,0:T(8,128)(2,1)} async-done(((bf16[4,64,1152]{2,1,0:T(8,128)(2,1)}), bf16[4,64,1152]{2,1,0:T(8,128)(2,1)}, u32[]{:S(2)}, u32[]{:S(2)}) %all-to-all-start) | async-done | bytes 589856 | tf_op jit(solution)/shard_map/all_to_all | solution.py:298
  58.5 8.7 %all-to-all-start.1 = ((f32[8,16,384]{2,1,0:T(8,128)}), f32[8,16,384]{2,1,0:T(8,128)}, u32[]{:S(2)}, u32[]{:S(2)}) async-start(f32[8,16,384]{2,1,0:T(8,128)} %bitcast.29), calls=%async_computation.1 | async-start | bytes 393216 | tf_op jit(solution)/shard_map/all_to_all | solution.py:315
  67.1 0.0 collective-permute-done.8.refs_1_
  67.1 1.6 %collective-permute-start.9 = (bf16[1152,384]{1,0:T(8,128)(2,1)}, bf16[1152,384]{1,0:T(8,128)(2,1)}, u32[]{:S(2)}, u32[]{:S(2)}) collective-permute-start(bf16[1152,384]{1,0:T(8,128)(2,1)} %collective-permute-done.8.refs_1_), channel_id=1, source_target_pairs={{2,3},{6,7},{10,11},{14,15},{18,19},{22,23},{26,27},{30,31}} | collective-permute-start | bytes 2654216 | tf_op jit(solution)/shard_map/ppermute | solution.py:288
  68.7 1.1 %collective-permute-done.10.refs_4_ = bf16[1152,384]{1,0:T(8,128)(2,1)} collective-permute-done((bf16[1152,384]{1,0:T(8,128)(2,1)}, bf16[1152,384]{1,0:T(8,128)(2,1)}, u32[]{:S(2)}, u32[]{:S(2)}) %collective-permute-start.10) | collective-permute-done | bytes 884768 | tf_op jit(solution)/shard_map/ppermute | solution.py:289
  69.8 1.3 %collective-permute-start.11 = (bf16[1152,384]{1,0:T(8,128)(2,1)}, bf16[1152,384]{1,0:T(8,128)(2,1)}, u32[]{:S(2)}, u32[]{:S(2)}) collective-permute-start(bf16[1152,384]{1,0:T(8,128)(2,1)} %collective-permute-done.10.refs_4_), channel_id=1, source_target_pairs={{1,0},{5,4},{9,8},{13,12},{17,16},{21,20},{25,24},{29,28}} | collective-permute-start | bytes 2654216 | tf_op jit(solution)/shard_map/ppermute | solution.py:289
  71.1 8.1 %all-to-all-done.1 = f32[8,16,384]{2,1,0:T(8,128)} async-done(((f32[8,16,384]{2,1,0:T(8,128)}), f32[8,16,384]{2,1,0:T(8,128)}, u32[]{:S(2)}, u32[]{:S(2)}) %all-to-all-start.1) | async-done | bytes 196640 | tf_op jit(solution)/shard_map/all_to_all | solution.py:315
  79.2 1.5 %collective-permute-start.5 = (bf16[4,64,1152]{2,1,0:T(8,128)(2,1)}, bf16[4,64,1152]{2,1,0:T(8,128)(2,1)}, u32[]{:S(2)}, u32[]{:S(2)}) collective-permute-start(bf16[4,64,1152]{2,1,0:T(8,128)(2,1)} %all-to-all-done), channel_id=1, source_target_pairs={{4,0},{0,4},{5,1},{1,5},{6,2},{2,6},{7,3},{3,7},{12,8},{8,12},{13,... | collective-permute-start | bytes 1769480 | tf_op jit(solution)/shard_map/ppermute | solution.py:245
  80.7 2.4 %shard_map.87.up = bf16[6144,384]{1,0:T(8,128)(2,1)S(1)} custom-call(bf16[8192,384]{1,0:T(8,128)(2,1)} %bitcast.28), custom_call_target="tpu_custom_call" | custom-call | bytes 30000 | tf_op jit(solution)/shard_map/pallas_call | solution.py:129
  83.1 0.0 copy-start.10
  83.1 0.0 collective-permute-done.3.refs_1_
  83.1 0.0 copy-done.4
  83.1 1.2 %shard_map.88 = (f32[2,64,384]{2,1,0:T(8,128)S(1)}, f32[2,64,384]{2,1,0:T(8,128)S(1)}) custom-call(s32[1]{0:T(128)} %bitcast.me_at, s32[1]{0:T(128)} %bitcast.1.core_at, f32[128,384]{1,0:T(8,128)S(1)} %get-tuple-element.39.mine, bf16[6144,384]{1,0:T(8,128)(2,1)S(1)} %shard_map.87.up, f32[128,384]{1,0:T(8,128)S(1)} %copy-done.4, ...), custom_call_target="tpu_custom_call" | custom-call | bytes 30000 | tf_op jit(solution)/shard_map/pallas_call | solution.py:184
  84.3 0.1 collective-permute-start.4
  84.4 1.4 %collective-permute-done.4 = f32[2,64,384]{2,1,0:T(8,128)S(1)} collective-permute-done((f32[2,64,384]{2,1,0:T(8,128)S(1)}, f32[2,64,384]{2,1,0:T(8,128)S(1)}, u32[]{:S(2)}, u32[]{:S(2)}) %collective-permute-start.4) | collective-permute-done | bytes 196640 | tf_op jit(solution)/shard_map/ppermute | solution.py:312
  85.8 0.7 add.76
  86.6 6.2 %all-to-all-start.2 = ((f32[8,16,384]{2,1,0:T(8,128)}), f32[8,16,384]{2,1,0:T(8,128)}, u32[]{:S(2)}, u32[]{:S(2)}) async-start(f32[8,16,384]{2,1,0:T(8,128)} %bitcast.7), calls=%async_computation.2 | async-start | bytes 393216 | tf_op jit(solution)/shard_map/all_to_all | solution.py:315
  92.8 2.0 %collective-permute-done.5.low = bf16[4,64,1152]{2,1,0:T(8,128)(2,1)} collective-permute-done((bf16[4,64,1152]{2,1,0:T(8,128)(2,1)}, bf16[4,64,1152]{2,1,0:T(8,128)(2,1)}, u32[]{:S(2)}, u32[]{:S(2)}) %collective-permute-start.5) | collective-permute-done | bytes 589856 | tf_op jit(solution)/shard_map/ppermute | solution.py:245
  94.7 0.0 collective-permute-done.9.refs_2_
  94.7 0.0 collective-permute-done.11.refs_5_
  94.7 2.4 %shard_map.89 = f32[64,384]{1,0:T(8,128)S(1)} custom-call(s32[1]{0:T(128)} %bitcast.8.at, bf16[4,64,1152]{2,1,0:T(8,128)(2,1)} %collective-permute-done.5.low, bf16[1152,384]{1,0:T(8,128)(2,1)S(1)} %slice_bitcast_fusion.mid, bf16[1152,384]{1,0:T(8,128)(2,1)S(1)} %collective-permute-done.6.refs_0_, bf16[1152,384]{1,0:T(8,128)(2,1)} %collective-permute-done.8.refs_1_, ...), custom_call_target="tpu_custom_call" | custom-call | bytes 30000 | tf_op jit(solution)/shard_map/pallas_call | solution.py:224
  97.2 0.1 collective-permute-start.14
  97.3 1.8 %collective-permute-start.13 = (f32[32,384]{1,0:T(8,128)S(1)}, f32[32,384]{1,0:T(8,128)S(1)}, u32[]{:S(2)}, u32[]{:S(2)}) collective-permute-start(f32[32,384]{1,0:T(8,128)S(1)} %get-tuple-element.52), channel_id=1, source_target_pairs={{0,16},{8,24},{16,0},{24,8},{1,17},{9,25},{17,1},{25,9},{2,18},{10... | collective-permute-start | bytes 147464 | tf_op jit(solution)/shard_map/ppermute | solution.py:340
  99.1 0.2 collective-permute-start.12
  99.3 0.9 reduce_sum.18
  100.2 1.5 %all-to-all-done.2 = f32[8,16,384]{2,1,0:T(8,128)} async-done(((f32[8,16,384]{2,1,0:T(8,128)}), f32[8,16,384]{2,1,0:T(8,128)}, u32[]{:S(2)}, u32[]{:S(2)}) %all-to-all-start.2) | async-done | bytes 196640 | tf_op jit(solution)/shard_map/all_to_all | solution.py:315
  101.7 0.9 reduce_sum.19
  102.7 0.0 collective-permute-done.14
  102.7 0.0 collective-permute-done.13
  102.7 0.2 collective-permute-done.12
  102.9 0.7 fusion.2
  (25 shorter events, 0.1 us)
Async XLA Ops:
  1.1 14.4 %collective-permute-start = (bf16[896,256]{1,0:T(8,128)(2,1)S(1)}, bf16[896,256]{1,0:T(8,128)(2,1)S(1)}, u32[]{:S(2)}, u32[]{:S(2)}) collective-permute-start(bf16[896,256]{1,0:T(8,128)(2,1)S(1)} %slice_bitcast_fusion.2), channel_id=1, source_target_pairs={{4,0},{0,4},{5,1},{1,5},{6,2},{2,6},{7,3},{3,7},{12,8},{8,12},{13,... | collective-permute-start | bytes 1376264 | tf_op jit(solution)/shard_map/ppermute | solution.py:245
  10.1 5.3 %copy-start.9 = (bf16[128,6144]{1,0:T(8,128)(2,1)}, bf16[128,6144]{1,0:T(8,128)(2,1)S(1)}, u32[]{:S(2)}) copy-start(bf16[128,6144]{1,0:T(8,128)(2,1)S(1)} %get-tuple-element.42) | copy-start | bytes 4718596
  10.1 40.7 %collective-permute-start.1 = (bf16[128,6144]{1,0:T(8,128)(2,1)}, bf16[128,6144]{1,0:T(8,128)(2,1)}, u32[]{:S(2)}, u32[]{:S(2)}) collective-permute-start(bf16[128,6144]{1,0:T(8,128)(2,1)} %get-tuple-element.29), channel_id=1, source_target_pairs={{4,0},{0,4},{5,1},{1,5},{6,2},{2,6},{7,3},{3,7},{12,8},{8,12},{13,... | collective-permute-start | bytes 4718600 | tf_op jit(solution)/shard_map/ppermute | solution.py:245
  15.4 0.8 copy-start.1
  16.2 26.4 %collective-permute-start.6 = (bf16[1152,384]{1,0:T(8,128)(2,1)S(1)}, bf16[1152,384]{1,0:T(8,128)(2,1)S(1)}, u32[]{:S(2)}, u32[]{:S(2)}) collective-permute-start(bf16[1152,384]{1,0:T(8,128)(2,1)S(1)} %slice_bitcast_fusion.mid), channel_id=1, source_target_pairs={{0,1},{1,2},{2,3},{4,5},{5,6},{6,7},{8,9},{9,10},{10,11},{12,13},{... | collective-permute-start | bytes 2654216 | tf_op jit(solution)/shard_map/ppermute | solution.py:288
  20.3 25.2 %collective-permute-start.7 = (bf16[1152,384]{1,0:T(8,128)(2,1)S(1)}, bf16[1152,384]{1,0:T(8,128)(2,1)}, u32[]{:S(2)}, u32[]{:S(2)}) collective-permute-start(bf16[1152,384]{1,0:T(8,128)(2,1)S(1)} %slice_bitcast_fusion.mid), channel_id=1, source_target_pairs={{1,0},{2,1},{3,2},{5,4},{6,5},{7,6},{9,8},{10,9},{11,10},{13,12},{... | collective-permute-start | bytes 2654216 | tf_op jit(solution)/shard_map/ppermute | solution.py:289
  21.6 36.9 %all-to-all-start = ((bf16[4,64,1152]{2,1,0:T(8,128)(2,1)}), bf16[4,64,1152]{2,1,0:T(8,128)(2,1)}, u32[]{:S(2)}, u32[]{:S(2)}) async-start(bf16[4,64,1152]{2,1,0:T(8,128)(2,1)} %get-tuple-element.37), calls=%async_computation | async-start | bytes 1179648 | tf_op jit(solution)/shard_map/all_to_all | solution.py:298
  28.4 54.7 %collective-permute-start.3 = (bf16[128,6144]{1,0:T(8,128)(2,1)}, bf16[128,6144]{1,0:T(8,128)(2,1)S(1)}, u32[]{:S(2)}, u32[]{:S(2)}) collective-permute-start(bf16[128,6144]{1,0:T(8,128)(2,1)} %copy-done.9), channel_id=1, source_target_pairs={{4,0},{0,4},{5,1},{1,5},{6,2},{2,6},{7,3},{3,7},{12,8},{8,12},{13,... | collective-permute-start | bytes 4718600 | tf_op jit(solution)/shard_map/ppermute | solution.py:245
  32.0 2.2 %copy-start = (bf16[1,8192,256]{2,1,0:T(8,128)(2,1)S(1)}, bf16[1,8192,256]{2,1,0:T(8,128)(2,1)}, u32[]{:S(2)}) copy-start(bf16[1,8192,256]{2,1,0:T(8,128)(2,1)} %param.8) | copy-start | bytes 12582916
  34.1 5.4 %copy-start.2 = (bf16[896,256]{1,0:T(8,128)(2,1)S(1)}, bf16[896,256]{1,0:T(8,128)(2,1)}, u32[]{:S(2)}) copy-start(bf16[896,256]{1,0:T(8,128)(2,1)} %copy-done.1) | copy-start | bytes 1376260
  39.5 5.9 %copy-start.5 = (f32[128,384]{1,0:T(8,128)}, f32[128,384]{1,0:T(8,128)S(1)}, u32[]{:S(2)}) copy-start(f32[128,384]{1,0:T(8,128)S(1)} %get-tuple-element.31.mine) | copy-start | bytes 589828
  41.2 0.7 copy-start.3
  41.9 0.7 copy-start.7
  45.5 21.6 %collective-permute-start.8 = (bf16[1152,384]{1,0:T(8,128)(2,1)S(1)}, bf16[1152,384]{1,0:T(8,128)(2,1)}, u32[]{:S(2)}, u32[]{:S(2)}) collective-permute-start(bf16[1152,384]{1,0:T(8,128)(2,1)S(1)} %collective-permute-done.6.refs_0_), channel_id=1, source_target_pairs={{1,2},{2,3},{5,6},{6,7},{9,10},{10,11},{13,14},{14,15},{17,18},{18... | collective-permute-start | bytes 2654216 | tf_op jit(solution)/shard_map/ppermute | solution.py:288
  47.1 22.8 %collective-permute-start.10 = (bf16[1152,384]{1,0:T(8,128)(2,1)}, bf16[1152,384]{1,0:T(8,128)(2,1)}, u32[]{:S(2)}, u32[]{:S(2)}) collective-permute-start(bf16[1152,384]{1,0:T(8,128)(2,1)} %collective-permute-done.7.refs_3_), channel_id=1, source_target_pairs={{1,0},{2,1},{5,4},{6,5},{9,8},{10,9},{13,12},{14,13},{17,16},{18,1... | collective-permute-start | bytes 2654216 | tf_op jit(solution)/shard_map/ppermute | solution.py:289
  48.4 2.4 %copy-start.6 = (f32[128,384]{1,0:T(8,128)S(1)}, f32[128,384]{1,0:T(8,128)}, u32[]{:S(2)}) copy-start(f32[128,384]{1,0:T(8,128)} %copy-done.5) | copy-start | bytes 589828
  48.4 2.4 %copy-start.8 = (f32[128,384]{1,0:T(8,128)S(1)}, f32[128,384]{1,0:T(8,128)}, u32[]{:S(2)}) copy-start(f32[128,384]{1,0:T(8,128)} %copy-done.7) | copy-start | bytes 589828
  53.2 1.5 %collective-permute-start.2 = (f32[2,64,384]{2,1,0:T(8,128)S(1)}, f32[2,64,384]{2,1,0:T(8,128)S(1)}, u32[]{:S(2)}, u32[]{:S(2)}) collective-permute-start(f32[2,64,384]{2,1,0:T(8,128)S(1)} %get-tuple-element.36), channel_id=1, source_target_pairs={{0,8},{8,0},{16,24},{24,16},{1,9},{9,1},{17,25},{25,17},{2,10},{10... | collective-permute-start | bytes 589832 | tf_op jit(solution)/shard_map/ppermute | solution.py:312
  58.5 20.7 %all-to-all-start.1 = ((f32[8,16,384]{2,1,0:T(8,128)}), f32[8,16,384]{2,1,0:T(8,128)}, u32[]{:S(2)}, u32[]{:S(2)}) async-start(f32[8,16,384]{2,1,0:T(8,128)} %bitcast.29), calls=%async_computation.1 | async-start | bytes 393216 | tf_op jit(solution)/shard_map/all_to_all | solution.py:315
  67.1 27.6 %collective-permute-start.9 = (bf16[1152,384]{1,0:T(8,128)(2,1)}, bf16[1152,384]{1,0:T(8,128)(2,1)}, u32[]{:S(2)}, u32[]{:S(2)}) collective-permute-start(bf16[1152,384]{1,0:T(8,128)(2,1)} %collective-permute-done.8.refs_1_), channel_id=1, source_target_pairs={{2,3},{6,7},{10,11},{14,15},{18,19},{22,23},{26,27},{30,31}} | collective-permute-start | bytes 2654216 | tf_op jit(solution)/shard_map/ppermute | solution.py:288
  69.8 24.9 %collective-permute-start.11 = (bf16[1152,384]{1,0:T(8,128)(2,1)}, bf16[1152,384]{1,0:T(8,128)(2,1)}, u32[]{:S(2)}, u32[]{:S(2)}) collective-permute-start(bf16[1152,384]{1,0:T(8,128)(2,1)} %collective-permute-done.10.refs_4_), channel_id=1, source_target_pairs={{1,0},{5,4},{9,8},{13,12},{17,16},{21,20},{25,24},{29,28}} | collective-permute-start | bytes 2654216 | tf_op jit(solution)/shard_map/ppermute | solution.py:289
  79.2 15.5 %collective-permute-start.5 = (bf16[4,64,1152]{2,1,0:T(8,128)(2,1)}, bf16[4,64,1152]{2,1,0:T(8,128)(2,1)}, u32[]{:S(2)}, u32[]{:S(2)}) collective-permute-start(bf16[4,64,1152]{2,1,0:T(8,128)(2,1)} %all-to-all-done), channel_id=1, source_target_pairs={{4,0},{0,4},{5,1},{1,5},{6,2},{2,6},{7,3},{3,7},{12,8},{8,12},{13,... | collective-permute-start | bytes 1769480 | tf_op jit(solution)/shard_map/ppermute | solution.py:245
  80.7 2.4 %copy-start.4 = (f32[128,384]{1,0:T(8,128)S(1)}, f32[128,384]{1,0:T(8,128)}, u32[]{:S(2)}) copy-start(f32[128,384]{1,0:T(8,128)} %copy-done.3) | copy-start | bytes 589828
  83.1 1.3 %copy-start.10 = (s32[384]{0:T(512)S(1)}, s32[384]{0:T(512)}, u32[]{:S(2)}) copy-start(s32[384]{0:T(512)} %param.15) | copy-start | bytes 4612
  84.3 1.5 %collective-permute-start.4 = (f32[2,64,384]{2,1,0:T(8,128)S(1)}, f32[2,64,384]{2,1,0:T(8,128)S(1)}, u32[]{:S(2)}, u32[]{:S(2)}) collective-permute-start(f32[2,64,384]{2,1,0:T(8,128)S(1)} %get-tuple-element.44), channel_id=1, source_target_pairs={{0,8},{8,0},{16,24},{24,16},{1,9},{9,1},{17,25},{25,17},{2,10},{10... | collective-permute-start | bytes 589832 | tf_op jit(solution)/shard_map/ppermute | solution.py:312
  85.8 13.5 %copy-start.15 = (s32[32]{0:T(128)S(1)}, s32[32]{0:T(128)}, u32[]{:S(2)}) copy-start(s32[32]{0:T(128)} %param.12) | copy-start | bytes 388
  86.5 16.3 %copy-start.11 = (f32[384]{0:T(512)S(1)}, f32[384]{0:T(512)}, u32[]{:S(2)}) copy-start(f32[384]{0:T(512)} %param.11) | copy-start | bytes 4612
  86.5 16.3 %copy-start.12 = (s32[384]{0:T(512)S(1)}, s32[384]{0:T(512)}, u32[]{:S(2)}) copy-start(s32[384]{0:T(512)} %param.13) | copy-start | bytes 4612
  86.5 16.3 %copy-start.13 = (f32[32]{0:T(128)S(1)}, f32[32]{0:T(128)}, u32[]{:S(2)}) copy-start(f32[32]{0:T(128)} %param.10) | copy-start | bytes 388
  86.5 16.3 %copy-start.14 = (s32[32]{0:T(128)S(1)}, s32[32]{0:T(128)}, u32[]{:S(2)}) copy-start(s32[32]{0:T(128)} %param.14) | copy-start | bytes 388
  86.6 15.2 %all-to-all-start.2 = ((f32[8,16,384]{2,1,0:T(8,128)}), f32[8,16,384]{2,1,0:T(8,128)}, u32[]{:S(2)}, u32[]{:S(2)}) async-start(f32[8,16,384]{2,1,0:T(8,128)} %bitcast.7), calls=%async_computation.2 | async-start | bytes 393216 | tf_op jit(solution)/shard_map/all_to_all | solution.py:315
  97.2 5.5 %collective-permute-start.14 = (f32[32,384]{1,0:T(8,128)S(1)}, f32[32,384]{1,0:T(8,128)S(1)}, u32[]{:S(2)}, u32[]{:S(2)}) collective-permute-start(f32[32,384]{1,0:T(8,128)S(1)} %dynamic-slice_bitcast_fusion), channel_id=1, source_target_pairs={{0,8},{8,0},{16,24},{24,16},{1,9},{9,1},{17,25},{25,17},{2,10},{10... | collective-permute-start | bytes 147464 | tf_op jit(solution)/shard_map/ppermute | solution.py:340
  97.3 5.4 %collective-permute-start.13 = (f32[32,384]{1,0:T(8,128)S(1)}, f32[32,384]{1,0:T(8,128)S(1)}, u32[]{:S(2)}, u32[]{:S(2)}) collective-permute-start(f32[32,384]{1,0:T(8,128)S(1)} %get-tuple-element.52), channel_id=1, source_target_pairs={{0,16},{8,24},{16,0},{24,8},{1,17},{9,25},{17,1},{25,9},{2,18},{10... | collective-permute-start | bytes 147464 | tf_op jit(solution)/shard_map/ppermute | solution.py:340
  99.1 3.8 %collective-permute-start.12 = (f32[32,384]{1,0:T(8,128)S(1)}, f32[32,384]{1,0:T(8,128)S(1)}, u32[]{:S(2)}, u32[]{:S(2)}) collective-permute-start(f32[32,384]{1,0:T(8,128)S(1)} %get-tuple-element.51), channel_id=1, source_target_pairs={{0,24},{8,16},{16,8},{24,0},{1,25},{9,17},{17,9},{25,1},{2,26},{10... | collective-permute-start | bytes 147464 | tf_op jit(solution)/shard_map/ppermute | solution.py:340

commit v8 on v7

--- a/solution.py
+++ b/solution.py
@@ -236,6 +236,31 @@
     )(depth.reshape(1), got, own, *forward, *backward)
 
 
+def finished(from_a, from_b, terms, cubed, weight, mask):
+    _, half, width = from_a.shape
+
+    def body(a, b, cube, scale, keep, *refs):
+        out = refs[-1]
+        tail = refs[0][...]
+        for ref in refs[1:-1]:
+            tail = tail + ref[...]
+        for part, sums in enumerate((jnp.sum(a[...], axis=0), jnp.sum(b[...], axis=0))):
+            rows = slice(part * half, (part + 1) * half)
+            total = sums + tail[rows]
+            value = cube[rows] * (total * total) / scale[...]
+            out[rows] = jnp.where(keep[rows] > 0, value, jnp.zeros_like(value))
+
+    vmem = pl.BlockSpec(memory_space=pltpu.VMEM)
+    return pl.pallas_call(
+        body,
+        in_specs=[vmem] * (5 + len(terms)),
+        out_specs=vmem,
+        out_shape=jax.ShapeDtypeStruct((2 * half, width), jnp.float32),
+        compiler_params=params(),
+        cost_estimate=cost(),
+    )(from_a, from_b, cubed, weight, mask, *terms)
+
+
 def make_local(n_low, n_up, n_dep):
     n_core = n_low // n_up
     others = range(1, n_up)
@@ -316,11 +341,9 @@
 
         held_a = held_rows(after(upper_rows, *so_far[0]), rows - n_main, n_main)
         sent_a, from_a = reduced(0, crossed[1], held_a, sorted_tail)
-        held_b = held_rows(after(upper_rows, sent_a), rows - n_main, n_main)
+        held_b = held_rows(after(upper_rows, from_a), rows - n_main, n_main)
         cross(sorted_tail, from_a)
         last, from_b = reduced(1, crossed[2], held_b, from_a)
-        sum_a, sum_b = jnp.sum(from_a, axis=0), jnp.sum(from_b, axis=0)
-        main = jnp.concatenate([sum_a, sum_b], axis=0)
 
         terms = [tail_product(depth, after(g, last), up_tail, forward, backward) for g in crossed[3]]
 
@@ -330,7 +353,7 @@
                 block = jnp.where((me + s) % n_up == y % n_up, terms[s - 1], block)
             return block
 
-        total = main
+        ends = []
         for t in reversed(range(n_up)):
             by_core = term_for(my_y + t).reshape(n_core, mine, width)
             for k in reversed(range(n_core)):
@@ -338,9 +361,8 @@
                 if t or k:
                     pairs = [(low(y, c), low(y + t, (c + k) % n_core)) for y in range(n_up) for c in range(n_core)]
                     term = lax.ppermute(term, "lower", pairs)
-                total = total + term
-        value = cubed * (total * total) / weight_upper[None, :]
-        return jnp.where(allowed, value, jnp.zeros_like(value))
+                ends.append(term)
+        return finished(from_a, from_b, ends, cubed, weight_upper[None, :], allowed.astype(jnp.int32))
 
     return local
 

time: 105 us -> 105 us (level)
  other arithmetic: 4.08 us -> 2.21 us
  waiting for transfers between devices: 25 us -> 26.2 us
    reduce_sum x2 -> x0, other arithmetic: 1.89 us -> none  [local(): sum_a, sum_b = (jnp.sum(from_a, axis=0), jnp.sum(from_b, axis=0))]
    ppermute x3, waiting for transfers between devices: 4.02 us -> 5.76 us  [pass_on(): backward.append(lax.ppermute(held_down, 'depth', down[:n_dep - 1 - i]))]
    ppermute x3, waiting for transfers between devices: 0.2 us -> 1.84 us  [local(): term = lax.ppermute(term, 'lower', pairs)]
    all_to_all x2, waiting for transfers between devices: 9.58 us -> 8.37 us  [reduced(): lax.all_to_all(by_owner, OWNERS, 0, 0, axis_index_groups=same_core)]
    all_to_all x1, waiting for transfers between devices: 3 us -> 1.9 us  [local(): sorted_tail = lax.all_to_all(tail_rows, 'depth', 0, 0)]
    unnamed x32 -> x34, local copies, waits for them, and re-layouts: 4.37 us -> 4.38 us
  transfers between devices with their start and end apart: 18 -> 18, of which waited for: 10 -> 10; matrix products, arithmetic and copies ran while one was open for 7% -> 6% of each run, Pallas kernels for 23% -> 23%
where the time goes in v8:
time: 105 us; the launch traced here: 104 us
  starting transfers between devices  41.5 us (40%)
  waiting for transfers between devices  26.2 us (25%)
  Pallas kernels  24.5 us (23%)
  local copies, waits for them, and re-layouts  9.28 us (9%)
  other arithmetic  2.21 us (2%)
    all_to_all x2, starting transfers between devices, reduced(): lax.all_to_all(by_owner, OWNERS, 0, 0, axis_index_groups=same_core)  15.1 us
    all_to_all x2, waiting for transfers between devices, reduced(): lax.all_to_all(by_owner, OWNERS, 0, 0, axis_index_groups=same_core)  8.37 us
    ppermute x3, starting transfers between devices, pass_on(): forward.append(lax.ppermute(held_up, 'depth', up[i:]))  7.29 us
    pallas_call x2, Pallas kernels, rows_product(): pl.pallas_call(body, grid=(steps,), in_specs=[pl.BlockSpec((block, states...  7 us
    all_to_all x1, starting transfers between devices, local(): sorted_tail = lax.all_to_all(tail_rows, 'depth', 0, 0)  6.83 us
    pallas_call x1, Pallas kernels, turn(): pl.pallas_call(body, grid=(steps,), in_specs=[pl.BlockSpec((block, cols),...  6.07 us
    ppermute x4, starting transfers between devices, shifted(): lax.ppermute(x, 'upper', [((u + shift) % n_up, u) for u in range(n_up)])  6.03 us
    ppermute x3, waiting for transfers between devices, pass_on(): backward.append(lax.ppermute(held_down, 'depth', down[:n_dep - 1 - i]))  5.76 us
  transfers between devices with their start and end apart: 18, of which 10 were waited for; matrix products, arithmetic and copies ran while one was open for 6% of the time, Pallas kernels for 23%

profile of v8, /device:TPU:0, one launch (start us, length us, event | category | flops | bytes accessed | tf_op | source)
XLA Modules:
  0.0 104.0 jit_solution(4390994881590487149)
XLA Ops:
  0.0 1.0 %slice_bitcast_fusion.2 = bf16[896,256]{1,0:T(8,128)(2,1)S(1)} fusion(bf16[1,8192,256]{2,1,0:T(8,128)(2,1)} %param.8), kind=kLoop, calls=%fused_computation.2 | loop fusion | bytes 917504 | tf_op jit(solution)/shard_map/slice | solution.py:316
  1.1 3.0 %collective-permute-start = (bf16[896,256]{1,0:T(8,128)(2,1)S(1)}, bf16[896,256]{1,0:T(8,128)(2,1)S(1)}, u32[]{:S(2)}, u32[]{:S(2)}) collective-permute-start(bf16[896,256]{1,0:T(8,128)(2,1)S(1)} %slice_bitcast_fusion.2), channel_id=1, source_target_pairs={{4,0},{0,4},{5,1},{1,5},{6,2},{2,6},{7,3},{3,7},{12,8},{8,12},{13,... | collective-permute-start | bytes 1376264 | tf_op jit(solution)/shard_map/ppermute | solution.py:270
  4.1 6.1 %shard_map.82 = (bf16[128,6144]{1,0:T(8,128)(2,1)}, bf16[128,6144]{1,0:T(8,128)(2,1)S(1)}, bf16[4,64,1152]{2,1,0:T(8,128)(2,1)}) custom-call(bf16[8192,256]{1,0:T(8,128)(2,1)} %bitcast.23, bf16[8192,256]{1,0:T(8,128)(2,1)} %bitcast.24), custom_call_target="tpu_custom_call" | custom-call | bytes 30000 | tf_op jit(solution)/shard_map/pallas_call | solution.py:60
  10.1 0.0 collective-permute-start.1
  10.2 1.8 %slice_bitcast_fusion.mid = bf16[1152,384]{1,0:T(8,128)(2,1)S(1)} fusion(bf16[1,8192,384]{2,1,0:T(8,128)(2,1)} %param.9), kind=kLoop, calls=%fused_computation | loop fusion | bytes 1769472 | tf_op jit(solution)/shard_map/slice | solution.py:321
  12.0 3.4 %collective-permute-done.low = bf16[896,256]{1,0:T(8,128)(2,1)S(1)} collective-permute-done((bf16[896,256]{1,0:T(8,128)(2,1)S(1)}, bf16[896,256]{1,0:T(8,128)(2,1)S(1)}, u32[]{:S(2)}, u32[]{:S(2)}) %collective-permute-start) | collective-permute-done | bytes 458784 | tf_op jit(solution)/shard_map/ppermute | solution.py:270
  15.4 0.8 copy-done.1
  16.2 4.1 %collective-permute-start.6 = (bf16[1152,384]{1,0:T(8,128)(2,1)S(1)}, bf16[1152,384]{1,0:T(8,128)(2,1)S(1)}, u32[]{:S(2)}, u32[]{:S(2)}) collective-permute-start(bf16[1152,384]{1,0:T(8,128)(2,1)S(1)} %slice_bitcast_fusion.mid), channel_id=1, source_target_pairs={{0,1},{1,2},{2,3},{4,5},{5,6},{6,7},{8,9},{9,10},{10,11},{12,13},{... | collective-permute-start | bytes 2654216 | tf_op jit(solution)/shard_map/ppermute | solution.py:313
  20.3 1.3 %collective-permute-start.7 = (bf16[1152,384]{1,0:T(8,128)(2,1)S(1)}, bf16[1152,384]{1,0:T(8,128)(2,1)}, u32[]{:S(2)}, u32[]{:S(2)}) collective-permute-start(bf16[1152,384]{1,0:T(8,128)(2,1)S(1)} %slice_bitcast_fusion.mid), channel_id=1, source_target_pairs={{1,0},{2,1},{3,2},{5,4},{6,5},{7,6},{9,8},{10,9},{11,10},{13,12},{... | collective-permute-start | bytes 2654216 | tf_op jit(solution)/shard_map/ppermute | solution.py:314
  21.6 6.8 %all-to-all-start = ((bf16[4,64,1152]{2,1,0:T(8,128)(2,1)}), bf16[4,64,1152]{2,1,0:T(8,128)(2,1)}, u32[]{:S(2)}, u32[]{:S(2)}) async-start(bf16[4,64,1152]{2,1,0:T(8,128)(2,1)} %get-tuple-element.37), calls=%async_computation | async-start | bytes 1179648 | tf_op jit(solution)/shard_map/all_to_all | solution.py:323
  28.4 1.5 %collective-permute-start.3 = (bf16[128,6144]{1,0:T(8,128)(2,1)}, bf16[128,6144]{1,0:T(8,128)(2,1)S(1)}, u32[]{:S(2)}, u32[]{:S(2)}) collective-permute-start(bf16[128,6144]{1,0:T(8,128)(2,1)} %copy-done.10), channel_id=1, source_target_pairs={{4,0},{0,4},{5,1},{1,5},{6,2},{2,6},{7,3},{3,7},{12,8},{8,12},{13,... | collective-permute-start | bytes 4718600 | tf_op jit(solution)/shard_map/ppermute | solution.py:270
  29.9 2.0 %slice_bitcast_fusion.1.up = bf16[896,384]{1,0:T(8,128)(2,1)} fusion(bf16[1,8192,384]{2,1,0:T(8,128)(2,1)} %param.9), kind=kLoop, calls=%fused_computation.1 | loop fusion | bytes 1376256 | tf_op jit(solution)/shard_map/slice | solution.py:326
  31.9 2.2 %copy-done = bf16[1,8192,256]{2,1,0:T(8,128)(2,1)S(1)} copy-done((bf16[1,8192,256]{2,1,0:T(8,128)(2,1)S(1)}, bf16[1,8192,256]{2,1,0:T(8,128)(2,1)}, u32[]{:S(2)}) %copy-start) | copy-done | bytes 4194328
  34.1 5.4 %shard_map.83 = (f32[128,384]{1,0:T(8,128)S(1)}, f32[128,384]{1,0:T(8,128)S(1)}) custom-call(bf16[8192,256]{1,0:T(8,128)(2,1)S(1)} %bitcast.25, bf16[8192,384]{1,0:T(8,128)(2,1)} %bitcast.26), custom_call_target="tpu_custom_call" | custom-call | bytes 30000 | tf_op jit(solution)/shard_map/pallas_call | solution.py:105
  39.5 1.6 %shard_map.84 = (f32[128,384]{1,0:T(8,128)S(1)}, f32[128,384]{1,0:T(8,128)S(1)}) custom-call(bf16[896,256]{1,0:T(8,128)(2,1)S(1)} %copy-done.2, bf16[896,384]{1,0:T(8,128)(2,1)} %slice_bitcast_fusion.1.up), custom_call_target="tpu_custom_call" | custom-call | bytes 30000 | tf_op jit(solution)/shard_map/pallas_call | solution.py:105
  41.2 0.0 copy-start.5
  41.2 0.7 copy-done.5
  41.8 0.7 copy-done.7
  42.5 0.0 collective-permute-done.6.refs_0_
  42.5 4.1 %collective-permute-done.7.refs_3_ = bf16[1152,384]{1,0:T(8,128)(2,1)} collective-permute-done((bf16[1152,384]{1,0:T(8,128)(2,1)S(1)}, bf16[1152,384]{1,0:T(8,128)(2,1)}, u32[]{:S(2)}, u32[]{:S(2)}) %collective-permute-start.7) | collective-permute-done | bytes 884768 | tf_op jit(solution)/shard_map/ppermute | solution.py:314
  46.6 1.3 %collective-permute-start.10 = (bf16[1152,384]{1,0:T(8,128)(2,1)}, bf16[1152,384]{1,0:T(8,128)(2,1)}, u32[]{:S(2)}, u32[]{:S(2)}) collective-permute-start(bf16[1152,384]{1,0:T(8,128)(2,1)} %collective-permute-done.7.refs_3_), channel_id=1, source_target_pairs={{1,0},{2,1},{5,4},{6,5},{9,8},{10,9},{13,12},{14,13},{17,16},{18,1... | collective-permute-start | bytes 2654216 | tf_op jit(solution)/shard_map/ppermute | solution.py:314
  47.9 1.6 %collective-permute-start.8 = (bf16[1152,384]{1,0:T(8,128)(2,1)S(1)}, bf16[1152,384]{1,0:T(8,128)(2,1)}, u32[]{:S(2)}, u32[]{:S(2)}) collective-permute-start(bf16[1152,384]{1,0:T(8,128)(2,1)S(1)} %collective-permute-done.6.refs_0_), channel_id=1, source_target_pairs={{1,2},{2,3},{5,6},{6,7},{9,10},{10,11},{13,14},{14,15},{17,18},{18... | collective-permute-start | bytes 2654216 | tf_op jit(solution)/shard_map/ppermute | solution.py:313
  49.5 2.4 %shard_map.85.up = bf16[6144,384]{1,0:T(8,128)(2,1)S(1)} custom-call(bf16[8192,384]{1,0:T(8,128)(2,1)} %bitcast.27), custom_call_target="tpu_custom_call" | custom-call | bytes 30000 | tf_op jit(solution)/shard_map/pallas_call | solution.py:129
  51.9 0.0 copy-start.15
  51.9 0.0 copy-start.11
  51.9 0.0 copy-start.13
  51.9 0.0 copy-start.14
  51.9 0.0 collective-permute-done.1.refs_1_
  51.9 2.4 %shard_map.86 = (f32[2,64,384]{2,1,0:T(8,128)S(1)}, f32[2,64,384]{2,1,0:T(8,128)S(1)}) custom-call(s32[1]{0:T(128)} %bitcast.me_at, s32[1]{0:T(128)} %bitcast.1.core_at, f32[128,384]{1,0:T(8,128)S(1)} %get-tuple-element.31.mine, bf16[6144,384]{1,0:T(8,128)(2,1)S(1)} %shard_map.85.up, f32[128,384]{1,0:T(8,128)S(1)} %copy-done.8, ...), custom_call_target="tpu_custom_call" | custom-call | bytes 30000 | tf_op jit(solution)/shard_map/pallas_call | solution.py:184
  54.4 0.1 collective-permute-start.2
  54.5 1.4 %collective-permute-done.2 = f32[2,64,384]{2,1,0:T(8,128)S(1)} collective-permute-done((f32[2,64,384]{2,1,0:T(8,128)S(1)}, f32[2,64,384]{2,1,0:T(8,128)S(1)}, u32[]{:S(2)}, u32[]{:S(2)}) %collective-permute-start.2) | collective-permute-done | bytes 196640 | tf_op jit(solution)/shard_map/ppermute | solution.py:337
  55.9 0.7 add.62
  56.6 1.9 %all-to-all-done = bf16[4,64,1152]{2,1,0:T(8,128)(2,1)} async-done(((bf16[4,64,1152]{2,1,0:T(8,128)(2,1)}), bf16[4,64,1152]{2,1,0:T(8,128)(2,1)}, u32[]{:S(2)}, u32[]{:S(2)}) %all-to-all-start) | async-done | bytes 589856 | tf_op jit(solution)/shard_map/all_to_all | solution.py:323
  58.5 9.7 %all-to-all-start.1 = ((f32[8,16,384]{2,1,0:T(8,128)}), f32[8,16,384]{2,1,0:T(8,128)S(1)}, u32[]{:S(2)}, u32[]{:S(2)}) async-start(f32[8,16,384]{2,1,0:T(8,128)} %bitcast.29), calls=%async_computation.1 | async-start | bytes 393216 | tf_op jit(solution)/shard_map/all_to_all | solution.py:340
  68.1 1.7 %collective-permute-done.10.refs_4_ = bf16[1152,384]{1,0:T(8,128)(2,1)} collective-permute-done((bf16[1152,384]{1,0:T(8,128)(2,1)}, bf16[1152,384]{1,0:T(8,128)(2,1)}, u32[]{:S(2)}, u32[]{:S(2)}) %collective-permute-start.10) | collective-permute-done | bytes 884768 | tf_op jit(solution)/shard_map/ppermute | solution.py:314
  69.8 1.3 %collective-permute-start.11 = (bf16[1152,384]{1,0:T(8,128)(2,1)}, bf16[1152,384]{1,0:T(8,128)(2,1)}, u32[]{:S(2)}, u32[]{:S(2)}) collective-permute-start(bf16[1152,384]{1,0:T(8,128)(2,1)} %collective-permute-done.10.refs_4_), channel_id=1, source_target_pairs={{1,0},{5,4},{9,8},{13,12},{17,16},{21,20},{25,24},{29,28}} | collective-permute-start | bytes 2654216 | tf_op jit(solution)/shard_map/ppermute | solution.py:314
  71.1 0.0 collective-permute-done.8.refs_1_
  71.1 1.6 %collective-permute-start.9 = (bf16[1152,384]{1,0:T(8,128)(2,1)}, bf16[1152,384]{1,0:T(8,128)(2,1)}, u32[]{:S(2)}, u32[]{:S(2)}) collective-permute-start(bf16[1152,384]{1,0:T(8,128)(2,1)} %collective-permute-done.8.refs_1_), channel_id=1, source_target_pairs={{2,3},{6,7},{10,11},{14,15},{18,19},{22,23},{26,27},{30,31}} | collective-permute-start | bytes 2654216 | tf_op jit(solution)/shard_map/ppermute | solution.py:313
  72.7 6.4 %all-to-all-done.1.a = f32[8,16,384]{2,1,0:T(8,128)S(1)} async-done(((f32[8,16,384]{2,1,0:T(8,128)}), f32[8,16,384]{2,1,0:T(8,128)S(1)}, u32[]{:S(2)}, u32[]{:S(2)}) %all-to-all-start.1) | async-done | bytes 196640 | tf_op jit(solution)/shard_map/all_to_all | solution.py:340
  79.1 1.5 %collective-permute-start.5 = (bf16[4,64,1152]{2,1,0:T(8,128)(2,1)}, bf16[4,64,1152]{2,1,0:T(8,128)(2,1)}, u32[]{:S(2)}, u32[]{:S(2)}) collective-permute-start(bf16[4,64,1152]{2,1,0:T(8,128)(2,1)} %all-to-all-done), channel_id=1, source_target_pairs={{4,0},{0,4},{5,1},{1,5},{6,2},{2,6},{7,3},{3,7},{12,8},{8,12},{13,... | collective-permute-start | bytes 1769480 | tf_op jit(solution)/shard_map/ppermute | solution.py:270
  80.6 0.0 copy-done.15
  80.6 0.7 fusion.1.keep
  81.3 2.4 %shard_map.87.up = bf16[6144,384]{1,0:T(8,128)(2,1)S(1)} custom-call(bf16[8192,384]{1,0:T(8,128)(2,1)} %bitcast.28), custom_call_target="tpu_custom_call" | custom-call | bytes 30000 | tf_op jit(solution)/shard_map/pallas_call | solution.py:129
  83.8 0.0 copy-start.12
  83.8 0.0 copy-start.16
  83.8 0.0 collective-permute-done.3.refs_1_
  83.8 1.2 %shard_map.88 = (f32[2,64,384]{2,1,0:T(8,128)S(1)}, f32[2,64,384]{2,1,0:T(8,128)S(1)}) custom-call(s32[1]{0:T(128)} %bitcast.me_at, s32[1]{0:T(128)} %bitcast.1.core_at, f32[128,384]{1,0:T(8,128)S(1)} %copy-done.4, bf16[6144,384]{1,0:T(8,128)(2,1)S(1)} %shard_map.87.up, f32[128,384]{1,0:T(8,128)S(1)} %copy-done.6, ...), custom_call_target="tpu_custom_call" | custom-call | bytes 30000 | tf_op jit(solution)/shard_map/pallas_call | solution.py:184
  85.0 0.1 collective-permute-start.4
  85.1 0.1 multiply_multiply_fusion.cube
  85.2 1.3 %collective-permute-done.4 = f32[2,64,384]{2,1,0:T(8,128)S(1)} collective-permute-done((f32[2,64,384]{2,1,0:T(8,128)S(1)}, f32[2,64,384]{2,1,0:T(8,128)S(1)}, u32[]{:S(2)}, u32[]{:S(2)}) %collective-permute-start.4) | collective-permute-done | bytes 196640 | tf_op jit(solution)/shard_map/ppermute | solution.py:337
  86.5 0.7 add.63
  87.2 5.4 %all-to-all-start.2 = ((f32[8,16,384]{2,1,0:T(8,128)}), f32[8,16,384]{2,1,0:T(8,128)S(1)}, u32[]{:S(2)}, u32[]{:S(2)}) async-start(f32[8,16,384]{2,1,0:T(8,128)} %bitcast.7), calls=%async_computation.2 | async-start | bytes 393216 | tf_op jit(solution)/shard_map/all_to_all | solution.py:340
  92.6 2.1 %collective-permute-done.5.low = bf16[4,64,1152]{2,1,0:T(8,128)(2,1)} collective-permute-done((bf16[4,64,1152]{2,1,0:T(8,128)(2,1)}, bf16[4,64,1152]{2,1,0:T(8,128)(2,1)}, u32[]{:S(2)}, u32[]{:S(2)}) %collective-permute-start.5) | collective-permute-done | bytes 589856 | tf_op jit(solution)/shard_map/ppermute | solution.py:270
  94.7 0.0 collective-permute-done.11.refs_5_
  94.7 0.0 collective-permute-done.9.refs_2_
  94.7 2.4 %shard_map.89 = f32[64,384]{1,0:T(8,128)S(1)} custom-call(s32[1]{0:T(128)} %bitcast.8.at, bf16[4,64,1152]{2,1,0:T(8,128)(2,1)} %collective-permute-done.5.low, bf16[1152,384]{1,0:T(8,128)(2,1)S(1)} %slice_bitcast_fusion.mid, bf16[1152,384]{1,0:T(8,128)(2,1)S(1)} %collective-permute-done.6.refs_0_, bf16[1152,384]{1,0:T(8,128)(2,1)} %collective-permute-done.8.refs_1_, ...), custom_call_target="tpu_custom_call" | custom-call | bytes 30000 | tf_op jit(solution)/shard_map/pallas_call | solution.py:224
  97.2 0.1 collective-permute-start.14
  97.3 1.9 %collective-permute-start.12 = (f32[32,384]{1,0:T(8,128)S(1)}, f32[32,384]{1,0:T(8,128)S(1)}, u32[]{:S(2)}, u32[]{:S(2)}) collective-permute-start(f32[32,384]{1,0:T(8,128)S(1)} %get-tuple-element.56), channel_id=1, source_target_pairs={{0,24},{8,16},{16,8},{24,0},{1,25},{9,17},{17,9},{25,1},{2,26},{10... | collective-permute-start | bytes 147464 | tf_op jit(solution)/shard_map/ppermute | solution.py:363
  99.2 0.3 collective-permute-start.13
  99.5 2.0 %all-to-all-done.2.b = f32[8,16,384]{2,1,0:T(8,128)S(1)} async-done(((f32[8,16,384]{2,1,0:T(8,128)}), f32[8,16,384]{2,1,0:T(8,128)S(1)}, u32[]{:S(2)}, u32[]{:S(2)}) %all-to-all-start.2) | async-done | bytes 196640 | tf_op jit(solution)/shard_map/all_to_all | solution.py:340
  101.5 0.0 collective-permute-done.14.refs_2_
  101.5 0.0 collective-permute-done.12.refs_0_
  101.5 1.8 %collective-permute-done.13.refs_1_ = f32[32,384]{1,0:T(8,128)S(1)} collective-permute-done((f32[32,384]{1,0:T(8,128)S(1)}, f32[32,384]{1,0:T(8,128)S(1)}, u32[]{:S(2)}, u32[]{:S(2)}) %collective-permute-start.13) | collective-permute-done | bytes 49184 | tf_op jit(solution)/shard_map/ppermute | solution.py:363
  103.3 0.7 shard_map.90
  (28 shorter events, 0.1 us)
Async XLA Ops:
  1.1 14.4 %collective-permute-start = (bf16[896,256]{1,0:T(8,128)(2,1)S(1)}, bf16[896,256]{1,0:T(8,128)(2,1)S(1)}, u32[]{:S(2)}, u32[]{:S(2)}) collective-permute-start(bf16[896,256]{1,0:T(8,128)(2,1)S(1)} %slice_bitcast_fusion.2), channel_id=1, source_target_pairs={{4,0},{0,4},{5,1},{1,5},{6,2},{2,6},{7,3},{3,7},{12,8},{8,12},{13,... | collective-permute-start | bytes 1376264 | tf_op jit(solution)/shard_map/ppermute | solution.py:270
  10.1 5.3 %copy-start.10 = (bf16[128,6144]{1,0:T(8,128)(2,1)}, bf16[128,6144]{1,0:T(8,128)(2,1)S(1)}, u32[]{:S(2)}) copy-start(bf16[128,6144]{1,0:T(8,128)(2,1)S(1)} %get-tuple-element.42) | copy-start | bytes 4718596
  10.1 41.8 %collective-permute-start.1 = (bf16[128,6144]{1,0:T(8,128)(2,1)}, bf16[128,6144]{1,0:T(8,128)(2,1)}, u32[]{:S(2)}, u32[]{:S(2)}) collective-permute-start(bf16[128,6144]{1,0:T(8,128)(2,1)} %get-tuple-element.29), channel_id=1, source_target_pairs={{4,0},{0,4},{5,1},{1,5},{6,2},{2,6},{7,3},{3,7},{12,8},{8,12},{13,... | collective-permute-start | bytes 4718600 | tf_op jit(solution)/shard_map/ppermute | solution.py:270
  15.4 0.8 copy-start.1
  16.2 26.3 %collective-permute-start.6 = (bf16[1152,384]{1,0:T(8,128)(2,1)S(1)}, bf16[1152,384]{1,0:T(8,128)(2,1)S(1)}, u32[]{:S(2)}, u32[]{:S(2)}) collective-permute-start(bf16[1152,384]{1,0:T(8,128)(2,1)S(1)} %slice_bitcast_fusion.mid), channel_id=1, source_target_pairs={{0,1},{1,2},{2,3},{4,5},{5,6},{6,7},{8,9},{9,10},{10,11},{12,13},{... | collective-permute-start | bytes 2654216 | tf_op jit(solution)/shard_map/ppermute | solution.py:313
  20.3 26.3 %collective-permute-start.7 = (bf16[1152,384]{1,0:T(8,128)(2,1)S(1)}, bf16[1152,384]{1,0:T(8,128)(2,1)}, u32[]{:S(2)}, u32[]{:S(2)}) collective-permute-start(bf16[1152,384]{1,0:T(8,128)(2,1)S(1)} %slice_bitcast_fusion.mid), channel_id=1, source_target_pairs={{1,0},{2,1},{3,2},{5,4},{6,5},{7,6},{9,8},{10,9},{11,10},{13,12},{... | collective-permute-start | bytes 2654216 | tf_op jit(solution)/shard_map/ppermute | solution.py:314
  21.6 36.9 %all-to-all-start = ((bf16[4,64,1152]{2,1,0:T(8,128)(2,1)}), bf16[4,64,1152]{2,1,0:T(8,128)(2,1)}, u32[]{:S(2)}, u32[]{:S(2)}) async-start(bf16[4,64,1152]{2,1,0:T(8,128)(2,1)} %get-tuple-element.37), calls=%async_computation | async-start | bytes 1179648 | tf_op jit(solution)/shard_map/all_to_all | solution.py:323
  28.4 55.4 %collective-permute-start.3 = (bf16[128,6144]{1,0:T(8,128)(2,1)}, bf16[128,6144]{1,0:T(8,128)(2,1)S(1)}, u32[]{:S(2)}, u32[]{:S(2)}) collective-permute-start(bf16[128,6144]{1,0:T(8,128)(2,1)} %copy-done.10), channel_id=1, source_target_pairs={{4,0},{0,4},{5,1},{1,5},{6,2},{2,6},{7,3},{3,7},{12,8},{8,12},{13,... | collective-permute-start | bytes 4718600 | tf_op jit(solution)/shard_map/ppermute | solution.py:270
  31.9 2.2 %copy-start = (bf16[1,8192,256]{2,1,0:T(8,128)(2,1)S(1)}, bf16[1,8192,256]{2,1,0:T(8,128)(2,1)}, u32[]{:S(2)}) copy-start(bf16[1,8192,256]{2,1,0:T(8,128)(2,1)} %param.8) | copy-start | bytes 12582916
  34.1 5.4 %copy-start.2 = (bf16[896,256]{1,0:T(8,128)(2,1)S(1)}, bf16[896,256]{1,0:T(8,128)(2,1)}, u32[]{:S(2)}) copy-start(bf16[896,256]{1,0:T(8,128)(2,1)} %copy-done.1) | copy-start | bytes 1376260
  39.5 7.1 %copy-start.3 = (f32[128,384]{1,0:T(8,128)}, f32[128,384]{1,0:T(8,128)S(1)}, u32[]{:S(2)}) copy-start(f32[128,384]{1,0:T(8,128)S(1)} %get-tuple-element.39.mine) | copy-start | bytes 589828
  41.2 0.7 copy-start.5
  41.8 0.7 copy-start.7
  46.6 23.2 %collective-permute-start.10 = (bf16[1152,384]{1,0:T(8,128)(2,1)}, bf16[1152,384]{1,0:T(8,128)(2,1)}, u32[]{:S(2)}, u32[]{:S(2)}) collective-permute-start(bf16[1152,384]{1,0:T(8,128)(2,1)} %collective-permute-done.7.refs_3_), channel_id=1, source_target_pairs={{1,0},{2,1},{5,4},{6,5},{9,8},{10,9},{13,12},{14,13},{17,16},{18,1... | collective-permute-start | bytes 2654216 | tf_op jit(solution)/shard_map/ppermute | solution.py:314
  47.9 23.2 %collective-permute-start.8 = (bf16[1152,384]{1,0:T(8,128)(2,1)S(1)}, bf16[1152,384]{1,0:T(8,128)(2,1)}, u32[]{:S(2)}, u32[]{:S(2)}) collective-permute-start(bf16[1152,384]{1,0:T(8,128)(2,1)S(1)} %collective-permute-done.6.refs_0_), channel_id=1, source_target_pairs={{1,2},{2,3},{5,6},{6,7},{9,10},{10,11},{13,14},{14,15},{17,18},{18... | collective-permute-start | bytes 2654216 | tf_op jit(solution)/shard_map/ppermute | solution.py:313
  49.5 2.5 %copy-start.8 = (f32[128,384]{1,0:T(8,128)S(1)}, f32[128,384]{1,0:T(8,128)}, u32[]{:S(2)}) copy-start(f32[128,384]{1,0:T(8,128)} %copy-done.7) | copy-start | bytes 589828
  51.9 28.7 %copy-start.15 = (s32[32]{0:T(128)S(1)}, s32[32]{0:T(128)}, u32[]{:S(2)}) copy-start(s32[32]{0:T(128)} %param.12) | copy-start | bytes 388
  51.9 28.7 %copy-start.11 = (s32[384]{0:T(512)S(1)}, s32[384]{0:T(512)}, u32[]{:S(2)}) copy-start(s32[384]{0:T(512)} %param.15) | copy-start | bytes 4612
  51.9 28.7 %copy-start.13 = (s32[384]{0:T(512)S(1)}, s32[384]{0:T(512)}, u32[]{:S(2)}) copy-start(s32[384]{0:T(512)} %param.13) | copy-start | bytes 4612
  51.9 28.7 %copy-start.14 = (s32[32]{0:T(128)S(1)}, s32[32]{0:T(128)}, u32[]{:S(2)}) copy-start(s32[32]{0:T(128)} %param.14) | copy-start | bytes 388
  54.4 1.5 %collective-permute-start.2 = (f32[2,64,384]{2,1,0:T(8,128)S(1)}, f32[2,64,384]{2,1,0:T(8,128)S(1)}, u32[]{:S(2)}, u32[]{:S(2)}) collective-permute-start(f32[2,64,384]{2,1,0:T(8,128)S(1)} %get-tuple-element.36), channel_id=1, source_target_pairs={{0,8},{8,0},{16,24},{24,16},{1,9},{9,1},{17,25},{25,17},{2,10},{10... | collective-permute-start | bytes 589832 | tf_op jit(solution)/shard_map/ppermute | solution.py:337
  58.5 20.6 %all-to-all-start.1 = ((f32[8,16,384]{2,1,0:T(8,128)}), f32[8,16,384]{2,1,0:T(8,128)S(1)}, u32[]{:S(2)}, u32[]{:S(2)}) async-start(f32[8,16,384]{2,1,0:T(8,128)} %bitcast.29), calls=%async_computation.1 | async-start | bytes 393216 | tf_op jit(solution)/shard_map/all_to_all | solution.py:340
  69.8 24.9 %collective-permute-start.11 = (bf16[1152,384]{1,0:T(8,128)(2,1)}, bf16[1152,384]{1,0:T(8,128)(2,1)}, u32[]{:S(2)}, u32[]{:S(2)}) collective-permute-start(bf16[1152,384]{1,0:T(8,128)(2,1)} %collective-permute-done.10.refs_4_), channel_id=1, source_target_pairs={{1,0},{5,4},{9,8},{13,12},{17,16},{21,20},{25,24},{29,28}} | collective-permute-start | bytes 2654216 | tf_op jit(solution)/shard_map/ppermute | solution.py:314
  71.1 23.6 %collective-permute-start.9 = (bf16[1152,384]{1,0:T(8,128)(2,1)}, bf16[1152,384]{1,0:T(8,128)(2,1)}, u32[]{:S(2)}, u32[]{:S(2)}) collective-permute-start(bf16[1152,384]{1,0:T(8,128)(2,1)} %collective-permute-done.8.refs_1_), channel_id=1, source_target_pairs={{2,3},{6,7},{10,11},{14,15},{18,19},{22,23},{26,27},{30,31}} | collective-permute-start | bytes 2654216 | tf_op jit(solution)/shard_map/ppermute | solution.py:313
  79.1 15.6 %collective-permute-start.5 = (bf16[4,64,1152]{2,1,0:T(8,128)(2,1)}, bf16[4,64,1152]{2,1,0:T(8,128)(2,1)}, u32[]{:S(2)}, u32[]{:S(2)}) collective-permute-start(bf16[4,64,1152]{2,1,0:T(8,128)(2,1)} %all-to-all-done), channel_id=1, source_target_pairs={{4,0},{0,4},{5,1},{1,5},{6,2},{2,6},{7,3},{3,7},{12,8},{8,12},{13,... | collective-permute-start | bytes 1769480 | tf_op jit(solution)/shard_map/ppermute | solution.py:270
  81.3 2.4 %copy-start.4 = (f32[128,384]{1,0:T(8,128)S(1)}, f32[128,384]{1,0:T(8,128)}, u32[]{:S(2)}) copy-start(f32[128,384]{1,0:T(8,128)} %copy-done.3) | copy-start | bytes 589828
  81.3 2.5 %copy-start.6 = (f32[128,384]{1,0:T(8,128)S(1)}, f32[128,384]{1,0:T(8,128)}, u32[]{:S(2)}) copy-start(f32[128,384]{1,0:T(8,128)} %copy-done.5) | copy-start | bytes 589828
  83.8 1.3 %copy-start.12 = (f32[384]{0:T(512)S(1)}, f32[384]{0:T(512)}, u32[]{:S(2)}) copy-start(f32[384]{0:T(512)} %param.11) | copy-start | bytes 4612
  83.8 1.3 %copy-start.16 = (f32[32]{0:T(128)S(1)}, f32[32]{0:T(128)}, u32[]{:S(2)}) copy-start(f32[32]{0:T(128)} %param.10) | copy-start | bytes 388
  85.0 1.5 %collective-permute-start.4 = (f32[2,64,384]{2,1,0:T(8,128)S(1)}, f32[2,64,384]{2,1,0:T(8,128)S(1)}, u32[]{:S(2)}, u32[]{:S(2)}) collective-permute-start(f32[2,64,384]{2,1,0:T(8,128)S(1)} %get-tuple-element.44), channel_id=1, source_target_pairs={{0,8},{8,0},{16,24},{24,16},{1,9},{9,1},{17,25},{25,17},{2,10},{10... | collective-permute-start | bytes 589832 | tf_op jit(solution)/shard_map/ppermute | solution.py:337
  86.5 16.8 %copy-start.9 = (s32[32,384]{1,0:T(8,128)S(1)}, s32[32,384]{1,0:T(8,128)}, u32[]{:S(2)}) copy-start(s32[32,384]{1,0:T(8,128)} %fusion.1.keep) | copy-start | bytes 147460
  87.2 14.2 %all-to-all-start.2 = ((f32[8,16,384]{2,1,0:T(8,128)}), f32[8,16,384]{2,1,0:T(8,128)S(1)}, u32[]{:S(2)}, u32[]{:S(2)}) async-start(f32[8,16,384]{2,1,0:T(8,128)} %bitcast.7), calls=%async_computation.2 | async-start | bytes 393216 | tf_op jit(solution)/shard_map/all_to_all | solution.py:340
  97.2 4.3 %collective-permute-start.14 = (f32[32,384]{1,0:T(8,128)S(1)}, f32[32,384]{1,0:T(8,128)S(1)}, u32[]{:S(2)}, u32[]{:S(2)}) collective-permute-start(f32[32,384]{1,0:T(8,128)S(1)} %get-tuple-element.52), channel_id=1, source_target_pairs={{0,8},{8,0},{16,24},{24,16},{1,9},{9,1},{17,25},{25,17},{2,10},{10... | collective-permute-start | bytes 147464 | tf_op jit(solution)/shard_map/ppermute | solution.py:363
  97.3 4.2 %collective-permute-start.12 = (f32[32,384]{1,0:T(8,128)S(1)}, f32[32,384]{1,0:T(8,128)S(1)}, u32[]{:S(2)}, u32[]{:S(2)}) collective-permute-start(f32[32,384]{1,0:T(8,128)S(1)} %get-tuple-element.56), channel_id=1, source_target_pairs={{0,24},{8,16},{16,8},{24,0},{1,25},{9,17},{17,9},{25,1},{2,26},{10... | collective-permute-start | bytes 147464 | tf_op jit(solution)/shard_map/ppermute | solution.py:363
  99.2 4.1 %collective-permute-start.13 = (f32[32,384]{1,0:T(8,128)S(1)}, f32[32,384]{1,0:T(8,128)S(1)}, u32[]{:S(2)}, u32[]{:S(2)}) collective-permute-start(f32[32,384]{1,0:T(8,128)S(1)} %get-tuple-element.55), channel_id=1, source_target_pairs={{0,16},{8,24},{16,0},{24,8},{1,17},{9,25},{17,1},{25,9},{2,18},{10... | collective-permute-start | bytes 147464 | tf_op jit(solution)/shard_map/ppermute | solution.py:363

commit v9 on v7

--- a/solution.py
+++ b/solution.py
@@ -137,7 +137,7 @@
     )(in_hbm(rows))
 
 
-def turned_products(me, core, own, so_far, got, rows, n_core):
+def turned_products(me, core, own, so_far, got, rows, n_core, n_dep):
     n_up = 1 + len(got)
     states, k = got[0].shape
     width = rows.shape[1]
@@ -163,13 +163,13 @@
             )
 
         def put(slot, product):
-            by_core = product.reshape(n_core, share, width)
+            by_core = product.reshape(n_core, n_dep, share // n_dep, width)
             for c in range(n_core):
                 for t, out in enumerate(outs):
 
                     @pl.when(lax.rem(core_at[0] + t, n_core) == c)
                     def _():
-                        out[slot] = by_core[c]
+                        out[:, slot] = by_core[c]
 
         put(me_at[0], mine[...])
         totals = [before[...] for before in befores]
@@ -185,7 +185,7 @@
         body,
         in_specs=[pl.BlockSpec(memory_space=pltpu.SMEM)] * 2 + [vmem] * (n_up + 1) + [hbm] * (n_up - 1),
         out_specs=[vmem] * n_core,
-        out_shape=[jax.ShapeDtypeStruct((n_up, share, width), jnp.float32)] * n_core,
+        out_shape=[jax.ShapeDtypeStruct((n_dep, n_up, share // n_dep, width), jnp.float32)] * n_core,
         scratch_shapes=[
             pltpu.VMEM((n_up - 1, steps, states, block), got[0].dtype),
             pltpu.SemaphoreType.DMA((n_up - 1, steps)),
@@ -239,7 +239,7 @@
 def make_local(n_low, n_up, n_dep):
     n_core = n_low // n_up
     others = range(1, n_up)
-    same_core = [[(y * n_core + c) * n_dep + z for y in range(n_up) for z in range(n_dep)] for c in range(n_core)]
+    same_core = [[(y * n_core + c) * n_dep + z for z in range(n_dep) for y in range(n_up)] for c in range(n_core)]
 
     def shifted(x, shift):
         return lax.ppermute(x, "upper", [((u + shift) % n_up, u) for u in range(n_up)])
@@ -305,7 +305,7 @@
             pass_on(*(after(held, *own, *so_far[0]) if i == 1 else held))
 
         def reduced(i, got, main_held, *others_first):
-            mine_of, *for_others = turned_products(me, my_core, own[i], [x[i] for x in so_far], got, main_held, n_core)
+            mine_of, *for_others = turned_products(me, my_core, own[i], [x[i] for x in so_far], got, main_held, n_core, n_dep)
             total = mine_of
             for k, leaving in enumerate(for_others, 1):
                 pairs = [(low(y, c), low(y, (c + k) % n_core)) for y in range(n_up) for c in range(n_core)]

time: 105 us -> 105 us (level)
    all_to_all x2, waiting for transfers between devices: 9.58 us -> 8.32 us  [reduced(): lax.all_to_all(by_owner, OWNERS, 0, 0, axis_index_groups=same_core)]
  transfers between devices with their start and end apart: 18 -> 18, of which waited for: 10 -> 11; matrix products, arithmetic and copies ran while one was open for 7% -> 7% of each run, Pallas kernels for 23% -> 23%
where the time goes in v9:
time: 105 us; the launch traced here: 104 us
  starting transfers between devices  41.4 us (39%)
  waiting for transfers between devices  24.7 us (24%)
  Pallas kernels  23.8 us (23%)
  local copies, waits for them, and re-layouts  9.28 us (9%)
  other arithmetic  4.08 us (4%)
    all_to_all x2, starting transfers between devices, reduced(): lax.all_to_all(by_owner, OWNERS, 0, 0, axis_index_groups=same_core)  15.2 us
    all_to_all x2, waiting for transfers between devices, reduced(): lax.all_to_all(by_owner, OWNERS, 0, 0, axis_index_groups=same_core)  8.32 us
    ppermute x3, starting transfers between devices, pass_on(): forward.append(lax.ppermute(held_up, 'depth', up[i:]))  7.25 us
    pallas_call x2, Pallas kernels, rows_product(): pl.pallas_call(body, grid=(steps,), in_specs=[pl.BlockSpec((block, states...  7 us
    all_to_all x1, starting transfers between devices, local(): sorted_tail = lax.all_to_all(tail_rows, 'depth', 0, 0)  6.85 us
    pallas_call x1, Pallas kernels, turn(): pl.pallas_call(body, grid=(steps,), in_specs=[pl.BlockSpec((block, cols),...  6.05 us
    ppermute x4, starting transfers between devices, shifted(): lax.ppermute(x, 'upper', [((u + shift) % n_up, u) for u in range(n_up)])  6.03 us
    ppermute x4, waiting for transfers between devices, shifted(): lax.ppermute(x, 'upper', [((u + shift) % n_up, u) for u in range(n_up)])  5.9 us
  transfers between devices with their start and end apart: 18, of which 11 were waited for; matrix products, arithmetic and copies ran while one was open for 7% of the time, Pallas kernels for 23%

profile of v9, /device:TPU:0, one launch (start us, length us, event | category | flops | bytes accessed | tf_op | source)
XLA Modules:
  0.0 103.6 jit_solution(715155272414441833)
XLA Ops:
  0.0 1.0 %slice_bitcast_fusion.2 = bf16[896,256]{1,0:T(8,128)(2,1)S(1)} fusion(bf16[1,8192,256]{2,1,0:T(8,128)(2,1)} %param.8), kind=kLoop, calls=%fused_computation.2 | loop fusion | bytes 917504 | tf_op jit(solution)/shard_map/slice | solution.py:291
  1.1 3.0 %collective-permute-start = (bf16[896,256]{1,0:T(8,128)(2,1)S(1)}, bf16[896,256]{1,0:T(8,128)(2,1)S(1)}, u32[]{:S(2)}, u32[]{:S(2)}) collective-permute-start(bf16[896,256]{1,0:T(8,128)(2,1)S(1)} %slice_bitcast_fusion.2), channel_id=1, source_target_pairs={{4,0},{0,4},{5,1},{1,5},{6,2},{2,6},{7,3},{3,7},{12,8},{8,12},{13,... | collective-permute-start | bytes 1376264 | tf_op jit(solution)/shard_map/ppermute | solution.py:245
  4.1 6.0 %shard_map.82 = (bf16[128,6144]{1,0:T(8,128)(2,1)}, bf16[128,6144]{1,0:T(8,128)(2,1)S(1)}, bf16[4,64,1152]{2,1,0:T(8,128)(2,1)}) custom-call(bf16[8192,256]{1,0:T(8,128)(2,1)} %bitcast.23, bf16[8192,256]{1,0:T(8,128)(2,1)} %bitcast.24), custom_call_target="tpu_custom_call" | custom-call | bytes 30000 | tf_op jit(solution)/shard_map/pallas_call | solution.py:60
  10.1 0.0 collective-permute-start.1
  10.1 1.8 %slice_bitcast_fusion.mid = bf16[1152,384]{1,0:T(8,128)(2,1)S(1)} fusion(bf16[1,8192,384]{2,1,0:T(8,128)(2,1)} %param.9), kind=kLoop, calls=%fused_computation | loop fusion | bytes 1769472 | tf_op jit(solution)/shard_map/slice | solution.py:296
  12.0 3.5 %collective-permute-done.low = bf16[896,256]{1,0:T(8,128)(2,1)S(1)} collective-permute-done((bf16[896,256]{1,0:T(8,128)(2,1)S(1)}, bf16[896,256]{1,0:T(8,128)(2,1)S(1)}, u32[]{:S(2)}, u32[]{:S(2)}) %collective-permute-start) | collective-permute-done | bytes 458784 | tf_op jit(solution)/shard_map/ppermute | solution.py:245
  15.4 0.0 copy-done.9
  15.4 0.8 copy-done.1
  16.2 4.1 %collective-permute-start.6 = (bf16[1152,384]{1,0:T(8,128)(2,1)S(1)}, bf16[1152,384]{1,0:T(8,128)(2,1)S(1)}, u32[]{:S(2)}, u32[]{:S(2)}) collective-permute-start(bf16[1152,384]{1,0:T(8,128)(2,1)S(1)} %slice_bitcast_fusion.mid), channel_id=1, source_target_pairs={{0,1},{1,2},{2,3},{4,5},{5,6},{6,7},{8,9},{9,10},{10,11},{12,13},{... | collective-permute-start | bytes 2654216 | tf_op jit(solution)/shard_map/ppermute | solution.py:288
  20.3 1.3 %collective-permute-start.7 = (bf16[1152,384]{1,0:T(8,128)(2,1)S(1)}, bf16[1152,384]{1,0:T(8,128)(2,1)}, u32[]{:S(2)}, u32[]{:S(2)}) collective-permute-start(bf16[1152,384]{1,0:T(8,128)(2,1)S(1)} %slice_bitcast_fusion.mid), channel_id=1, source_target_pairs={{1,0},{2,1},{3,2},{5,4},{6,5},{7,6},{9,8},{10,9},{11,10},{13,12},{... | collective-permute-start | bytes 2654216 | tf_op jit(solution)/shard_map/ppermute | solution.py:289
  21.6 6.8 %all-to-all-start = ((bf16[4,64,1152]{2,1,0:T(8,128)(2,1)}), bf16[4,64,1152]{2,1,0:T(8,128)(2,1)}, u32[]{:S(2)}, u32[]{:S(2)}) async-start(bf16[4,64,1152]{2,1,0:T(8,128)(2,1)} %get-tuple-element.37), calls=%async_computation | async-start | bytes 1179648 | tf_op jit(solution)/shard_map/all_to_all | solution.py:298
  28.4 1.5 %collective-permute-start.3 = (bf16[128,6144]{1,0:T(8,128)(2,1)}, bf16[128,6144]{1,0:T(8,128)(2,1)S(1)}, u32[]{:S(2)}, u32[]{:S(2)}) collective-permute-start(bf16[128,6144]{1,0:T(8,128)(2,1)} %copy-done.9), channel_id=1, source_target_pairs={{4,0},{0,4},{5,1},{1,5},{6,2},{2,6},{7,3},{3,7},{12,8},{8,12},{13,... | collective-permute-start | bytes 4718600 | tf_op jit(solution)/shard_map/ppermute | solution.py:245
  29.9 2.0 %slice_bitcast_fusion.1.up = bf16[896,384]{1,0:T(8,128)(2,1)} fusion(bf16[1,8192,384]{2,1,0:T(8,128)(2,1)} %param.9), kind=kLoop, calls=%fused_computation.1 | loop fusion | bytes 1376256 | tf_op jit(solution)/shard_map/slice | solution.py:301
  32.0 2.2 %copy-done = bf16[1,8192,256]{2,1,0:T(8,128)(2,1)S(1)} copy-done((bf16[1,8192,256]{2,1,0:T(8,128)(2,1)S(1)}, bf16[1,8192,256]{2,1,0:T(8,128)(2,1)}, u32[]{:S(2)}) %copy-start) | copy-done | bytes 4194328
  34.2 5.4 %shard_map.83 = (f32[128,384]{1,0:T(8,128)S(1)}, f32[128,384]{1,0:T(8,128)S(1)}) custom-call(bf16[8192,256]{1,0:T(8,128)(2,1)S(1)} %bitcast.25, bf16[8192,384]{1,0:T(8,128)(2,1)} %bitcast.26), custom_call_target="tpu_custom_call" | custom-call | bytes 30000 | tf_op jit(solution)/shard_map/pallas_call | solution.py:105
  39.5 0.0 copy-done.2
  39.5 0.0 copy-start.5
  39.6 1.6 %shard_map.84 = (f32[128,384]{1,0:T(8,128)S(1)}, f32[128,384]{1,0:T(8,128)S(1)}) custom-call(bf16[896,256]{1,0:T(8,128)(2,1)S(1)} %copy-done.2, bf16[896,384]{1,0:T(8,128)(2,1)} %slice_bitcast_fusion.1.up), custom_call_target="tpu_custom_call" | custom-call | bytes 30000 | tf_op jit(solution)/shard_map/pallas_call | solution.py:105
  41.2 0.0 copy-start.3
  41.2 0.7 copy-done.3
  41.9 0.7 copy-done.7
  42.6 0.0 collective-permute-done.6.refs_0_
  42.6 2.9 %collective-permute-done.7.refs_3_ = bf16[1152,384]{1,0:T(8,128)(2,1)} collective-permute-done((bf16[1152,384]{1,0:T(8,128)(2,1)S(1)}, bf16[1152,384]{1,0:T(8,128)(2,1)}, u32[]{:S(2)}, u32[]{:S(2)}) %collective-permute-start.7) | collective-permute-done | bytes 884768 | tf_op jit(solution)/shard_map/ppermute | solution.py:289
  45.5 0.0 copy-done.5
  45.5 1.6 %collective-permute-start.8 = (bf16[1152,384]{1,0:T(8,128)(2,1)S(1)}, bf16[1152,384]{1,0:T(8,128)(2,1)}, u32[]{:S(2)}, u32[]{:S(2)}) collective-permute-start(bf16[1152,384]{1,0:T(8,128)(2,1)S(1)} %collective-permute-done.6.refs_0_), channel_id=1, source_target_pairs={{1,2},{2,3},{5,6},{6,7},{9,10},{10,11},{13,14},{14,15},{17,18},{18... | collective-permute-start | bytes 2654216 | tf_op jit(solution)/shard_map/ppermute | solution.py:288
  47.1 1.3 %collective-permute-start.10 = (bf16[1152,384]{1,0:T(8,128)(2,1)}, bf16[1152,384]{1,0:T(8,128)(2,1)}, u32[]{:S(2)}, u32[]{:S(2)}) collective-permute-start(bf16[1152,384]{1,0:T(8,128)(2,1)} %collective-permute-done.7.refs_3_), channel_id=1, source_target_pairs={{1,0},{2,1},{5,4},{6,5},{9,8},{10,9},{13,12},{14,13},{17,16},{18,1... | collective-permute-start | bytes 2654216 | tf_op jit(solution)/shard_map/ppermute | solution.py:289
  48.4 0.0 copy-start.6
  48.4 0.0 copy-start.8
  48.4 2.4 %shard_map.85.up = bf16[6144,384]{1,0:T(8,128)(2,1)S(1)} custom-call(bf16[8192,384]{1,0:T(8,128)(2,1)} %bitcast.27), custom_call_target="tpu_custom_call" | custom-call | bytes 30000 | tf_op jit(solution)/shard_map/pallas_call | solution.py:129
  50.8 0.0 collective-permute-done.1.refs_1_
  50.8 2.4 %shard_map.86 = (f32[4,2,16,384]{3,2,1,0:T(8,128)S(1)}, f32[4,2,16,384]{3,2,1,0:T(8,128)S(1)}) custom-call(s32[1]{0:T(128)} %bitcast.me_at, s32[1]{0:T(128)} %bitcast.1.core_at, f32[128,384]{1,0:T(8,128)S(1)} %copy-done.6, bf16[6144,384]{1,0:T(8,128)(2,1)S(1)} %shard_map.85.up, f32[128,384]{1,0:T(8,128)S(1)} %copy-done.8, ...), custom_call_target="tpu_custom_call" | custom-call | bytes 30000 | tf_op jit(solution)/shard_map/pallas_call | solution.py:184
  53.2 0.1 collective-permute-start.2
  53.3 1.4 %collective-permute-done.2 = f32[4,2,16,384]{3,2,1,0:T(8,128)S(1)} collective-permute-done((f32[4,2,16,384]{3,2,1,0:T(8,128)S(1)}, f32[4,2,16,384]{3,2,1,0:T(8,128)S(1)}, u32[]{:S(2)}, u32[]{:S(2)}) %collective-permute-start.2) | collective-permute-done | bytes 196640 | tf_op jit(solution)/shard_map/ppermute | solution.py:312
  54.8 0.7 add.75
  55.5 3.0 %all-to-all-done = bf16[4,64,1152]{2,1,0:T(8,128)(2,1)} async-done(((bf16[4,64,1152]{2,1,0:T(8,128)(2,1)}), bf16[4,64,1152]{2,1,0:T(8,128)(2,1)}, u32[]{:S(2)}, u32[]{:S(2)}) %all-to-all-start) | async-done | bytes 589856 | tf_op jit(solution)/shard_map/all_to_all | solution.py:298
  58.5 8.7 %all-to-all-start.1 = ((f32[8,16,384]{2,1,0:T(8,128)}), f32[8,16,384]{2,1,0:T(8,128)}, u32[]{:S(2)}, u32[]{:S(2)}) async-start(f32[8,16,384]{2,1,0:T(8,128)} %bitcast.29), calls=%async_computation.1 | async-start | bytes 393216 | tf_op jit(solution)/shard_map/all_to_all | solution.py:315
  67.1 0.0 collective-permute-done.8.refs_1_
  67.1 1.6 %collective-permute-start.9 = (bf16[1152,384]{1,0:T(8,128)(2,1)}, bf16[1152,384]{1,0:T(8,128)(2,1)}, u32[]{:S(2)}, u32[]{:S(2)}) collective-permute-start(bf16[1152,384]{1,0:T(8,128)(2,1)} %collective-permute-done.8.refs_1_), channel_id=1, source_target_pairs={{2,3},{6,7},{10,11},{14,15},{18,19},{22,23},{26,27},{30,31}} | collective-permute-start | bytes 2654216 | tf_op jit(solution)/shard_map/ppermute | solution.py:288
  68.7 1.1 %collective-permute-done.10.refs_4_ = bf16[1152,384]{1,0:T(8,128)(2,1)} collective-permute-done((bf16[1152,384]{1,0:T(8,128)(2,1)}, bf16[1152,384]{1,0:T(8,128)(2,1)}, u32[]{:S(2)}, u32[]{:S(2)}) %collective-permute-start.10) | collective-permute-done | bytes 884768 | tf_op jit(solution)/shard_map/ppermute | solution.py:289
  69.8 1.3 %collective-permute-start.11 = (bf16[1152,384]{1,0:T(8,128)(2,1)}, bf16[1152,384]{1,0:T(8,128)(2,1)}, u32[]{:S(2)}, u32[]{:S(2)}) collective-permute-start(bf16[1152,384]{1,0:T(8,128)(2,1)} %collective-permute-done.10.refs_4_), channel_id=1, source_target_pairs={{1,0},{5,4},{9,8},{13,12},{17,16},{21,20},{25,24},{29,28}} | collective-permute-start | bytes 2654216 | tf_op jit(solution)/shard_map/ppermute | solution.py:289
  71.1 7.3 %all-to-all-done.1 = f32[8,16,384]{2,1,0:T(8,128)} async-done(((f32[8,16,384]{2,1,0:T(8,128)}), f32[8,16,384]{2,1,0:T(8,128)}, u32[]{:S(2)}, u32[]{:S(2)}) %all-to-all-start.1) | async-done | bytes 196640 | tf_op jit(solution)/shard_map/all_to_all | solution.py:315
  78.4 1.5 %collective-permute-start.5 = (bf16[4,64,1152]{2,1,0:T(8,128)(2,1)}, bf16[4,64,1152]{2,1,0:T(8,128)(2,1)}, u32[]{:S(2)}, u32[]{:S(2)}) collective-permute-start(bf16[4,64,1152]{2,1,0:T(8,128)(2,1)} %all-to-all-done), channel_id=1, source_target_pairs={{4,0},{0,4},{5,1},{1,5},{6,2},{2,6},{7,3},{3,7},{12,8},{8,12},{13,... | collective-permute-start | bytes 1769480 | tf_op jit(solution)/shard_map/ppermute | solution.py:245
  79.9 2.4 %shard_map.87.up = bf16[6144,384]{1,0:T(8,128)(2,1)S(1)} custom-call(bf16[8192,384]{1,0:T(8,128)(2,1)} %bitcast.28), custom_call_target="tpu_custom_call" | custom-call | bytes 30000 | tf_op jit(solution)/shard_map/pallas_call | solution.py:129
  82.3 0.0 copy-start.10
  82.3 0.5 collective-permute-done.3.refs_1_
  82.8 1.2 %shard_map.88 = (f32[4,2,16,384]{3,2,1,0:T(8,128)S(1)}, f32[4,2,16,384]{3,2,1,0:T(8,128)S(1)}) custom-call(s32[1]{0:T(128)} %bitcast.me_at, s32[1]{0:T(128)} %bitcast.1.core_at, f32[128,384]{1,0:T(8,128)S(1)} %get-tuple-element.39.mine, bf16[6144,384]{1,0:T(8,128)(2,1)S(1)} %shard_map.87.up, f32[128,384]{1,0:T(8,128)S(1)} %copy-done.4, ...), custom_call_target="tpu_custom_call" | custom-call | bytes 30000 | tf_op jit(solution)/shard_map/pallas_call | solution.py:184
  84.0 0.1 collective-permute-start.4
  84.1 1.4 %collective-permute-done.4 = f32[4,2,16,384]{3,2,1,0:T(8,128)S(1)} collective-permute-done((f32[4,2,16,384]{3,2,1,0:T(8,128)S(1)}, f32[4,2,16,384]{3,2,1,0:T(8,128)S(1)}, u32[]{:S(2)}, u32[]{:S(2)}) %collective-permute-start.4) | collective-permute-done | bytes 196640 | tf_op jit(solution)/shard_map/ppermute | solution.py:312
  85.5 0.7 add.76
  86.2 6.5 %all-to-all-start.2 = ((f32[8,16,384]{2,1,0:T(8,128)}), f32[8,16,384]{2,1,0:T(8,128)}, u32[]{:S(2)}, u32[]{:S(2)}) async-start(f32[8,16,384]{2,1,0:T(8,128)} %bitcast.7), calls=%async_computation.2 | async-start | bytes 393216 | tf_op jit(solution)/shard_map/all_to_all | solution.py:315
  92.8 2.0 %collective-permute-done.5.low = bf16[4,64,1152]{2,1,0:T(8,128)(2,1)} collective-permute-done((bf16[4,64,1152]{2,1,0:T(8,128)(2,1)}, bf16[4,64,1152]{2,1,0:T(8,128)(2,1)}, u32[]{:S(2)}, u32[]{:S(2)}) %collective-permute-start.5) | collective-permute-done | bytes 589856 | tf_op jit(solution)/shard_map/ppermute | solution.py:245
  94.7 0.0 collective-permute-done.9.refs_2_
  94.7 0.0 collective-permute-done.11.refs_5_
  94.7 2.4 %shard_map.89 = f32[64,384]{1,0:T(8,128)S(1)} custom-call(s32[1]{0:T(128)} %bitcast.8.at, bf16[4,64,1152]{2,1,0:T(8,128)(2,1)} %collective-permute-done.5.low, bf16[1152,384]{1,0:T(8,128)(2,1)S(1)} %slice_bitcast_fusion.mid, bf16[1152,384]{1,0:T(8,128)(2,1)S(1)} %collective-permute-done.6.refs_0_, bf16[1152,384]{1,0:T(8,128)(2,1)} %collective-permute-done.8.refs_1_, ...), custom_call_target="tpu_custom_call" | custom-call | bytes 30000 | tf_op jit(solution)/shard_map/pallas_call | solution.py:224
  97.2 0.1 collective-permute-start.14
  97.3 1.8 %collective-permute-start.13 = (f32[32,384]{1,0:T(8,128)S(1)}, f32[32,384]{1,0:T(8,128)S(1)}, u32[]{:S(2)}, u32[]{:S(2)}) collective-permute-start(f32[32,384]{1,0:T(8,128)S(1)} %get-tuple-element.52), channel_id=1, source_target_pairs={{0,16},{8,24},{16,0},{24,8},{1,17},{9,25},{17,1},{25,9},{2,18},{10... | collective-permute-start | bytes 147464 | tf_op jit(solution)/shard_map/ppermute | solution.py:340
  99.1 0.2 collective-permute-start.12
  99.3 0.9 reduce_sum.18
  100.2 1.0 all-to-all-done.2
  101.2 0.9 reduce_sum.19
  102.2 0.0 collective-permute-done.14
  102.2 0.0 collective-permute-done.13
  102.2 0.7 collective-permute-done.12
  102.9 0.7 fusion.2
  (25 shorter events, 0.1 us)
Async XLA Ops:
  1.1 14.4 %collective-permute-start = (bf16[896,256]{1,0:T(8,128)(2,1)S(1)}, bf16[896,256]{1,0:T(8,128)(2,1)S(1)}, u32[]{:S(2)}, u32[]{:S(2)}) collective-permute-start(bf16[896,256]{1,0:T(8,128)(2,1)S(1)} %slice_bitcast_fusion.2), channel_id=1, source_target_pairs={{4,0},{0,4},{5,1},{1,5},{6,2},{2,6},{7,3},{3,7},{12,8},{8,12},{13,... | collective-permute-start | bytes 1376264 | tf_op jit(solution)/shard_map/ppermute | solution.py:245
  10.1 5.3 %copy-start.9 = (bf16[128,6144]{1,0:T(8,128)(2,1)}, bf16[128,6144]{1,0:T(8,128)(2,1)S(1)}, u32[]{:S(2)}) copy-start(bf16[128,6144]{1,0:T(8,128)(2,1)S(1)} %get-tuple-element.42) | copy-start | bytes 4718596
  10.1 40.7 %collective-permute-start.1 = (bf16[128,6144]{1,0:T(8,128)(2,1)}, bf16[128,6144]{1,0:T(8,128)(2,1)}, u32[]{:S(2)}, u32[]{:S(2)}) collective-permute-start(bf16[128,6144]{1,0:T(8,128)(2,1)} %get-tuple-element.29), channel_id=1, source_target_pairs={{4,0},{0,4},{5,1},{1,5},{6,2},{2,6},{7,3},{3,7},{12,8},{8,12},{13,... | collective-permute-start | bytes 4718600 | tf_op jit(solution)/shard_map/ppermute | solution.py:245
  15.4 0.8 copy-start.1
  16.2 26.4 %collective-permute-start.6 = (bf16[1152,384]{1,0:T(8,128)(2,1)S(1)}, bf16[1152,384]{1,0:T(8,128)(2,1)S(1)}, u32[]{:S(2)}, u32[]{:S(2)}) collective-permute-start(bf16[1152,384]{1,0:T(8,128)(2,1)S(1)} %slice_bitcast_fusion.mid), channel_id=1, source_target_pairs={{0,1},{1,2},{2,3},{4,5},{5,6},{6,7},{8,9},{9,10},{10,11},{12,13},{... | collective-permute-start | bytes 2654216 | tf_op jit(solution)/shard_map/ppermute | solution.py:288
  20.3 25.2 %collective-permute-start.7 = (bf16[1152,384]{1,0:T(8,128)(2,1)S(1)}, bf16[1152,384]{1,0:T(8,128)(2,1)}, u32[]{:S(2)}, u32[]{:S(2)}) collective-permute-start(bf16[1152,384]{1,0:T(8,128)(2,1)S(1)} %slice_bitcast_fusion.mid), channel_id=1, source_target_pairs={{1,0},{2,1},{3,2},{5,4},{6,5},{7,6},{9,8},{10,9},{11,10},{13,12},{... | collective-permute-start | bytes 2654216 | tf_op jit(solution)/shard_map/ppermute | solution.py:289
  21.6 36.9 %all-to-all-start = ((bf16[4,64,1152]{2,1,0:T(8,128)(2,1)}), bf16[4,64,1152]{2,1,0:T(8,128)(2,1)}, u32[]{:S(2)}, u32[]{:S(2)}) async-start(bf16[4,64,1152]{2,1,0:T(8,128)(2,1)} %get-tuple-element.37), calls=%async_computation | async-start | bytes 1179648 | tf_op jit(solution)/shard_map/all_to_all | solution.py:298
  28.4 54.4 %collective-permute-start.3 = (bf16[128,6144]{1,0:T(8,128)(2,1)}, bf16[128,6144]{1,0:T(8,128)(2,1)S(1)}, u32[]{:S(2)}, u32[]{:S(2)}) collective-permute-start(bf16[128,6144]{1,0:T(8,128)(2,1)} %copy-done.9), channel_id=1, source_target_pairs={{4,0},{0,4},{5,1},{1,5},{6,2},{2,6},{7,3},{3,7},{12,8},{8,12},{13,... | collective-permute-start | bytes 4718600 | tf_op jit(solution)/shard_map/ppermute | solution.py:245
  32.0 2.2 %copy-start = (bf16[1,8192,256]{2,1,0:T(8,128)(2,1)S(1)}, bf16[1,8192,256]{2,1,0:T(8,128)(2,1)}, u32[]{:S(2)}) copy-start(bf16[1,8192,256]{2,1,0:T(8,128)(2,1)} %param.8) | copy-start | bytes 12582916
  34.1 5.4 %copy-start.2 = (bf16[896,256]{1,0:T(8,128)(2,1)S(1)}, bf16[896,256]{1,0:T(8,128)(2,1)}, u32[]{:S(2)}) copy-start(bf16[896,256]{1,0:T(8,128)(2,1)} %copy-done.1) | copy-start | bytes 1376260
  39.5 5.9 %copy-start.5 = (f32[128,384]{1,0:T(8,128)}, f32[128,384]{1,0:T(8,128)S(1)}, u32[]{:S(2)}) copy-start(f32[128,384]{1,0:T(8,128)S(1)} %get-tuple-element.31.mine) | copy-start | bytes 589828
  41.2 0.7 copy-start.3
  41.9 0.7 copy-start.7
  45.5 21.6 %collective-permute-start.8 = (bf16[1152,384]{1,0:T(8,128)(2,1)S(1)}, bf16[1152,384]{1,0:T(8,128)(2,1)}, u32[]{:S(2)}, u32[]{:S(2)}) collective-permute-start(bf16[1152,384]{1,0:T(8,128)(2,1)S(1)} %collective-permute-done.6.refs_0_), channel_id=1, source_target_pairs={{1,2},{2,3},{5,6},{6,7},{9,10},{10,11},{13,14},{14,15},{17,18},{18... | collective-permute-start | bytes 2654216 | tf_op jit(solution)/shard_map/ppermute | solution.py:288
  47.1 22.8 %collective-permute-start.10 = (bf16[1152,384]{1,0:T(8,128)(2,1)}, bf16[1152,384]{1,0:T(8,128)(2,1)}, u32[]{:S(2)}, u32[]{:S(2)}) collective-permute-start(bf16[1152,384]{1,0:T(8,128)(2,1)} %collective-permute-done.7.refs_3_), channel_id=1, source_target_pairs={{1,0},{2,1},{5,4},{6,5},{9,8},{10,9},{13,12},{14,13},{17,16},{18,1... | collective-permute-start | bytes 2654216 | tf_op jit(solution)/shard_map/ppermute | solution.py:289
  48.4 2.4 %copy-start.6 = (f32[128,384]{1,0:T(8,128)S(1)}, f32[128,384]{1,0:T(8,128)}, u32[]{:S(2)}) copy-start(f32[128,384]{1,0:T(8,128)} %copy-done.5) | copy-start | bytes 589828
  48.4 2.4 %copy-start.8 = (f32[128,384]{1,0:T(8,128)S(1)}, f32[128,384]{1,0:T(8,128)}, u32[]{:S(2)}) copy-start(f32[128,384]{1,0:T(8,128)} %copy-done.7) | copy-start | bytes 589828
  53.2 1.5 %collective-permute-start.2 = (f32[4,2,16,384]{3,2,1,0:T(8,128)S(1)}, f32[4,2,16,384]{3,2,1,0:T(8,128)S(1)}, u32[]{:S(2)}, u32[]{:S(2)}) collective-permute-start(f32[4,2,16,384]{3,2,1,0:T(8,128)S(1)} %get-tuple-element.36), channel_id=1, source_target_pairs={{0,8},{8,0},{16,24},{24,16},{1,9},{9,1},{17,25},{25,17},{2,10},{10... | collective-permute-start | bytes 589832 | tf_op jit(solution)/shard_map/ppermute | solution.py:312
  58.5 19.9 %all-to-all-start.1 = ((f32[8,16,384]{2,1,0:T(8,128)}), f32[8,16,384]{2,1,0:T(8,128)}, u32[]{:S(2)}, u32[]{:S(2)}) async-start(f32[8,16,384]{2,1,0:T(8,128)} %bitcast.29), calls=%async_computation.1 | async-start | bytes 393216 | tf_op jit(solution)/shard_map/all_to_all | solution.py:315
  67.1 27.6 %collective-permute-start.9 = (bf16[1152,384]{1,0:T(8,128)(2,1)}, bf16[1152,384]{1,0:T(8,128)(2,1)}, u32[]{:S(2)}, u32[]{:S(2)}) collective-permute-start(bf16[1152,384]{1,0:T(8,128)(2,1)} %collective-permute-done.8.refs_1_), channel_id=1, source_target_pairs={{2,3},{6,7},{10,11},{14,15},{18,19},{22,23},{26,27},{30,31}} | collective-permute-start | bytes 2654216 | tf_op jit(solution)/shard_map/ppermute | solution.py:288
  69.8 24.9 %collective-permute-start.11 = (bf16[1152,384]{1,0:T(8,128)(2,1)}, bf16[1152,384]{1,0:T(8,128)(2,1)}, u32[]{:S(2)}, u32[]{:S(2)}) collective-permute-start(bf16[1152,384]{1,0:T(8,128)(2,1)} %collective-permute-done.10.refs_4_), channel_id=1, source_target_pairs={{1,0},{5,4},{9,8},{13,12},{17,16},{21,20},{25,24},{29,28}} | collective-permute-start | bytes 2654216 | tf_op jit(solution)/shard_map/ppermute | solution.py:289
  78.4 16.3 %collective-permute-start.5 = (bf16[4,64,1152]{2,1,0:T(8,128)(2,1)}, bf16[4,64,1152]{2,1,0:T(8,128)(2,1)}, u32[]{:S(2)}, u32[]{:S(2)}) collective-permute-start(bf16[4,64,1152]{2,1,0:T(8,128)(2,1)} %all-to-all-done), channel_id=1, source_target_pairs={{4,0},{0,4},{5,1},{1,5},{6,2},{2,6},{7,3},{3,7},{12,8},{8,12},{13,... | collective-permute-start | bytes 1769480 | tf_op jit(solution)/shard_map/ppermute | solution.py:245
  79.9 2.9 %copy-start.4 = (f32[128,384]{1,0:T(8,128)S(1)}, f32[128,384]{1,0:T(8,128)}, u32[]{:S(2)}) copy-start(f32[128,384]{1,0:T(8,128)} %copy-done.3) | copy-start | bytes 589828
  82.3 1.8 %copy-start.10 = (s32[384]{0:T(512)S(1)}, s32[384]{0:T(512)}, u32[]{:S(2)}) copy-start(s32[384]{0:T(512)} %param.15) | copy-start | bytes 4612
  84.0 1.5 %collective-permute-start.4 = (f32[4,2,16,384]{3,2,1,0:T(8,128)S(1)}, f32[4,2,16,384]{3,2,1,0:T(8,128)S(1)}, u32[]{:S(2)}, u32[]{:S(2)}) collective-permute-start(f32[4,2,16,384]{3,2,1,0:T(8,128)S(1)} %get-tuple-element.44), channel_id=1, source_target_pairs={{0,8},{8,0},{16,24},{24,16},{1,9},{9,1},{17,25},{25,17},{2,10},{10... | collective-permute-start | bytes 589832 | tf_op jit(solution)/shard_map/ppermute | solution.py:312
  85.5 13.8 %copy-start.15 = (s32[32]{0:T(128)S(1)}, s32[32]{0:T(128)}, u32[]{:S(2)}) copy-start(s32[32]{0:T(128)} %param.12) | copy-start | bytes 388
  86.2 16.7 %copy-start.11 = (f32[384]{0:T(512)S(1)}, f32[384]{0:T(512)}, u32[]{:S(2)}) copy-start(f32[384]{0:T(512)} %param.11) | copy-start | bytes 4612
  86.2 16.7 %copy-start.12 = (s32[384]{0:T(512)S(1)}, s32[384]{0:T(512)}, u32[]{:S(2)}) copy-start(s32[384]{0:T(512)} %param.13) | copy-start | bytes 4612
  86.2 16.7 %copy-start.13 = (f32[32]{0:T(128)S(1)}, f32[32]{0:T(128)}, u32[]{:S(2)}) copy-start(f32[32]{0:T(128)} %param.10) | copy-start | bytes 388
  86.2 16.7 %copy-start.14 = (s32[32]{0:T(128)S(1)}, s32[32]{0:T(128)}, u32[]{:S(2)}) copy-start(s32[32]{0:T(128)} %param.14) | copy-start | bytes 388
  86.2 15.0 %all-to-all-start.2 = ((f32[8,16,384]{2,1,0:T(8,128)}), f32[8,16,384]{2,1,0:T(8,128)}, u32[]{:S(2)}, u32[]{:S(2)}) async-start(f32[8,16,384]{2,1,0:T(8,128)} %bitcast.7), calls=%async_computation.2 | async-start | bytes 393216 | tf_op jit(solution)/shard_map/all_to_all | solution.py:315
  97.2 5.0 %collective-permute-start.14 = (f32[32,384]{1,0:T(8,128)S(1)}, f32[32,384]{1,0:T(8,128)S(1)}, u32[]{:S(2)}, u32[]{:S(2)}) collective-permute-start(f32[32,384]{1,0:T(8,128)S(1)} %dynamic-slice_bitcast_fusion), channel_id=1, source_target_pairs={{0,8},{8,0},{16,24},{24,16},{1,9},{9,1},{17,25},{25,17},{2,10},{10... | collective-permute-start | bytes 147464 | tf_op jit(solution)/shard_map/ppermute | solution.py:340
  97.3 4.9 %collective-permute-start.13 = (f32[32,384]{1,0:T(8,128)S(1)}, f32[32,384]{1,0:T(8,128)S(1)}, u32[]{:S(2)}, u32[]{:S(2)}) collective-permute-start(f32[32,384]{1,0:T(8,128)S(1)} %get-tuple-element.52), channel_id=1, source_target_pairs={{0,16},{8,24},{16,0},{24,8},{1,17},{9,25},{17,1},{25,9},{2,18},{10... | collective-permute-start | bytes 147464 | tf_op jit(solution)/shard_map/ppermute | solution.py:340
  99.1 3.8 %collective-permute-start.12 = (f32[32,384]{1,0:T(8,128)S(1)}, f32[32,384]{1,0:T(8,128)S(1)}, u32[]{:S(2)}, u32[]{:S(2)}) collective-permute-start(f32[32,384]{1,0:T(8,128)S(1)} %get-tuple-element.51), channel_id=1, source_target_pairs={{0,24},{8,16},{16,8},{24,0},{1,25},{9,17},{17,9},{25,1},{2,26},{10... | collective-permute-start | bytes 147464 | tf_op jit(solution)/shard_map/ppermute | solution.py:340
